TPU v7x, 512 devices: a whole 4x8x8 slice. The times are simulated.
512 devices in a mesh: sec: 4 (over x_lo, core), seq: 128 (over z, y, x_hi).
Axes of the slice: x: 4 (x_hi: 2, x_lo: 2; x = x_hi * 2 + x_lo), y: 8, z: 8, core: 2. Of those that a mesh axis runs over, the one named last changes fastest.
Arguments:
- queries: bfloat16 [4, 4096, 3072], P('sec', 'seq'), may hold values from -21 to 21
- keys: bfloat16 [4, 4096, 3072], P('sec', 'seq'), may hold values from -8 to 8
- values: bfloat16 [4, 4096, 3072], P('sec', 'seq'), may hold values from -6 to 6
- residual: bfloat16 [4, 4096, 3072], P('sec', 'seq'), may hold values from -6 to 6
- shift_mod: float32 [4, 3072], P('sec'), may hold values from -4 to 4
- scale_mod: float32 [4, 3072], P('sec'), may hold values from -4 to 4
- gate_mod: float32 [4, 3072], P('sec'), may hold values from 0.5 to 1.5
- final_weight: bfloat16 [3072, 64], replicated, may hold values from -0.109375 to 0.109375
- final_bias: float32 [64], replicated, may hold values from -4 to 4
- conv_weight: bfloat16 [432, 512], replicated, may hold values from -0.3125 to 0.3125
- conv_bias: float32 [512], replicated, may hold values from -4 to 4
- group_gain: float32 [512], replicated, may hold values from 0.1 to 1.9
- group_bias: float32 [512], replicated, may hold values from -4 to 4
Outputs:
- features: bfloat16 [4, 16, 128, 8, 512], P(None, 'sec', 'seq')
All inputs are finite; a program needn't handle non-finite values.
Results may differ from a plain program's by a relative error of at most 0.015.
Values may be sent and summed in bfloat16 or wider, within the bound.
A program may use at most 64 MiB of HBM per device.

v0:
```python
import jax
import jax.numpy as jnp
from jax import lax
from jax.sharding import PartitionSpec as P

H = 24
HD = 128
LATC = 16
F = 16
BR = 2
BC = 4


scaling = 0.476986
norm_eps = 1e-06


def passed_along(array, axis, by):
    size = lax.axis_size(axis)
    pairs = [(i, i + by) for i in range(size) if 0 <= i + by < size]
    return lax.ppermute(array, axis, pairs)


def each_head(single, arrays):
    stacked = tuple((member[0] for member in arrays))
    result = lax.map(lambda head_items: single(*head_items), stacked)
    return jax.tree.map(lambda member: member[None], result)


def block_rows(query_rows, key_rows, value_rows):
    scores = jnp.einsum(
        "qd,kd->qk", query_rows, key_rows, preferred_element_type=jnp.float32
    ) * HD ** (-0.5)
    row_peak = jnp.max(scores, axis=1, keepdims=True)
    weights = jnp.exp(scores - row_peak)
    row_total = jnp.sum(weights, axis=1)
    mixed_rows = jnp.dot(
        weights.astype(jnp.bfloat16), value_rows, preferred_element_type=jnp.float32
    )
    return (mixed_rows, row_peak[:, 0], row_total)


def tile_rim_shift(edge, offset):
    return passed_along(edge, "seq", offset)


def on_device(
    queries,
    keys,
    values,
    residual,
    shift_mod,
    scale_mod,
    gate_mod,
    final_weight,
    final_bias,
    conv_weight,
    conv_bias,
    group_gain,
    group_bias,
):
    seq_count = lax.axis_size("seq")
    sec_count = lax.axis_size("sec")
    tok_dev = queries.shape[1]
    qblocks = max(1, seq_count // 8)
    per_dev = H * qblocks // seq_count
    block_len = tok_dev // qblocks
    q_loc = queries[0].reshape(tok_dev, H, HD)
    k_loc = keys[0].reshape(tok_dev, H, HD)
    v_loc = values[0].reshape(tok_dev, H, HD)

    def spread_block(local_rows):
        return (
            local_rows.reshape(qblocks, block_len, H, HD)
            .transpose(2, 0, 1, 3)
            .reshape(seq_count, per_dev, block_len, HD)
        )

    heads_first = q_loc.transpose(1, 0, 2)[:, None]
    mixed_rows, row_peak, row_total = each_head(
        block_rows,
        (
            lax.all_to_all(
                jnp.broadcast_to(heads_first, (H, qblocks, tok_dev, HD)).reshape(
                    seq_count, per_dev, tok_dev, HD
                ),
                "seq",
                split_axis=0,
                concat_axis=2,
                tiled=True,
            ),
            lax.all_to_all(spread_block(k_loc), "seq", split_axis=0, concat_axis=2, tiled=True),
            lax.all_to_all(spread_block(v_loc), "seq", split_axis=0, concat_axis=2, tiled=True),
        ),
    )
    mixed_rows, row_peak, row_total = (
        lax.all_to_all(mixed_rows, "seq", split_axis=2, concat_axis=0, tiled=True),
        lax.all_to_all(row_peak, "seq", split_axis=2, concat_axis=0, tiled=True),
        lax.all_to_all(row_total, "seq", split_axis=2, concat_axis=0, tiled=True),
    )
    mixed_rows = mixed_rows.reshape(H, qblocks, tok_dev, HD)
    row_peak = row_peak.reshape(H, qblocks, tok_dev, 1)
    row_total = row_total.reshape(H, qblocks, tok_dev, 1)
    joint_peak = jnp.max(row_peak, axis=1, keepdims=True)
    factor = jnp.exp(row_peak - joint_peak)
    heads_out = (jnp.sum(factor * mixed_rows, axis=1) / jnp.sum(factor * row_total, axis=1)).astype(
        jnp.bfloat16
    )
    attended = heads_out.transpose(1, 0, 2).reshape(tok_dev, H * HD)
    hidden = residual[0].astype(jnp.float32) + gate_mod * attended.astype(jnp.float32)
    center = hidden - jnp.mean(hidden, axis=1, keepdims=True)
    normed = center * lax.rsqrt(jnp.mean(center * center, axis=1, keepdims=True) + norm_eps)
    modulated = (normed * (1.0 + scale_mod) + shift_mod).astype(jnp.bfloat16)
    patches = (
        (jnp.dot(modulated, final_weight, preferred_element_type=jnp.float32) + final_bias)
        / scaling
    ).astype(jnp.bfloat16)
    latent_grid = (
        patches.reshape(F, BR // 2, BC // 2, 2, 2, LATC)
        .transpose(0, 1, 3, 2, 4, 5)
        .reshape(F, BR, BC, LATC)
    )
    frame_span = F // sec_count
    padded = jnp.concatenate([latent_grid[:1], latent_grid[:1], latent_grid], axis=0)
    pieces = jnp.stack(
        [
            padded[sec_block * frame_span : sec_block * frame_span + frame_span + 2]
            for sec_block in range(sec_count)
        ]
    )
    chosen = lax.all_to_all(pieces, "sec", split_axis=0, concat_axis=0, tiled=True)
    grid_cols = min(16, seq_count)
    col_index = lax.axis_index("seq") % grid_cols
    left_rim = tile_rim_shift(chosen[:, :, :, -1:], 1)
    left_rim = jnp.where(col_index > 0, left_rim, jnp.zeros_like(left_rim))
    right_rim = tile_rim_shift(chosen[:, :, :, :1], -1)
    right_rim = jnp.where(col_index < grid_cols - 1, right_rim, jnp.zeros_like(right_rim))
    widened = jnp.concatenate([left_rim, chosen, right_rim], axis=3)
    upper_rim = tile_rim_shift(widened[:, :, -1:], grid_cols)
    lower_rim = tile_rim_shift(widened[:, :, :1], -grid_cols)
    extended = jnp.concatenate([upper_rim, widened, lower_rim], axis=2)
    columns = jnp.concatenate(
        [
            extended[:, t_step : t_step + frame_span, y_step : y_step + BR, x_step : x_step + BC]
            for t_step in range(3)
            for y_step in range(3)
            for x_step in range(3)
        ],
        axis=-1,
    )
    vae_width = conv_weight.shape[1]
    conv_out = (
        jnp.dot(
            columns.reshape(-1, conv_weight.shape[0]),
            conv_weight,
            preferred_element_type=jnp.float32,
        )
        + conv_bias
    )
    normed_out = (
        conv_out.reshape(sec_count, frame_span, BR * BC, vae_width) * group_gain + group_bias
    )
    activated = jax.nn.silu(normed_out).astype(jnp.bfloat16)
    return activated.reshape(sec_count, frame_span, 1, BR * BC, vae_width)


def solution(mesh):
    return jax.shard_map(
        on_device,
        mesh=mesh,
        in_specs=(
            P("sec", "seq", None),
            P("sec", "seq", None),
            P("sec", "seq", None),
            P("sec", "seq", None),
            P("sec", None),
            P("sec", None),
            P("sec", None),
            P(),
            P(),
            P(),
            P(),
            P(),
            P(),
        ),
        out_specs=P(None, "sec", "seq", None, None),
        check_vma=False,
    )
```

profile of v0, /device:TPU:28, one launch (start us, length us, event | category | flops | bytes accessed | tf_op | source)
XLA Modules:
  0.0 510.2 jit_solution(15659717260912903904)
XLA Ops:
  0.0 1.0 copy.116
  1.0 0.8 copy.95
  1.8 19.5 %all-to-all-start.1 = ((bf16[128,3,2,128]{3,2,1,0:T(2,128)(2,1)}), bf16[128,3,2,128]{3,2,1,0:T(2,128)(2,1)S(1)}, u32[]{:S(2)}, u32[]{:S(2)}) async-start(bf16[128,3,2,128]{3,2,1,0:T(2,128)(2,1)} %bitcast.14), calls=%async_computation.1 | async-start | bytes 393216 | tf_op jit(solution)/shard_map/all_to_all | solution.py:92
  21.4 1.0 copy.117
  22.4 0.8 copy.97
  23.2 9.0 %all-to-all-done.1 = bf16[128,3,2,128]{3,2,1,0:T(2,128)(2,1)S(1)} async-done(((bf16[128,3,2,128]{3,2,1,0:T(2,128)(2,1)}), bf16[128,3,2,128]{3,2,1,0:T(2,128)(2,1)S(1)}, u32[]{:S(2)}, u32[]{:S(2)}) %all-to-all-start.1) | async-done | bytes 196640 | tf_op jit(solution)/shard_map/all_to_all | solution.py:92
  32.2 10.1 %all-to-all-start.2 = ((bf16[128,3,2,128]{3,2,1,0:T(2,128)(2,1)}), bf16[128,3,2,128]{3,2,1,0:T(2,128)(2,1)S(1)}, u32[]{:S(2)}, u32[]{:S(2)}) async-start(bf16[128,3,2,128]{3,2,1,0:T(2,128)(2,1)} %bitcast.19), calls=%async_computation.2 | async-start | bytes 393216 | tf_op jit(solution)/shard_map/all_to_all | solution.py:93
  42.3 1.0 copy.115
  43.3 9.2 %all-to-all-done.2 = bf16[128,3,2,128]{3,2,1,0:T(2,128)(2,1)S(1)} async-done(((bf16[128,3,2,128]{3,2,1,0:T(2,128)(2,1)}), bf16[128,3,2,128]{3,2,1,0:T(2,128)(2,1)S(1)}, u32[]{:S(2)}, u32[]{:S(2)}) %all-to-all-start.2) | async-done | bytes 196640 | tf_op jit(solution)/shard_map/all_to_all | solution.py:93
  52.5 2.2 broadcast_in_dim.38
  54.7 11.3 %all-to-all-start = ((bf16[128,3,32,128]{3,2,1,0:T(8,128)(2,1)}), bf16[128,3,32,128]{3,2,1,0:T(8,128)(2,1)}, u32[]{:S(2)}, u32[]{:S(2)}) async-start(bf16[128,3,32,128]{3,2,1,0:T(8,128)(2,1)} %bitcast.139), calls=%async_computation | async-start | bytes 6291456 | tf_op jit(solution)/shard_map/all_to_all | solution.py:83
  66.4 72.5 %all-to-all-done = bf16[128,3,32,128]{3,2,1,0:T(8,128)(2,1)} async-done(((bf16[128,3,32,128]{3,2,1,0:T(8,128)(2,1)}), bf16[128,3,32,128]{3,2,1,0:T(8,128)(2,1)}, u32[]{:S(2)}, u32[]{:S(2)}) %all-to-all-start) | async-done | bytes 3145760 | tf_op jit(solution)/shard_map/all_to_all | solution.py:83
  138.9 4.3 copy.94
  143.2 16.0 %while.14 = (s32[]{:T(128)}, f32[3,4096,128]{2,1,0:T(8,128)}, f32[3,4096]{1,0:T(4,128)S(1)}, f32[3,4096]{1,0:T(4,128)S(1)}, bf16[3,4096,128]{2,1,0:T(8,128)(2,1)...) while((s32[]{:T(128)}, f32[3,4096,128]{2,1,0:T(8,128)}, ...), condition=%wide.region_3.4_spmd, body=%wide.region_0.3_spmd.sunk | while | flops 543154176 | bytes 15992933 | solution.py:26
  143.2 1.9 fusion.45
  145.2 2.3 fusion.46
  147.4 0.6 fusion.47
  148.5 1.9 fusion.45
  150.5 2.2 fusion.46
  152.7 0.6 fusion.47
  153.9 1.9 fusion.45
  155.8 2.3 fusion.46
  158.1 0.6 fusion.47
  159.2 2.0 copy.99
  161.2 9.7 %all-to-all-start.3 = ((f32[1,3,4096]{1,0,2:T(1,128)}), f32[1,3,4096]{1,0,2:T(1,128)S(1)}, u32[]{:S(2)}, u32[]{:S(2)}) async-start(f32[1,3,4096]{1,0,2:T(1,128)} %bitcast.142), calls=%async_computation.3 | async-start | bytes 4194304 | tf_op jit(solution)/shard_map/all_to_all | solution.py:98
  170.9 2.0 copy.106
  172.8 48.8 %all-to-all-done.3 = f32[1,3,4096]{1,0,2:T(1,128)S(1)} async-done(((f32[1,3,4096]{1,0,2:T(1,128)}), f32[1,3,4096]{1,0,2:T(1,128)S(1)}, u32[]{:S(2)}, u32[]{:S(2)}) %all-to-all-start.3) | async-done | bytes 49184 | tf_op jit(solution)/shard_map/all_to_all | solution.py:98
  221.7 10.9 %all-to-all-start.5 = ((f32[1,3,4096]{1,0,2:T(1,128)}), f32[1,3,4096]{1,0,2:T(1,128)}, u32[]{:S(2)}, u32[]{:S(2)}) async-start(f32[1,3,4096]{1,0,2:T(1,128)} %bitcast.141), calls=%async_computation.5 | async-start | bytes 4194304 | tf_op jit(solution)/shard_map/all_to_all | solution.py:99
  232.6 8.6 %copy.102 = f32[1,3,4096,128]{3,0,1,2:T(1,128)} copy(f32[1,3,4096,128]{3,2,1,0:T(8,128)} %bitcast.144) | data formatting | bytes 12582912 | tf_op jit(solution)/shard_map/broadcast_in_dim | solution.py:27
  241.1 41.5 %all-to-all-done.5 = f32[1,3,4096]{1,0,2:T(1,128)} async-done(((f32[1,3,4096]{1,0,2:T(1,128)}), f32[1,3,4096]{1,0,2:T(1,128)}, u32[]{:S(2)}, u32[]{:S(2)}) %all-to-all-start.5) | async-done | bytes 49184 | tf_op jit(solution)/shard_map/all_to_all | solution.py:99
  282.6 10.8 %all-to-all-start.4 = ((f32[1,3,4096,128]{3,0,1,2:T(1,128)}), f32[1,3,4096,128]{3,0,1,2:T(1,128)}, u32[]{:S(2)}, u32[]{:S(2)}) async-start(f32[1,3,4096,128]{3,0,1,2:T(1,128)} %copy.102), calls=%async_computation.4 | async-start | bytes 12582912 | tf_op jit(solution)/shard_map/all_to_all | solution.py:97
  293.5 0.9 copy.112
  294.8 2.5 copy.113
  297.6 0.4 multiply_reduce_fusion.2
  298.0 165.3 %all-to-all-done.4 = f32[1,3,4096,128]{3,0,1,2:T(1,128)} async-done(((f32[1,3,4096,128]{3,0,1,2:T(1,128)}), f32[1,3,4096,128]{3,0,1,2:T(1,128)}, u32[]{:S(2)}, u32[]{:S(2)}) %all-to-all-start.4) | async-done | bytes 6291488 | tf_op jit(solution)/shard_map/all_to_all | solution.py:97
  463.3 3.2 copy.103
  466.5 0.7 copy.104
  467.3 2.0 multiply_reduce_fusion
  470.0 0.4 fusion.14
  470.8 6.1 %all_to_all.95 = bf16[4,2,384]{2,1,0:T(2,128)(2,1)S(1)} all-to-all(bf16[4,2,384]{2,1,0:T(2,128)(2,1)S(1)} %reshape.151), channel_id=1, replica_groups=mesh['sec'=4,'seq'=128] {'sec'}, dimensions={0} | all-to-all | bytes 12288 | tf_op jit(solution)/shard_map/all_to_all | solution.py:131
  477.1 1.9 collective-permute-start
  479.0 5.4 %collective-permute-start.1 = (bf16[4,6,2,1,16]{4,3,2,1,0:T(2,128)(2,1)S(1)}, bf16[4,6,2,1,16]{4,3,2,1,0:T(2,128)(2,1)S(1)}, u32[]{:S(2)}, u32[]{:S(2)}) collective-permute-start(bf16[4,6,2,1,16]{4,3,2,1,0:T(2,128)(2,1)S(1)} %get-tuple-element.98), channel_id=1, source_target_pairs={{1,0},{2,1},{3,2},{4,3},{5,4},{6,5},{7,6},{8,7},{9,8},{10,9},{11,1... | collective-permute-start | bytes 4616 | tf_op jit(solution)/shard_map/ppermute | solution.py:21
  484.5 3.9 collective-permute-done.1
  488.5 3.5 collective-permute-start.2
  492.0 1.3 collective-permute-start.3
  493.7 13.7 %collective-permute-done.3 = bf16[4,6,1,6,16]{4,3,2,1,0:T(8,128)(2,1)S(1)} collective-permute-done((bf16[4,6,1,6,16]{4,3,2,1,0:T(8,128)(2,1)S(1)}, bf16[4,6,1,6,16]{4,3,2,1,0:T(8,128)(2,1)S(1)}, u32[]{:S(2)}, u32[]{:S(2)}) %collective-permute-start.3) | collective-permute-done | bytes 4640 | tf_op jit(solution)/shard_map/ppermute | solution.py:21
  507.9 1.2 concatenate.48
  509.5 0.7 multiply_convert_fusion
  (63 shorter events, 5.0 us)
Async XLA Ops:
  0.0 509.2 %copy-start = (bf16[432,512]{1,0:T(8,128)(2,1)S(1)}, bf16[432,512]{1,0:T(8,128)(2,1)}, u32[]{:S(2)}) copy-start(bf16[432,512]{1,0:T(8,128)(2,1)} %param.24) | copy-start | bytes 1327108
  1.8 30.3 %all-to-all-start.1 = ((bf16[128,3,2,128]{3,2,1,0:T(2,128)(2,1)}), bf16[128,3,2,128]{3,2,1,0:T(2,128)(2,1)S(1)}, u32[]{:S(2)}, u32[]{:S(2)}) async-start(bf16[128,3,2,128]{3,2,1,0:T(2,128)(2,1)} %bitcast.14), calls=%async_computation.1 | async-start | bytes 393216 | tf_op jit(solution)/shard_map/all_to_all | solution.py:92
  32.2 20.4 %all-to-all-start.2 = ((bf16[128,3,2,128]{3,2,1,0:T(2,128)(2,1)}), bf16[128,3,2,128]{3,2,1,0:T(2,128)(2,1)S(1)}, u32[]{:S(2)}, u32[]{:S(2)}) async-start(bf16[128,3,2,128]{3,2,1,0:T(2,128)(2,1)} %bitcast.19), calls=%async_computation.2 | async-start | bytes 393216 | tf_op jit(solution)/shard_map/all_to_all | solution.py:93
  54.7 84.2 %all-to-all-start = ((bf16[128,3,32,128]{3,2,1,0:T(8,128)(2,1)}), bf16[128,3,32,128]{3,2,1,0:T(8,128)(2,1)}, u32[]{:S(2)}, u32[]{:S(2)}) async-start(bf16[128,3,32,128]{3,2,1,0:T(8,128)(2,1)} %bitcast.139), calls=%async_computation | async-start | bytes 6291456 | tf_op jit(solution)/shard_map/all_to_all | solution.py:83
  161.2 60.5 %all-to-all-start.3 = ((f32[1,3,4096]{1,0,2:T(1,128)}), f32[1,3,4096]{1,0,2:T(1,128)S(1)}, u32[]{:S(2)}, u32[]{:S(2)}) async-start(f32[1,3,4096]{1,0,2:T(1,128)} %bitcast.142), calls=%async_computation.3 | async-start | bytes 4194304 | tf_op jit(solution)/shard_map/all_to_all | solution.py:98
  221.7 60.9 %all-to-all-start.5 = ((f32[1,3,4096]{1,0,2:T(1,128)}), f32[1,3,4096]{1,0,2:T(1,128)}, u32[]{:S(2)}, u32[]{:S(2)}) async-start(f32[1,3,4096]{1,0,2:T(1,128)} %bitcast.141), calls=%async_computation.5 | async-start | bytes 4194304 | tf_op jit(solution)/shard_map/all_to_all | solution.py:99
  241.1 52.3 %copy-start.3 = (f32[1,3072]{1,0:T(1,128)S(1)}, f32[1,3072]{1,0:T(1,128)}, u32[]{:S(2)}) copy-start(f32[1,3072]{1,0:T(1,128)} %param.20) | copy-start | bytes 36868
  282.6 180.8 %all-to-all-start.4 = ((f32[1,3,4096,128]{3,0,1,2:T(1,128)}), f32[1,3,4096,128]{3,0,1,2:T(1,128)}, u32[]{:S(2)}, u32[]{:S(2)}) async-start(f32[1,3,4096,128]{3,0,1,2:T(1,128)} %copy.102), calls=%async_computation.4 | async-start | bytes 12582912 | tf_op jit(solution)/shard_map/all_to_all | solution.py:97
  467.3 2.1 copy-start.1
  467.3 2.1 copy-start.2
  467.3 2.7 copy-start.7
  467.3 2.7 copy-start.8
  467.3 2.7 copy-start.9
  469.4 39.8 %copy-start.4 = (f32[512]{0:T(512)S(1)}, f32[512]{0:T(512)}, u32[]{:S(2)}) copy-start(f32[512]{0:T(512)} %param.25) | copy-start | bytes 6148
  469.7 39.8 %copy-start.5 = (f32[512]{0:T(512)S(1)}, f32[512]{0:T(512)}, u32[]{:S(2)}) copy-start(f32[512]{0:T(512)} %param.27) | copy-start | bytes 6148
  469.7 39.8 %copy-start.6 = (f32[512]{0:T(512)S(1)}, f32[512]{0:T(512)}, u32[]{:S(2)}) copy-start(f32[512]{0:T(512)} %param.26) | copy-start | bytes 6148
  477.1 7.4 %collective-permute-start = (bf16[4,6,2,1,16]{4,3,2,1,0:T(2,128)(2,1)S(1)}, bf16[4,6,2,1,16]{4,3,2,1,0:T(2,128)(2,1)S(1)}, u32[]{:S(2)}, u32[]{:S(2)}) collective-permute-start(bf16[4,6,2,1,16]{4,3,2,1,0:T(2,128)(2,1)S(1)} %get-tuple-element.97), channel_id=1, source_target_pairs={{0,1},{1,2},{2,3},{3,4},{4,5},{5,6},{6,7},{7,8},{8,9},{9,10},{10,1... | collective-permute-start | bytes 4616 | tf_op jit(solution)/shard_map/ppermute | solution.py:21
  479.0 9.3 %collective-permute-start.1 = (bf16[4,6,2,1,16]{4,3,2,1,0:T(2,128)(2,1)S(1)}, bf16[4,6,2,1,16]{4,3,2,1,0:T(2,128)(2,1)S(1)}, u32[]{:S(2)}, u32[]{:S(2)}) collective-permute-start(bf16[4,6,2,1,16]{4,3,2,1,0:T(2,128)(2,1)S(1)} %get-tuple-element.98), channel_id=1, source_target_pairs={{1,0},{2,1},{3,2},{4,3},{5,4},{6,5},{7,6},{8,7},{9,8},{10,9},{11,1... | collective-permute-start | bytes 4616 | tf_op jit(solution)/shard_map/ppermute | solution.py:21
  488.5 5.2 %collective-permute-start.2 = (bf16[4,6,1,6,16]{4,3,2,1,0:T(8,128)(2,1)S(1)}, bf16[4,6,1,6,16]{4,3,2,1,0:T(8,128)(2,1)S(1)}, u32[]{:S(2)}, u32[]{:S(2)}) collective-permute-start(bf16[4,6,1,6,16]{4,3,2,1,0:T(8,128)(2,1)S(1)} %get-tuple-element.84), channel_id=1, source_target_pairs={{0,16},{1,17},{2,18},{3,19},{4,20},{5,21},{6,22},{7,23},{8,24},{9,... | collective-permute-start | bytes 13832 | tf_op jit(solution)/shard_map/ppermute | solution.py:21
  492.0 15.4 %collective-permute-start.3 = (bf16[4,6,1,6,16]{4,3,2,1,0:T(8,128)(2,1)S(1)}, bf16[4,6,1,6,16]{4,3,2,1,0:T(8,128)(2,1)S(1)}, u32[]{:S(2)}, u32[]{:S(2)}) collective-permute-start(bf16[4,6,1,6,16]{4,3,2,1,0:T(8,128)(2,1)S(1)} %get-tuple-element.83), channel_id=1, source_target_pairs={{16,0},{17,1},{18,2},{19,3},{20,4},{21,5},{22,6},{23,7},{24,8},{25... | collective-permute-start | bytes 13832 | tf_op jit(solution)/shard_map/ppermute | solution.py:21
where the time goes:
time: 511 us; the launch traced here: 510 us
  waiting for transfers between devices  364 us (71%)
  starting transfers between devices  84.6 us (17%)
  local copies, waits for them, and re-layouts  35.2 us (7%)
  matrix products  13.2 us (3%)
  other arithmetic  6.36 us (1%)
  blocking collectives  6.14 us (1%)
    all_to_all x1, waiting for transfers between devices, on_device(): lax.all_to_all(mixed_rows, 'seq', split_axis=2, concat_axis=0, tiled=True)  165 us
    all_to_all x1, waiting for transfers between devices, on_device(): lax.all_to_all(jnp.broadcast_to(heads_first, (H, qblocks, tok_dev, HD)).r...  72.5 us
    all_to_all x1, waiting for transfers between devices, on_device(): lax.all_to_all(row_peak, 'seq', split_axis=2, concat_axis=0, tiled=True)  48.8 us
    all_to_all x1, waiting for transfers between devices, on_device(): lax.all_to_all(row_total, 'seq', split_axis=2, concat_axis=0, tiled=True)  41.5 us
    all_to_all x1, starting transfers between devices, on_device(): lax.all_to_all(spread_block(k_loc), 'seq', split_axis=0, concat_axis=2, t...  19.5 us
    ppermute x4, waiting for transfers between devices, passed_along(): return lax.ppermute(array, axis, pairs)  17.7 us
    ppermute x4, starting transfers between devices, passed_along(): return lax.ppermute(array, axis, pairs)  12.1 us
    all_to_all x1, starting transfers between devices, on_device(): lax.all_to_all(jnp.broadcast_to(heads_first, (H, qblocks, tok_dev, HD)).r...  11.3 us
  transfers between devices with their start and end apart: 10, of which 9 were waited for; matrix products, arithmetic and copies ran while one was open for 4% of the time, Pallas kernels for 0%

commit v1 on v0

v1 whole, which is shorter than its diff:
```python
import functools

import jax
import jax.numpy as jnp
from jax import lax
from jax.experimental import pallas as pl
from jax.experimental.pallas import tpu as pltpu
from jax.sharding import PartitionSpec as P

H = 24
HD = 128
LATC = 16
F = 16
BR = 2
BC = 4
NZ = 8
NY = 8
TOK = 32
HG = 3
GW = HG * HD
NBLK = NZ * TOK

scaling = 0.476986
norm_eps = 1e-06
EXP2_SCALE = HD ** (-0.5) * 1.4426950408889634
F32 = jnp.float32
BF16 = jnp.bfloat16


def remote(src, dst, send_sem, recv_sem, sec, seq):
    return pltpu.make_async_remote_copy(
        src_ref=src,
        dst_ref=dst,
        send_sem=send_sem,
        recv_sem=recv_sem,
        device_id={"sec": sec, "seq": seq},
        device_id_type=pl.DeviceIdType.MESH,
    )


def signal(sem, sec, seq):
    pl.semaphore_signal(
        sem, inc=1, device_id={"sec": sec, "seq": seq}, device_id_type=pl.DeviceIdType.MESH
    )


def position():
    s = lax.axis_index("sec")
    g = lax.axis_index("seq")
    return s, g, s % 2, s // 2, g // (2 * NY), (g // 2) % NY, g % 2

NEAREST = (0, 1, 7, 2, 6, 3, 5, 4)
HALVES = 2
HALF = NBLK // HALVES
AROUND = [(dy, dx) for dy in (-1, 0, 1) for dx in (-1, 0, 1)]


def whole_kernel(
    q_ref,
    k_ref,
    v_ref,
    res_hbm,
    shift_hbm,
    scale_hbm,
    gate_hbm,
    fw_hbm,
    fb_hbm,
    cw_hbm,
    cb_hbm,
    gg_hbm,
    gb_hbm,
    out_ref,
    qb,
    kb,
    vb,
    ob,
    att,
    peak,
    total,
    acc,
    pat,
    tiles,
    near_tiles,
    windows,
    res_ref,
    shift_ref,
    scale_ref,
    gate_ref,
    fw_ref,
    fb_ref,
    cw_ref,
    cb_ref,
    gg_ref,
    gb_ref,
    load_sem,
    cw_sem,
    s1_send,
    s1_recv,
    ring_send,
    ring_recv,
    sib_send,
    sib_recv,
    o_send,
    o_recv,
    halo_send,
    halo_recv,
):
    s, g, core, xl, z, y, xh = position()
    stays = core == xh
    moves = jnp.logical_not(stays)
    swap_sec = xl * 2 + xh

    def swap_seq(zp):
        return (zp * NY + y) * 2 + core

    right = (z * NY + (y + 1) % NY) * 2 + xh
    left = (z * NY + (y + NY - 1) % NY) * 2 + xh
    sibling = xl * 2 + 1 - core
    col = y * 2 + xh
    last_col = 2 * NY - 1

    def there(dy, dx):
        row_ok = z + dy >= 0 if dy < 0 else z + dy < NZ
        col_ok = col + dx >= 0 if dx < 0 else col + dx <= last_col
        return jnp.logical_and(row_ok, col_ok)

    def for_sections(dy, dx, one):
        def body(ds, carry):
            one((s + ds) % 4)
            return carry

        if dy == 0 and dx == 0:
            lax.fori_loop(1, 4, body, 0)
        else:

            @pl.when(there(dy, dx))
            def _():
                lax.fori_loop(0, 4, body, 0)

    barrier = pltpu.get_barrier_semaphore()
    for e in NEAREST[1:]:
        signal(barrier, swap_sec, swap_seq((z + e) % NZ))

    @pl.when(moves)
    def _():
        signal(barrier, swap_sec, swap_seq(z))

    signal(barrier, s, right)
    signal(barrier, s, left)
    signal(barrier, sibling, g)
    for dy, dx in AROUND:
        for_sections(dy, dx, lambda sp: signal(barrier, sp, g + dy * 2 * NY + dx))

    loads = [
        pltpu.make_async_copy(src, dst, load_sem.at[i])
        for i, (src, dst) in enumerate(
            (
                (res_hbm, res_ref),
                (shift_hbm, shift_ref),
                (scale_hbm, scale_ref),
                (gate_hbm, gate_ref),
                (fw_hbm, fw_ref),
                (fb_hbm, fb_ref),
                (cb_hbm, cb_ref),
                (gg_hbm, gg_ref),
                (gb_hbm, gb_ref),
            )
        )
    ] + [
        pltpu.make_async_copy(
            cw_hbm.at[pl.ds(tap * 48, 48), :], cw_ref.at[tap, pl.ds(0, 48), :], cw_sem.at[tap]
        )
        for tap in range(9)
    ]
    for load in loads:
        load.start()

    n_rows = 3 - jnp.where(z == 0, 1, 0) - jnp.where(z == NZ - 1, 1, 0)
    n_cols = 3 - jnp.where(col == 0, 1, 0) - jnp.where(col == last_col, 1, 0)
    pl.semaphore_wait(barrier, NZ + 1 + jnp.where(stays, 0, 1) + 4 * n_rows * n_cols)

    def group_cols(zp):
        return pl.ds(pl.multiple_of(zp * GW, HD), GW)

    def block_rows(place):
        return pl.ds(place * TOK, TOK)

    stage_one = ((k_ref, kb.at[0]), (v_ref, vb.at[0]), (q_ref, qb))

    def stage_copy(t, e):
        src, buf = stage_one[t]
        zp = (z + e) % NZ
        place = NEAREST.index((NZ - e) % NZ)
        return remote(
            src.at[:, group_cols(zp)],
            buf.at[block_rows(place), :],
            s1_send.at[t, place],
            s1_recv.at[t, place],
            swap_sec,
            swap_seq(zp),
        )

    for t in range(3):

        @pl.when(stays)
        def _(t=t):
            src, buf = stage_one[t]
            pltpu.make_async_copy(
                src.at[:, group_cols(z)], buf.at[block_rows(0), :], s1_recv.at[t, 0]
            ).start()

        @pl.when(moves)
        def _(t=t):
            stage_copy(t, 0).start()

        for e in NEAREST[1:]:
            stage_copy(t, e).start()

    def await_stage(t, places):
        src, buf = stage_one[t]
        for place in places:
            pltpu.make_async_copy(
                src.at[:, group_cols(0)], buf.at[block_rows(place), :], s1_recv.at[t, place]
            ).wait()

    bufs = (kb, vb)

    def slot_of(way, hops):
        if hops in (0, 4):
            return hops
        return hops if way == 0 else 4 + hops

    def half_of(t, slot, half):
        return bufs[t].at[slot, pl.ds(half * HALF, HALF), :]

    def hop(way, t, half, hops):
        return remote(
            half_of(t, slot_of(way, hops - 1), half),
            half_of(t, slot_of(way, hops), half),
            ring_send.at[way, t, half, hops],
            ring_recv.at[way, t, half, hops],
            s,
            (right, left)[way],
        )

    def across(t, slot, half):
        return remote(
            half_of(t, slot, half),
            half_of(t, 8 + slot, half),
            sib_send.at[t, slot, half],
            sib_recv.at[t, slot, half],
            sibling,
            g,
        )

    hops_used = [
        (way, t, half, n)
        for n in range(1, 5)
        for t in range(2)
        for half in range(HALVES)
        for way in range(2)
        if n < 4 or way == t
    ]

    def attend(slots, first):
        def one_head(h):
            lanes = slice(h * HD, (h + 1) * HD)
            q = qb[:, lanes]
            scores = [
                lax.dot_general(
                    q, kb[slot, :, lanes], (((1,), (1,)), ((), ())), preferred_element_type=F32
                )
                for slot in slots
            ]
            top = functools.reduce(jnp.maximum, scores)
            top = jnp.max(top, axis=1, keepdims=True)
            top = jnp.broadcast_to(top, (NBLK, HD))
            if not first:
                old = peak[h]
                top = jnp.maximum(old, top)
            peak[h] = top
            wide = jnp.concatenate([top, top], axis=1)
            part = None
            mixed = None
            for slot, score in zip(slots, scores):
                weights = jnp.exp2((score - wide) * EXP2_SCALE)
                halves = weights[:, :HD] + weights[:, HD:]
                part = halves if part is None else part + halves
                term = jnp.dot(
                    weights.astype(BF16), vb[slot, :, lanes], preferred_element_type=F32
                )
                mixed = term if mixed is None else mixed + term
            if first:
                total[h] = part
                acc[h] = mixed
            else:
                fade = jnp.exp2((old - top) * EXP2_SCALE)
                total[h] = total[h] * fade + part
                acc[h] = acc[h] * fade + mixed

        for h in range(HG):
            one_head(h)

    per_half = NZ // HALVES
    for t in range(2):
        for half in range(HALVES):
            await_stage(t, range(half * per_half, (half + 1) * per_half))
            hop(0, t, half, 1).start()
            hop(1, t, half, 1).start()
            across(t, 0, half).start()
    cw_ref[:, 48:, :] = jnp.zeros((9, 80, cw_ref.shape[2]), BF16)
    pieces = [(t, half) for t in range(2) for half in range(HALVES)]
    for n in range(1, 4):
        for t, half in pieces:
            for way in range(2):
                hop(way, t, half, n).wait_recv()
                if (way, t, half, n + 1) in hops_used:
                    hop(way, t, half, n + 1).start()
                across(t, slot_of(way, n), half).start()
        if n == 1:
            await_stage(2, range(NZ))
            for t, half in pieces:
                across(t, 0, half).wait_recv()
            attend((0, 8), True)
        for t, half in pieces:
            for way in range(2):
                across(t, slot_of(way, n), half).wait_recv()
        attend((n, 4 + n, 8 + n, 12 + n), False)
    for half in range(HALVES):
        for t in range(2):
            hop(t, t, half, 4).wait_recv()
            across(t, 4, half).start()
    for t, half in pieces:
        across(t, 4, half).wait_recv()
    attend((4, 12), False)

    for h in range(HG):
        lanes = slice(h * HD, (h + 1) * HD)
        ob[:, lanes] = (acc[h] / jnp.sum(total[h], axis=1, keepdims=True)).astype(BF16)

    def back_copy(place):
        zp = (z + NEAREST[place]) % NZ
        return remote(
            ob.at[block_rows(place), :],
            att.at[:, group_cols(z)],
            o_send.at[place],
            o_recv.at[place],
            swap_sec,
            swap_seq(zp),
        )

    for place in range(NZ - 1, 0, -1):
        back_copy(place).start()

    @pl.when(moves)
    def _():
        back_copy(0).start()

    @pl.when(stays)
    def _():
        pltpu.make_async_copy(
            ob.at[block_rows(0), :], att.at[:, group_cols(z)], o_recv.at[0]
        ).start()

    for load in loads:
        load.wait()
    for place in range(NZ):
        zp = (z + NZ - NEAREST[place]) % NZ
        pltpu.make_async_copy(
            ob.at[block_rows(0), :], att.at[:, group_cols(zp)], o_recv.at[place]
        ).wait()

    hidden = res_ref[...].astype(F32) + gate_ref[...] * att[...].astype(F32)
    center = hidden - jnp.mean(hidden, axis=1, keepdims=True)
    normed = center * lax.rsqrt(jnp.mean(center * center, axis=1, keepdims=True) + norm_eps)
    modulated = (normed * (1.0 + scale_ref[...]) + shift_ref[...]).astype(BF16)
    patches = (
        lax.dot_general(
            modulated, fw_ref[...], (((1,), (1,)), ((), ())), preferred_element_type=F32
        )
        + fb_ref[...]
    ) / scaling
    pat[...] = patches.astype(BF16).astype(F32)
    even = pat[pl.ds(0, F, stride=2), :]
    odd = pat[pl.ds(1, F, stride=2), :]
    side = 2 * LATC
    tile = jnp.concatenate([even[:, :side], odd[:, :side], even[:, side:], odd[:, side:]], axis=1)
    tiles[0, 0:1, :] = tile[:1]
    tiles[0, 1:2, :] = tile[:1]
    tiles[0, 2:8, :] = tile[:6]
    for part in (1, 2):
        tiles[part] = tile[4 * part - 2 : 4 * part + 6]
    tiles[3, 0:6, :] = tile[10:16]
    tiles[3, 6:8, :] = tile[14:16]

    def halo_copy(dy, dx, sp):
        place = (1 - dy) * 3 + 1 - dx
        return remote(
            tiles.at[sp],
            near_tiles.at[s, place],
            halo_send.at[place, sp],
            halo_recv.at[place, s],
            sp,
            g + dy * 2 * NY + dx,
        )

    for dy, dx in AROUND:
        for_sections(dy, dx, lambda sp: halo_copy(dy, dx, sp).start())
    near_tiles[s, 4] = tiles[s]
    for dy, dx in AROUND:
        if (dy, dx) != (0, 0):
            place = (1 + dy) * 3 + 1 + dx

            @pl.when(jnp.logical_not(there(dy, dx)))
            def _():
                for sp in range(4):
                    near_tiles[sp, place] = jnp.zeros((8, 128), F32)

    for t in range(3):

        @pl.when(moves)
        def _(t=t):
            stage_copy(t, 0).wait_send()

        for e in NEAREST[1:]:
            stage_copy(t, e).wait_send()
    for used in hops_used:
        hop(*used).wait_send()
    for t, half in pieces:
        for slot in range(8):
            across(t, slot, half).wait_send()
    for place in range(1, NZ):
        back_copy(place).wait_send()

    @pl.when(moves)
    def _():
        back_copy(0).wait_send()

    def halo_wait(dy, dx, sp):
        place = (1 + dy) * 3 + 1 + dx
        pltpu.make_async_copy(
            tiles.at[0], near_tiles.at[sp, place], halo_recv.at[place, sp]
        ).wait()

    for dy, dx in AROUND:
        for_sections(dy, dx, lambda sp: halo_wait(dy, dx, sp))

    for yy in range(4):
        vert, dr = ((0, 1), (1, 0), (1, 1), (2, 0))[yy]
        lo = dr * BC * LATC
        hi = lo + BC * LATC
        sides = [near_tiles[:, vert * 3 + dx].reshape(32, 128) for dx in range(3)]
        strip = jnp.concatenate(
            [
                sides[0][:, hi - LATC : hi],
                sides[1][:, lo:hi],
                sides[2][:, lo : lo + LATC],
                jnp.zeros((32, 2 * LATC), F32),
            ],
            axis=1,
        )
        for x in range(BC):
            moved = strip if x == 0 else pltpu.roll(strip, 128 - x * LATC, axis=1)
            moved = moved.reshape(4, 8, 128)
            for dt in range(3):
                piece = moved[:, dt : dt + 4, :].reshape(16, 128)
                for dy in range(3):
                    row = yy - dy
                    if 0 <= row < BR:
                        windows[dt * 3 + dy, pl.ds(row * BC + x, 16, stride=8), :] = piece
    left_side = jnp.concatenate([windows[tap].astype(BF16) for tap in range(9)], axis=1)
    conv = jnp.dot(
        left_side, cw_ref[...].reshape(9 * 128, cw_ref.shape[2]), preferred_element_type=F32
    )
    conv = (conv + cb_ref[...]) * gg_ref[...] + gb_ref[...]
    out_ref[...] = (conv / (1.0 + jnp.exp(-conv))).astype(BF16)

    for dy, dx in AROUND:
        for_sections(dy, dx, lambda sp: halo_copy(dy, dx, sp).wait_send())


def on_device(
    queries,
    keys,
    values,
    residual,
    shift_mod,
    scale_mod,
    gate_mod,
    final_weight,
    final_bias,
    conv_weight,
    conv_bias,
    group_gain,
    group_bias,
):
    any_spec = pl.BlockSpec(memory_space=pl.ANY)
    dma = pltpu.SemaphoreType.DMA
    vae_width = conv_weight.shape[1]
    features = pl.pallas_call(
        whole_kernel,
        out_shape=jax.ShapeDtypeStruct((4 * 4 * BR * BC, vae_width), BF16),
        in_specs=[any_spec] * 13,
        out_specs=pl.BlockSpec(memory_space=pltpu.VMEM),
        scratch_shapes=[
            pltpu.VMEM((NBLK, GW), BF16),
            pltpu.VMEM((16, NBLK, GW), BF16),
            pltpu.VMEM((16, NBLK, GW), BF16),
            pltpu.VMEM((NBLK, GW), BF16),
            pltpu.VMEM((TOK, H * HD), BF16),
            pltpu.VMEM((HG, NBLK, HD), F32),
            pltpu.VMEM((HG, NBLK, HD), F32),
            pltpu.VMEM((HG, NBLK, HD), F32),
            pltpu.VMEM((TOK, 4 * LATC), F32),
            pltpu.VMEM((4, 8, 128), F32),
            pltpu.VMEM((4, 9, 8, 128), F32),
            pltpu.VMEM((9, 4 * 4 * BR * BC, 128), F32),
            pltpu.VMEM((TOK, H * HD), BF16),
            pltpu.VMEM((1, H * HD), F32),
            pltpu.VMEM((1, H * HD), F32),
            pltpu.VMEM((1, H * HD), F32),
            pltpu.VMEM((4 * LATC, H * HD), BF16),
            pltpu.VMEM((1, 4 * LATC), F32),
            pltpu.VMEM((9, 128, vae_width), BF16),
            pltpu.VMEM((1, vae_width), F32),
            pltpu.VMEM((1, vae_width), F32),
            pltpu.VMEM((1, vae_width), F32),
            dma((9,)),
            dma((9,)),
            dma((3, NZ)),
            dma((3, NZ)),
            dma((2, 2, HALVES, 5)),
            dma((2, 2, HALVES, 5)),
            dma((2, 8, HALVES)),
            dma((2, 8, HALVES)),
            dma((NZ,)),
            dma((NZ,)),
            dma((9, 4)),
            dma((9, 4)),
        ],
        compiler_params=pltpu.CompilerParams(
            collective_id=0, has_side_effects=True, vmem_limit_bytes=60 * 1024 * 1024
        ),
        name="whole",
    )(
        queries[0],
        keys[0],
        values[0],
        residual[0],
        shift_mod,
        scale_mod,
        gate_mod,
        final_weight.T,
        final_bias[None],
        conv_weight,
        conv_bias[None],
        group_gain[None],
        group_bias[None],
    )
    return features.reshape(4, 4, 1, BR * BC, vae_width)


def solution(mesh):
    return jax.shard_map(
        on_device,
        mesh=mesh,
        in_specs=(
            P("sec", "seq", None),
            P("sec", "seq", None),
            P("sec", "seq", None),
            P("sec", "seq", None),
            P("sec", None),
            P("sec", None),
            P("sec", None),
            P(),
            P(),
            P(),
            P(),
            P(),
            P(),
        ),
        out_specs=P(None, "sec", "seq", None, None),
        check_vma=False,
    )
```

time: 511 us -> 74.8 us (0.15)
  the two profiles are of different devices: /device:TPU:28 before, /device:TPU:1 now
where the time goes in v1:
time: 74.8 us; the launch traced here: 74.6 us
  Pallas kernels  73 us (98%)
  local copies, waits for them, and re-layouts  1.57 us (2%)
    pallas_call x1, Pallas kernels, on_device(): pl.pallas_call(whole_kernel, out_shape=jax.ShapeDtypeStruct((4 * 4 * BR *...  73 us
    unnamed x1, local copies, waits for them, and re-layouts  1.57 us

profile of v1, /device:TPU:1, one launch (start us, length us, event | category | flops | bytes accessed | tf_op | source)
XLA Modules:
  0.0 74.6 jit_solution(4426773460524631304)
XLA Ops:
  0.0 73.0 %whole.1 = bf16[128,512]{1,0:T(8,128)(2,1)} custom-call(bf16[32,3072]{1,0:T(8,128)(2,1)} %bitcast.14, bf16[32,3072]{1,0:T(8,128)(2,1)} %bitcast.15, bf16[32,3072]{1,0:T(8,128)(2,1)} %bitcast.16, bf16[32,3072]{1,0:T(8,128)(2,1)} %bitcast.17, f32[1,3072]{1,0:T(1,128)} %shift_hbm.1, f32[1,3072]{1,0:T(1,128)} %scale_hbm.1, f32[1,3072]{1,0:T(1,128)} %gate_hbm.1, ...), custom_call_target="tpu_custom_call" | custom-call | tf_op jit(solution)/shard_map/whole/pallas_call | solution.py:500
  73.0 1.6 %copy.16 = bf16[4,4,1,8,512]{4,3,2,1,0:T(8,128)(2,1)} copy(bf16[4,4,1,8,512]{4,3,2,1,0:T(8,128)(2,1)} %bitcast.12) | data formatting | bytes 262144

commit v2 on v1

v2 whole, which is shorter than its diff:
```python
import functools

import jax
import jax.numpy as jnp
from jax import lax
from jax.experimental import pallas as pl
from jax.experimental.pallas import tpu as pltpu
from jax.sharding import PartitionSpec as P

H = 24
HD = 128
LATC = 16
F = 16
BR = 2
BC = 4
NZ = 8
NY = 8
TOK = 32
HG = 3
GW = HG * HD
NBLK = NZ * TOK

scaling = 0.476986
norm_eps = 1e-06
EXP2_SCALE = HD ** (-0.5) * 1.4426950408889634
F32 = jnp.float32
BF16 = jnp.bfloat16


def remote(src, dst, send_sem, recv_sem, sec, seq):
    return pltpu.make_async_remote_copy(
        src_ref=src,
        dst_ref=dst,
        send_sem=send_sem,
        recv_sem=recv_sem,
        device_id={"sec": sec, "seq": seq},
        device_id_type=pl.DeviceIdType.MESH,
    )


def signal(sem, sec, seq):
    pl.semaphore_signal(
        sem, inc=1, device_id={"sec": sec, "seq": seq}, device_id_type=pl.DeviceIdType.MESH
    )


def position():
    s = lax.axis_index("sec")
    g = lax.axis_index("seq")
    return s, g, s % 2, s // 2, g // (2 * NY), (g // 2) % NY, g % 2

NEAREST = (0, 1, 7, 2, 6, 3, 5, 4)
AROUND = [(dy, dx) for dy in (-1, 0, 1) for dx in (-1, 0, 1)]

ITEMS = (
    ((0, 0), (0, 7), (0, 6)),
    ((0, 1), (0, 2), (0, 5)),
    ((0, 3), (0, 4), (1, 1)),
    ((1, 2), (1, 3), (1, 0)),
    ((1, 4), (1, 5), (1, 7)),
    ((1, 6), (2, 3), (2, 4)),
    ((2, 5), (2, 6), (2, 2)),
    ((2, 7), (2, 0), (2, 1)),
)
STREAM_START = ((5, 0, 3), (4, 7, 2))
STREAM_HOPS = ((5, 5, 4), (4, 5, 5))
STREAM_ENTRY = ((3, 2, 2), (2, 2, 3))
MOST_HOPS = 5
MOST_STEPS = 4
HALVES = 2
PER_HALF = NZ // HALVES
HALF = NBLK // HALVES
STREAMS = [(way, h) for h in range(HG) for way in range(2)]


def stream_place(way, h, y):
    first = STREAM_START[way][h]
    return (y + NY - first) % NY if way == 0 else (first + NY - y) % NY


def block_order(y, h):
    found = []
    for way in range(2):
        place = stream_place(way, h, y)
        past = place - STREAM_ENTRY[way][h]
        if past >= 0 and place <= STREAM_HOPS[way][h]:
            found += [(min(n, past + 1), n, way) for n in range(1, place + 1)]
    return [(h * 2 + way) * MOST_HOPS + n - 1 for _, n, way in sorted(found)]


ORDER = [
    [[block_order(y, ITEMS[y][i][0])[k] for y in range(NY)] for k in range(NY - 1)]
    for i in range(HG)
]


def pick(table, index):
    out = table[0]
    for k in range(1, len(table)):
        out = jnp.where(index == k, table[k], out)
    return out


def whole_kernel(
    q_ref,
    k_ref,
    v_ref,
    res_hbm,
    shift_hbm,
    scale_hbm,
    gate_hbm,
    fw_hbm,
    fb_hbm,
    cw_hbm,
    cb_hbm,
    gg_hbm,
    gb_hbm,
    out_ref,
    q_own,
    own,
    beside,
    ring,
    cross,
    qb,
    ob,
    att,
    peak,
    total,
    acc,
    pat,
    tiles,
    near_tiles,
    windows,
    res_ref,
    shift_ref,
    scale_ref,
    gate_ref,
    fw_ref,
    fb_ref,
    cw_ref,
    cb_ref,
    gg_ref,
    gb_ref,
    load_sem,
    cw_sem,
    s1_send,
    s1_recv,
    q_send,
    q_recv,
    ring_send,
    ring_recv,
    own_send,
    beside_send,
    beside_recv,
    cross_send,
    cross_recv,
    o_send,
    o_recv,
    sec_send,
    sec_recv,
    halo_send,
    halo_recv,
):
    s, g, core, xl, z, y, xh = position()
    stays = core == xh
    moves = jnp.logical_not(stays)
    swap_sec = xl * 2 + xh

    def swap_seq(zp, yp):
        return (zp * NY + yp) * 2 + core

    def ring_seq(yp):
        return (z * NY + yp) * 2 + xh

    steps = (1, NY - 1)
    sibling = xl * 2 + 1 - core
    col = y * 2 + xh
    last_col = 2 * NY - 1

    item_head = [pick([ITEMS[k][i][0] for k in range(NY)], y) for i in range(HG)]
    item_y = [pick([ITEMS[k][i][1] for k in range(NY)], y) for i in range(HG)]
    homes = {item: (k, i) for k in range(NY) for i, item in enumerate(ITEMS[k])}
    query_chip = [pick([homes[j, k][0] for k in range(NY)], y) for j in range(HG)]
    query_slot = [pick([homes[j, k][1] for k in range(NY)], y) for j in range(HG)]
    places = {(way, h): stream_place(way, h, y) for way, h in STREAMS}

    def sends_own(way, h):
        return places[way, h] < STREAM_HOPS[way][h]

    def takes(way, h, n):
        place = places[way, h]
        working = jnp.logical_and(place >= STREAM_ENTRY[way][h], place <= STREAM_HOPS[way][h])
        return jnp.logical_and(working, place >= n)

    def passes(way, h):
        place = places[way, h]
        return jnp.logical_and(place >= STREAM_ENTRY[way][h], place < STREAM_HOPS[way][h])

    def step_of(way, h, n):
        return jnp.minimum(n, places[way, h] - STREAM_ENTRY[way][h] + 1)

    def there(dy, dx):
        row_ok = z + dy >= 0 if dy < 0 else z + dy < NZ
        col_ok = col + dx >= 0 if dx < 0 else col + dx <= last_col
        return jnp.logical_and(row_ok, col_ok)

    neighbours = [(dy, dx) for dy, dx in AROUND if (dy, dx) != (0, 0)]

    barrier = pltpu.get_barrier_semaphore()
    for e in NEAREST[1:]:
        signal(barrier, swap_sec, swap_seq((z + e) % NZ, y))

    @pl.when(moves)
    def _():
        signal(barrier, swap_sec, swap_seq(z, y))

    for e in range(1, NY):
        signal(barrier, s, ring_seq((y + e) % NY))
    for ds in range(1, 4):
        signal(barrier, (s + ds) % 4, g)
    for dy, dx in neighbours:

        @pl.when(there(dy, dx))
        def _(dy=dy, dx=dx):
            signal(barrier, s, g + dy * 2 * NY + dx)

    loads = [
        pltpu.make_async_copy(src, dst, load_sem.at[i])
        for i, (src, dst) in enumerate(
            (
                (res_hbm, res_ref),
                (shift_hbm, shift_ref),
                (scale_hbm, scale_ref),
                (gate_hbm, gate_ref),
                (fw_hbm, fw_ref),
                (fb_hbm, fb_ref),
                (cb_hbm, cb_ref),
                (gg_hbm, gg_ref),
                (gb_hbm, gb_ref),
            )
        )
    ] + [
        pltpu.make_async_copy(
            cw_hbm.at[pl.ds(tap * 48, 48), :], cw_ref.at[tap, pl.ds(0, 48), :], cw_sem.at[tap]
        )
        for tap in range(9)
    ]
    for load in loads:
        load.start()

    n_rows = 3 - jnp.where(z == 0, 1, 0) - jnp.where(z == NZ - 1, 1, 0)
    n_cols = 3 - jnp.where(col == 0, 1, 0) - jnp.where(col == last_col, 1, 0)
    pl.semaphore_wait(barrier, 2 * NZ + 1 - jnp.where(stays, 1, 0) + n_rows * n_cols)

    def group_cols(zp):
        return pl.ds(pl.multiple_of(zp * GW, HD), GW)

    def head_cols(h):
        return pl.ds(pl.multiple_of(h * HD, HD), HD)

    def block_rows(place):
        return pl.ds(place * TOK, TOK)

    sources = (k_ref, v_ref, q_ref)

    def landing(t, place):
        if t == 2:
            return q_own.at[block_rows(place), :]
        return own.at[place // PER_HALF, t, block_rows(place % PER_HALF), :]

    def stage_copy(t, place):
        zp = (z + NZ - NEAREST[place]) % NZ
        return remote(
            sources[t].at[:, group_cols(zp)],
            landing(t, place),
            s1_send.at[t, place],
            s1_recv.at[t, place],
            swap_sec,
            swap_seq(zp, y),
        )

    def start_stage(t, first, last):
        for place in range(first, last):
            if place > 0:
                stage_copy(t, place).start()
                continue

            @pl.when(stays)
            def _():
                pltpu.make_async_copy(
                    sources[t].at[:, group_cols(z)], landing(t, 0), s1_recv.at[t, 0]
                ).start()

            @pl.when(moves)
            def _():
                stage_copy(t, 0).start()

    def await_stage(t, first, last):
        for place in range(first, last):
            pltpu.make_async_copy(
                sources[t].at[:, group_cols(0)], landing(t, place), s1_recv.at[t, place]
            ).wait()

    for half in range(HALVES):
        for t in range(2):
            start_stage(t, half * PER_HALF, (half + 1) * PER_HALF)
    start_stage(2, 0, NZ)

    def slot_of(way, h, n):
        return (h * 2 + way) * MOST_HOPS + n - 1

    def own_hop(way, h, half):
        place = places[way, h]
        target = jnp.maximum(STREAM_ENTRY[way][h], place + 1)
        slot = slot_of(way, h, target - place)
        first = STREAM_START[way][h]
        chip = (first + target) % NY if way == 0 else (first + NY - target) % NY
        return remote(
            own.at[half, :, :, pl.ds(h * HD, HD)],
            ring.at[slot, half],
            own_send.at[half, slot_of(way, h, 1)],
            ring_recv.at[half, slot],
            s,
            ring_seq(chip),
        )

    def hop(way, h, half, n):
        slot = slot_of(way, h, n)
        return remote(
            ring.at[slot, half],
            ring.at[slot + 1, half],
            ring_send.at[half, slot],
            ring_recv.at[half, slot + 1],
            s,
            ring_seq((y + steps[way]) % NY),
        )

    def arrived(way, h, half, n):
        slot = slot_of(way, h, n)
        return pltpu.make_async_copy(
            ring.at[slot, half], ring.at[slot, half], ring_recv.at[half, slot]
        )

    def own_across(half):
        return remote(
            own.at[half], beside.at[half], beside_send.at[half], beside_recv.at[half], sibling, g
        )

    def across(way, h, half, n):
        slot = slot_of(way, h, n)
        return remote(
            ring.at[slot, half],
            cross.at[slot, half],
            cross_send.at[half, slot],
            cross_recv.at[half, slot],
            sibling,
            g,
        )

    def start_streams(half):
        for t in range(2):
            await_stage(t, half * PER_HALF, (half + 1) * PER_HALF)
        for way, h in STREAMS:

            @pl.when(sends_own(way, h))
            def _(way=way, h=h):
                own_hop(way, h, half).start()

        own_across(half).start()

    def pass_on(half, step):
        for way, h in STREAMS:
            hops = STREAM_HOPS[way][h]
            for n in range(step, hops + 1):

                @pl.when(jnp.logical_and(takes(way, h, n), step_of(way, h, n) == step))
                def _(way=way, h=h, n=n):
                    arrived(way, h, half, n).wait()

                    if n < hops:

                        @pl.when(passes(way, h))
                        def _():
                            hop(way, h, half, n).start()

                    across(way, h, half, n).start()

    def for_crossed(half, one):
        for way, h in STREAMS:
            for n in range(1, STREAM_HOPS[way][h] + 1):

                @pl.when(takes(way, h, n))
                def _(way=way, h=h, n=n):
                    one(across(way, h, half, n))

    def attend(blocks_of, first):
        for i in range(HG):
            q = qb[i]
            blocks = blocks_of(i)
            scores = [
                lax.dot_general(
                    q, k_block(), (((1,), (1,)), ((), ())), preferred_element_type=F32
                )
                for k_block, _ in blocks
            ]
            top = functools.reduce(jnp.maximum, scores)
            top = jnp.max(top, axis=1, keepdims=True)
            top = jnp.broadcast_to(top, (NBLK, HD))
            if not first:
                old = peak[i]
                top = jnp.maximum(old, top)
            peak[i] = top
            wide = jnp.concatenate([top, top], axis=1)
            part = None
            mixed = None
            for (_, v_block), score in zip(blocks, scores):
                weights = jnp.exp2((score - wide) * EXP2_SCALE)
                halves = weights[:, :HD] + weights[:, HD:]
                part = halves if part is None else part + halves
                term = jnp.dot(weights.astype(BF16), v_block(), preferred_element_type=F32)
                mixed = term if mixed is None else mixed + term
            if first:
                total[i] = part
                acc[i] = mixed
            else:
                fade = jnp.exp2((old - top) * EXP2_SCALE)
                total[i] = total[i] * fade + part
                acc[i] = acc[i] * fade + mixed

    def joined(one, other):
        return lambda: jnp.concatenate([one(), other()], axis=0)

    def blocks_of(half, with_own, arrivals):
        def of(i):
            out = []
            if with_own:
                lanes = head_cols(item_head[i])
                out.append(
                    tuple(
                        joined(
                            lambda t=t: own[half, t, :, lanes], lambda t=t: beside[half, t, :, lanes]
                        )
                        for t in range(2)
                    )
                )
            for k in arrivals:
                slot = pick(ORDER[i][k], y)
                out.append(
                    tuple(
                        joined(
                            lambda t=t, slot=slot: ring[slot, half, t],
                            lambda t=t, slot=slot: cross[slot, half, t],
                        )
                        for t in range(2)
                    )
                )
            return out

        return of

    start_streams(0)
    cw_ref[:, 48:, :] = jnp.zeros((9, 80, cw_ref.shape[2]), BF16)
    pass_on(0, 1)
    pass_on(0, 2)
    start_streams(1)
    pass_on(0, 3)
    pass_on(0, 4)
    pass_on(1, 1)
    await_stage(2, 0, NZ)

    def query_copy(j):
        return remote(
            q_own.at[:, pl.ds(j * HD, HD)],
            qb.at[query_slot[j]],
            q_send.at[j],
            q_recv.at[query_slot[j]],
            s,
            ring_seq(query_chip[j]),
        )

    for j in range(HG):

        @pl.when(query_chip[j] != y)
        def _(j=j):
            query_copy(j).start()

        @pl.when(query_chip[j] == y)
        def _(j=j):
            pltpu.make_async_copy(
                q_own.at[:, pl.ds(j * HD, HD)], qb.at[query_slot[j]], q_recv.at[query_slot[j]]
            ).start()

    pass_on(1, 2)
    for i in range(HG):
        pltpu.make_async_copy(q_own.at[:, pl.ds(0, HD)], qb.at[i], q_recv.at[i]).wait()
    own_across(0).wait_recv()
    for_crossed(0, lambda copy: copy.wait_recv())
    attend(blocks_of(0, True, (0, 1, 2)), True)
    pass_on(1, 3)
    attend(blocks_of(0, False, (3, 4, 5, 6)), False)
    pass_on(1, 4)
    own_across(1).wait_recv()
    for_crossed(1, lambda copy: copy.wait_recv())
    attend(blocks_of(1, True, (0, 1, 2)), False)
    attend(blocks_of(1, False, (3, 4, 5, 6)), False)

    def back_copy(i, place):
        zp = (z + NEAREST[place]) % NZ
        return remote(
            ob.at[i, block_rows(place), :],
            att.at[:, head_cols(z * HG + item_head[i])],
            o_send.at[i, place],
            o_recv.at[item_head[i], place],
            swap_sec,
            swap_seq(zp, item_y[i]),
        )

    for i in range(HG):
        ob[i] = (acc[i] / jnp.sum(total[i], axis=1, keepdims=True)).astype(BF16)
        for place in range(NZ - 1, 0, -1):
            back_copy(i, place).start()
        here = jnp.logical_and(stays, item_y[i] == y)

        @pl.when(jnp.logical_not(here))
        def _(i=i):
            back_copy(i, 0).start()

        @pl.when(here)
        def _(i=i):
            pltpu.make_async_copy(
                ob.at[i, block_rows(0), :],
                att.at[:, head_cols(z * HG + item_head[i])],
                o_recv.at[item_head[i], 0],
            ).start()

    for load in loads:
        load.wait()
    for place in range(NZ):
        zp = (z + NZ - NEAREST[place]) % NZ
        for h in range(HG):
            pltpu.make_async_copy(
                ob.at[0, block_rows(0), :], att.at[:, head_cols(zp * HG + h)], o_recv.at[h, place]
            ).wait()

    hidden = res_ref[...].astype(F32) + gate_ref[...] * att[...].astype(F32)
    center = hidden - jnp.mean(hidden, axis=1, keepdims=True)
    normed = center * lax.rsqrt(jnp.mean(center * center, axis=1, keepdims=True) + norm_eps)
    modulated = (normed * (1.0 + scale_ref[...]) + shift_ref[...]).astype(BF16)
    patches = (
        lax.dot_general(
            modulated, fw_ref[...], (((1,), (1,)), ((), ())), preferred_element_type=F32
        )
        + fb_ref[...]
    ) / scaling
    pat[...] = patches.astype(BF16).astype(F32)
    even = pat[pl.ds(0, F, stride=2), :]
    odd = pat[pl.ds(1, F, stride=2), :]
    side = 2 * LATC
    tile = jnp.concatenate([even[:, :side], odd[:, :side], even[:, side:], odd[:, side:]], axis=1)
    tiles[0, 0:1, :] = tile[:1]
    tiles[0, 1:2, :] = tile[:1]
    tiles[0, 2:8, :] = tile[:6]
    for part in (1, 2):
        tiles[part] = tile[4 * part - 2 : 4 * part + 6]
    tiles[3, 0:6, :] = tile[10:16]
    tiles[3, 6:8, :] = tile[14:16]

    def frames_copy(ds):
        sp = (s + ds) % 4
        return remote(
            tiles.at[sp], near_tiles.at[4, s], sec_send.at[ds], sec_recv.at[4 - ds], sp, g
        )

    for ds in range(1, 4):
        frames_copy(ds).start()
    near_tiles[4, s] = tiles[s]

    def halo_copy(dy, dx):
        place = (1 - dy) * 3 + 1 - dx
        return remote(
            near_tiles.at[4],
            near_tiles.at[place],
            halo_send.at[place],
            halo_recv.at[place],
            s,
            g + dy * 2 * NY + dx,
        )

    for dy, dx in neighbours:

        @pl.when(jnp.logical_not(there(dy, dx)))
        def _(dy=dy, dx=dx):
            near_tiles[(1 + dy) * 3 + 1 + dx] = jnp.zeros((4, 8, 128), F32)

    for ds in range(1, 4):
        pltpu.make_async_copy(
            tiles.at[0], near_tiles.at[4, (s + ds) % 4], sec_recv.at[ds]
        ).wait()
    for dy, dx in neighbours:

        @pl.when(there(dy, dx))
        def _(dy=dy, dx=dx):
            halo_copy(dy, dx).start()

    for t in range(3):

        @pl.when(moves)
        def _(t=t):
            stage_copy(t, 0).wait_send()

        for place in range(1, NZ):
            stage_copy(t, place).wait_send()
    for j in range(HG):

        @pl.when(query_chip[j] != y)
        def _(j=j):
            query_copy(j).wait_send()

    for half in range(HALVES):
        own_across(half).wait_send()
        for way, h in STREAMS:

            @pl.when(sends_own(way, h))
            def _(way=way, h=h, half=half):
                own_hop(way, h, half).wait_send()

            for n in range(1, STREAM_HOPS[way][h]):

                @pl.when(jnp.logical_and(takes(way, h, n), passes(way, h)))
                def _(way=way, h=h, half=half, n=n):
                    hop(way, h, half, n).wait_send()

        for_crossed(half, lambda copy: copy.wait_send())
    for i in range(HG):
        for place in range(1, NZ):
            back_copy(i, place).wait_send()

        @pl.when(jnp.logical_not(jnp.logical_and(stays, item_y[i] == y)))
        def _(i=i):
            back_copy(i, 0).wait_send()

    for ds in range(1, 4):
        frames_copy(ds).wait_send()

    for dy, dx in neighbours:

        @pl.when(there(dy, dx))
        def _(dy=dy, dx=dx):
            place = (1 + dy) * 3 + 1 + dx
            pltpu.make_async_copy(
                near_tiles.at[4], near_tiles.at[place], halo_recv.at[place]
            ).wait()

    for yy in range(4):
        vert, dr = ((0, 1), (1, 0), (1, 1), (2, 0))[yy]
        lo = dr * BC * LATC
        hi = lo + BC * LATC
        sides = [near_tiles[vert * 3 + dx].reshape(32, 128) for dx in range(3)]
        strip = jnp.concatenate(
            [
                sides[0][:, hi - LATC : hi],
                sides[1][:, lo:hi],
                sides[2][:, lo : lo + LATC],
                jnp.zeros((32, 2 * LATC), F32),
            ],
            axis=1,
        )
        for x in range(BC):
            moved = strip if x == 0 else pltpu.roll(strip, 128 - x * LATC, axis=1)
            moved = moved.reshape(4, 8, 128)
            for dt in range(3):
                piece = moved[:, dt : dt + 4, :].reshape(16, 128)
                for dy in range(3):
                    row = yy - dy
                    if 0 <= row < BR:
                        windows[dt * 3 + dy, pl.ds(row * BC + x, 16, stride=8), :] = piece
    left_side = jnp.concatenate([windows[tap].astype(BF16) for tap in range(9)], axis=1)
    conv = jnp.dot(
        left_side, cw_ref[...].reshape(9 * 128, cw_ref.shape[2]), preferred_element_type=F32
    )
    conv = (conv + cb_ref[...]) * gg_ref[...] + gb_ref[...]
    out_ref[...] = (conv / (1.0 + jnp.exp(-conv))).astype(BF16)

    for dy, dx in neighbours:

        @pl.when(there(dy, dx))
        def _(dy=dy, dx=dx):
            halo_copy(dy, dx).wait_send()


def on_device(
    queries,
    keys,
    values,
    residual,
    shift_mod,
    scale_mod,
    gate_mod,
    final_weight,
    final_bias,
    conv_weight,
    conv_bias,
    group_gain,
    group_bias,
):
    any_spec = pl.BlockSpec(memory_space=pl.ANY)
    dma = pltpu.SemaphoreType.DMA
    vae_width = conv_weight.shape[1]
    slots = 2 * HG * MOST_HOPS
    features = pl.pallas_call(
        whole_kernel,
        out_shape=jax.ShapeDtypeStruct((4 * 4 * BR * BC, vae_width), BF16),
        in_specs=[any_spec] * 13,
        out_specs=pl.BlockSpec(memory_space=pltpu.VMEM),
        scratch_shapes=[
            pltpu.VMEM((NBLK, GW), BF16),
            pltpu.VMEM((HALVES, 2, HALF, GW), BF16),
            pltpu.VMEM((HALVES, 2, HALF, GW), BF16),
            pltpu.VMEM((slots, HALVES, 2, HALF, HD), BF16),
            pltpu.VMEM((slots, HALVES, 2, HALF, HD), BF16),
            pltpu.VMEM((HG, NBLK, HD), BF16),
            pltpu.VMEM((HG, NBLK, HD), BF16),
            pltpu.VMEM((TOK, H * HD), BF16),
            pltpu.VMEM((HG, NBLK, HD), F32),
            pltpu.VMEM((HG, NBLK, HD), F32),
            pltpu.VMEM((HG, NBLK, HD), F32),
            pltpu.VMEM((TOK, 4 * LATC), F32),
            pltpu.VMEM((4, 8, 128), F32),
            pltpu.VMEM((9, 4, 8, 128), F32),
            pltpu.VMEM((9, 4 * 4 * BR * BC, 128), F32),
            pltpu.VMEM((TOK, H * HD), BF16),
            pltpu.VMEM((1, H * HD), F32),
            pltpu.VMEM((1, H * HD), F32),
            pltpu.VMEM((1, H * HD), F32),
            pltpu.VMEM((4 * LATC, H * HD), BF16),
            pltpu.VMEM((1, 4 * LATC), F32),
            pltpu.VMEM((9, 128, vae_width), BF16),
            pltpu.VMEM((1, vae_width), F32),
            pltpu.VMEM((1, vae_width), F32),
            pltpu.VMEM((1, vae_width), F32),
            dma((9,)),
            dma((9,)),
            dma((3, NZ)),
            dma((3, NZ)),
            dma((HG,)),
            dma((HG,)),
            dma((HALVES, slots)),
            dma((HALVES, slots)),
            dma((HALVES, slots)),
            dma((HALVES,)),
            dma((HALVES,)),
            dma((HALVES, slots)),
            dma((HALVES, slots)),
            dma((HG, NZ)),
            dma((HG, NZ)),
            dma((4,)),
            dma((4,)),
            dma((9,)),
            dma((9,)),
        ],
        compiler_params=pltpu.CompilerParams(
            collective_id=0, has_side_effects=True, vmem_limit_bytes=60 * 1024 * 1024
        ),
        name="whole",
    )(
        queries[0],
        keys[0],
        values[0],
        residual[0],
        shift_mod,
        scale_mod,
        gate_mod,
        final_weight.T,
        final_bias[None],
        conv_weight,
        conv_bias[None],
        group_gain[None],
        group_bias[None],
    )
    return features.reshape(4, 4, 1, BR * BC, vae_width)


def solution(mesh):
    return jax.shard_map(
        on_device,
        mesh=mesh,
        in_specs=(
            P("sec", "seq", None),
            P("sec", "seq", None),
            P("sec", "seq", None),
            P("sec", "seq", None),
            P("sec", None),
            P("sec", None),
            P("sec", None),
            P(),
            P(),
            P(),
            P(),
            P(),
            P(),
        ),
        out_specs=P(None, "sec", "seq", None, None),
        check_vma=False,
    )
```

time: 74.8 us -> 82.7 us (1.11)
  the two profiles are of different devices: /device:TPU:1 before, /device:TPU:40 now
where the time goes in v2:
time: 82.7 us; the launch traced here: 82.5 us
  Pallas kernels  80.9 us (98%)
  local copies, waits for them, and re-layouts  1.57 us (2%)
    pallas_call x1, Pallas kernels, on_device(): pl.pallas_call(whole_kernel, out_shape=jax.ShapeDtypeStruct((4 * 4 * BR *...  80.9 us

profile of v2, /device:TPU:40, one launch (start us, length us, event | category | flops | bytes accessed | tf_op | source)
XLA Modules:
  0.0 82.5 jit_solution(18358465871751614734)
XLA Ops:
  0.0 80.9 %whole.1 = bf16[128,512]{1,0:T(8,128)(2,1)} custom-call(bf16[32,3072]{1,0:T(8,128)(2,1)} %bitcast.14, bf16[32,3072]{1,0:T(8,128)(2,1)} %bitcast.15, bf16[32,3072]{1,0:T(8,128)(2,1)} %bitcast.16, bf16[32,3072]{1,0:T(8,128)(2,1)} %bitcast.17, f32[1,3072]{1,0:T(1,128)} %shift_hbm.1, f32[1,3072]{1,0:T(1,128)} %scale_hbm.1, f32[1,3072]{1,0:T(1,128)} %gate_hbm.1, ...), custom_call_target="tpu_custom_call" | custom-call | tf_op jit(solution)/shard_map/whole/pallas_call | solution.py:710
  80.9 1.6 %copy.16 = bf16[4,4,1,8,512]{4,3,2,1,0:T(8,128)(2,1)} copy(bf16[4,4,1,8,512]{4,3,2,1,0:T(8,128)(2,1)} %bitcast.12) | data formatting | bytes 262144

commit v3 on v2

--- a/solution.py
+++ b/solution.py
@@ -101,48 +101,16 @@
     return out
 
 
-def whole_kernel(
+def gather_kernel(
     q_ref,
     k_ref,
     v_ref,
-    res_hbm,
-    shift_hbm,
-    scale_hbm,
-    gate_hbm,
-    fw_hbm,
-    fb_hbm,
-    cw_hbm,
-    cb_hbm,
-    gg_hbm,
-    gb_hbm,
-    out_ref,
-    q_own,
+    qb,
     own,
     beside,
     ring,
     cross,
-    qb,
-    ob,
-    att,
-    peak,
-    total,
-    acc,
-    pat,
-    tiles,
-    near_tiles,
-    windows,
-    res_ref,
-    shift_ref,
-    scale_ref,
-    gate_ref,
-    fw_ref,
-    fb_ref,
-    cw_ref,
-    cb_ref,
-    gg_ref,
-    gb_ref,
-    load_sem,
-    cw_sem,
+    q_own,
     s1_send,
     s1_recv,
     q_send,
@@ -154,12 +122,6 @@
     beside_recv,
     cross_send,
     cross_recv,
-    o_send,
-    o_recv,
-    sec_send,
-    sec_recv,
-    halo_send,
-    halo_recv,
 ):
     s, g, core, xl, z, y, xh = position()
     stays = core == xh
@@ -174,8 +136,6 @@
 
     steps = (1, NY - 1)
     sibling = xl * 2 + 1 - core
-    col = y * 2 + xh
-    last_col = 2 * NY - 1
 
     item_head = [pick([ITEMS[k][i][0] for k in range(NY)], y) for i in range(HG)]
     item_y = [pick([ITEMS[k][i][1] for k in range(NY)], y) for i in range(HG)]
@@ -199,13 +159,6 @@
     def step_of(way, h, n):
         return jnp.minimum(n, places[way, h] - STREAM_ENTRY[way][h] + 1)
 
-    def there(dy, dx):
-        row_ok = z + dy >= 0 if dy < 0 else z + dy < NZ
-        col_ok = col + dx >= 0 if dx < 0 else col + dx <= last_col
-        return jnp.logical_and(row_ok, col_ok)
-
-    neighbours = [(dy, dx) for dy, dx in AROUND if (dy, dx) != (0, 0)]
-
     barrier = pltpu.get_barrier_semaphore()
     for e in NEAREST[1:]:
         signal(barrier, swap_sec, swap_seq((z + e) % NZ, y))
@@ -216,41 +169,8 @@
 
     for e in range(1, NY):
         signal(barrier, s, ring_seq((y + e) % NY))
-    for ds in range(1, 4):
-        signal(barrier, (s + ds) % 4, g)
-    for dy, dx in neighbours:
-
-        @pl.when(there(dy, dx))
-        def _(dy=dy, dx=dx):
-            signal(barrier, s, g + dy * 2 * NY + dx)
-
-    loads = [
-        pltpu.make_async_copy(src, dst, load_sem.at[i])
-        for i, (src, dst) in enumerate(
-            (
-                (res_hbm, res_ref),
-                (shift_hbm, shift_ref),
-                (scale_hbm, scale_ref),
-                (gate_hbm, gate_ref),
-                (fw_hbm, fw_ref),
-                (fb_hbm, fb_ref),
-                (cb_hbm, cb_ref),
-                (gg_hbm, gg_ref),
-                (gb_hbm, gb_ref),
-            )
-        )
-    ] + [
-        pltpu.make_async_copy(
-            cw_hbm.at[pl.ds(tap * 48, 48), :], cw_ref.at[tap, pl.ds(0, 48), :], cw_sem.at[tap]
-        )
-        for tap in range(9)
-    ]
-    for load in loads:
-        load.start()
-
-    n_rows = 3 - jnp.where(z == 0, 1, 0) - jnp.where(z == NZ - 1, 1, 0)
-    n_cols = 3 - jnp.where(col == 0, 1, 0) - jnp.where(col == last_col, 1, 0)
-    pl.semaphore_wait(barrier, 2 * NZ + 1 - jnp.where(stays, 1, 0) + n_rows * n_cols)
+    signal(barrier, sibling, g)
+    pl.semaphore_wait(barrier, 2 * NZ - jnp.where(stays, 1, 0))
 
     def group_cols(zp):
         return pl.ds(pl.multiple_of(zp * GW, HD), GW)
@@ -392,6 +312,81 @@
                 @pl.when(takes(way, h, n))
                 def _(way=way, h=h, n=n):
                     one(across(way, h, half, n))
+
+    start_streams(0)
+    for step in range(1, MOST_STEPS + 1):
+        pass_on(0, step)
+        if step == 2:
+            start_streams(1)
+    pass_on(1, 1)
+    await_stage(2, 0, NZ)
+
+    def query_copy(j):
+        return remote(
+            q_own.at[:, pl.ds(j * HD, HD)],
+            qb.at[query_slot[j]],
+            q_send.at[j],
+            q_recv.at[query_slot[j]],
+            s,
+            ring_seq(query_chip[j]),
+        )
+
+    for j in range(HG):
+
+        @pl.when(query_chip[j] != y)
+        def _(j=j):
+            query_copy(j).start()
+
+        @pl.when(query_chip[j] == y)
+        def _(j=j):
+            pltpu.make_async_copy(
+                q_own.at[:, pl.ds(j * HD, HD)], qb.at[query_slot[j]], q_recv.at[query_slot[j]]
+            ).start()
+
+    for step in range(2, MOST_STEPS + 1):
+        pass_on(1, step)
+    for i in range(HG):
+        pltpu.make_async_copy(q_own.at[:, pl.ds(0, HD)], qb.at[i], q_recv.at[i]).wait()
+    for half in range(HALVES):
+        own_across(half).wait_recv()
+        for_crossed(half, lambda copy: copy.wait_recv())
+    for t in range(3):
+
+        @pl.when(moves)
+        def _(t=t):
+            stage_copy(t, 0).wait_send()
+
+        for place in range(1, NZ):
+            stage_copy(t, place).wait_send()
+    for j in range(HG):
+
+        @pl.when(query_chip[j] != y)
+        def _(j=j):
+            query_copy(j).wait_send()
+
+    for half in range(HALVES):
+        own_across(half).wait_send()
+        for way, h in STREAMS:
+
+            @pl.when(sends_own(way, h))
+            def _(way=way, h=h, half=half):
+                own_hop(way, h, half).wait_send()
+
+            for n in range(1, STREAM_HOPS[way][h]):
+
+                @pl.when(jnp.logical_and(takes(way, h, n), passes(way, h)))
+                def _(way=way, h=h, half=half, n=n):
+                    hop(way, h, half, n).wait_send()
+
+        for_crossed(half, lambda copy: copy.wait_send())
+
+
+def attention_kernel(qb, own, beside, ring, cross, ob, peak, total, acc):
+    y = (lax.axis_index("seq") // 2) % NY
+    item_head = [pick([ITEMS[k][i][0] for k in range(NY)], y) for i in range(HG)]
+
+    def head_cols(h):
+        return pl.ds(pl.multiple_of(h * HD, HD), HD)
 
     def attend(blocks_of, first):
         for i in range(HG):
@@ -458,51 +453,97 @@
 
         return of
 
-    start_streams(0)
-    cw_ref[:, 48:, :] = jnp.zeros((9, 80, cw_ref.shape[2]), BF16)
-    pass_on(0, 1)
-    pass_on(0, 2)
-    start_streams(1)
-    pass_on(0, 3)
-    pass_on(0, 4)
-    pass_on(1, 1)
-    await_stage(2, 0, NZ)
-
-    def query_copy(j):
-        return remote(
-            q_own.at[:, pl.ds(j * HD, HD)],
-            qb.at[query_slot[j]],
-            q_send.at[j],
-            q_recv.at[query_slot[j]],
-            s,
-            ring_seq(query_chip[j]),
-        )
-
-    for j in range(HG):
-
-        @pl.when(query_chip[j] != y)
-        def _(j=j):
-            query_copy(j).start()
-
-        @pl.when(query_chip[j] == y)
-        def _(j=j):
-            pltpu.make_async_copy(
-                q_own.at[:, pl.ds(j * HD, HD)], qb.at[query_slot[j]], q_recv.at[query_slot[j]]
-            ).start()
-
-    pass_on(1, 2)
-    for i in range(HG):
-        pltpu.make_async_copy(q_own.at[:, pl.ds(0, HD)], qb.at[i], q_recv.at[i]).wait()
-    own_across(0).wait_recv()
-    for_crossed(0, lambda copy: copy.wait_recv())
     attend(blocks_of(0, True, (0, 1, 2)), True)
-    pass_on(1, 3)
     attend(blocks_of(0, False, (3, 4, 5, 6)), False)
-    pass_on(1, 4)
-    own_across(1).wait_recv()
-    for_crossed(1, lambda copy: copy.wait_recv())
     attend(blocks_of(1, True, (0, 1, 2)), False)
     attend(blocks_of(1, False, (3, 4, 5, 6)), False)
+    for i in range(HG):
+        ob[i] = (acc[i] / jnp.sum(total[i], axis=1, keepdims=True)).astype(BF16)
+
+
+def return_kernel(
+    ob,
+    res_hbm,
+    shift_ref,
+    scale_ref,
+    gate_ref,
+    fw_ref,
+    fb_ref,
+    near_tiles,
+    att,
+    pat,
+    tiles,
+    res_ref,
+    load_sem,
+    o_send,
+    o_recv,
+    sec_send,
+    sec_recv,
+    halo_send,
+    halo_recv,
+):
+    s, g, core, xl, z, y, xh = position()
+    stays = core == xh
+    moves = jnp.logical_not(stays)
+    swap_sec = xl * 2 + xh
+
+    def swap_seq(zp, yp):
+        return (zp * NY + yp) * 2 + core
+
+    def ring_seq(yp):
+        return (z * NY + yp) * 2 + xh
+
+    col = y * 2 + xh
+    last_col = 2 * NY - 1
+
+    item_head = [pick([ITEMS[k][i][0] for k in range(NY)], y) for i in range(HG)]
+    item_y = [pick([ITEMS[k][i][1] for k in range(NY)], y) for i in range(HG)]
+    homes = {item: (k, i) for k in range(NY) for i, item in enumerate(ITEMS[k])}
+    query_chip = [pick([homes[j, k][0] for k in range(NY)], y) for j in range(HG)]
+    query_slot = [pick([homes[j, k][1] for k in range(NY)], y) for j in range(HG)]
+    def there(dy, dx):
+        row_ok = z + dy >= 0 if dy < 0 else z + dy < NZ
+        col_ok = col + dx >= 0 if dx < 0 else col + dx <= last_col
+        return jnp.logical_and(row_ok, col_ok)
+
+    neighbours = [(dy, dx) for dy, dx in AROUND if (dy, dx) != (0, 0)]
+
+    load = pltpu.make_async_copy(res_hbm, res_ref, load_sem)
+    load.start()
+
+    barrier = pltpu.get_barrier_semaphore()
+    for j in range(HG):
+        here = jnp.logical_and(stays, query_chip[j] == y)
+        for e in NEAREST[1:]:
+            signal(barrier, swap_sec, swap_seq((z + e) % NZ, query_chip[j]))
+
+        @pl.when(jnp.logical_not(here))
+        def _(j=j):
+            signal(barrier, swap_sec, swap_seq(z, query_chip[j]))
+
+    for ds in range(1, 4):
+        signal(barrier, (s + ds) % 4, g)
+    for dy, dx in neighbours:
+
+        @pl.when(there(dy, dx))
+        def _(dy=dy, dx=dx):
+            signal(barrier, s, g + dy * 2 * NY + dx)
+
+    n_rows = 3 - jnp.where(z == 0, 1, 0) - jnp.where(z == NZ - 1, 1, 0)
+    n_cols = 3 - jnp.where(col == 0, 1, 0) - jnp.where(col == last_col, 1, 0)
+    at_home = pick([sum(item[1] == k for item in ITEMS[k]) for k in range(NY)], y)
+    pl.semaphore_wait(
+        barrier, HG * NZ + 2 - jnp.where(stays, at_home, 0) + n_rows * n_cols
+    )
+
+    def group_cols(zp):
+        return pl.ds(pl.multiple_of(zp * GW, HD), GW)
+
+    def head_cols(h):
+        return pl.ds(pl.multiple_of(h * HD, HD), HD)
+
+    def block_rows(place):
+        return pl.ds(place * TOK, TOK)
 
     def back_copy(i, place):
         zp = (z + NEAREST[place]) % NZ
@@ -516,7 +557,6 @@
         )
 
     for i in range(HG):
-        ob[i] = (acc[i] / jnp.sum(total[i], axis=1, keepdims=True)).astype(BF16)
         for place in range(NZ - 1, 0, -1):
             back_copy(i, place).start()
         here = jnp.logical_and(stays, item_y[i] == y)
@@ -533,8 +573,7 @@
                 o_recv.at[item_head[i], 0],
             ).start()
 
-    for load in loads:
-        load.wait()
+    load.wait()
     for place in range(NZ):
         zp = (z + NZ - NEAREST[place]) % NZ
         for h in range(HG):
@@ -602,35 +641,6 @@
         def _(dy=dy, dx=dx):
             halo_copy(dy, dx).start()
 
-    for t in range(3):
-
-        @pl.when(moves)
-        def _(t=t):
-            stage_copy(t, 0).wait_send()
-
-        for place in range(1, NZ):
-            stage_copy(t, place).wait_send()
-    for j in range(HG):
-
-        @pl.when(query_chip[j] != y)
-        def _(j=j):
-            query_copy(j).wait_send()
-
-    for half in range(HALVES):
-        own_across(half).wait_send()
-        for way, h in STREAMS:
-
-            @pl.when(sends_own(way, h))
-            def _(way=way, h=h, half=half):
-                own_hop(way, h, half).wait_send()
-
-            for n in range(1, STREAM_HOPS[way][h]):
-
-                @pl.when(jnp.logical_and(takes(way, h, n), passes(way, h)))
-                def _(way=way, h=h, half=half, n=n):
-                    hop(way, h, half, n).wait_send()
-
-        for_crossed(half, lambda copy: copy.wait_send())
     for i in range(HG):
         for place in range(1, NZ):
             back_copy(i, place).wait_send()
@@ -651,6 +661,23 @@
                 near_tiles.at[4], near_tiles.at[place], halo_recv.at[place]
             ).wait()
 
+    for dy, dx in neighbours:
+
+        @pl.when(there(dy, dx))
+        def _(dy=dy, dx=dx):
+            halo_copy(dy, dx).wait_send()
+
+
+def conv_kernel(near_tiles, cw_hbm, cb_ref, gg_ref, gb_ref, out_ref, windows, cw_ref, cw_sem):
+    loads = [
+        pltpu.make_async_copy(
+            cw_hbm.at[pl.ds(tap * 48, 48), :], cw_ref.at[tap, pl.ds(0, 48), :], cw_sem.at[tap]
+        )
+        for tap in range(9)
+    ]
+    for load in loads:
+        load.start()
+    cw_ref[:, 48:, :] = jnp.zeros((9, 80, cw_ref.shape[2]), BF16)
     for yy in range(4):
         vert, dr = ((0, 1), (1, 0), (1, 1), (2, 0))[yy]
         lo = dr * BC * LATC
@@ -674,18 +701,14 @@
                     row = yy - dy
                     if 0 <= row < BR:
                         windows[dt * 3 + dy, pl.ds(row * BC + x, 16, stride=8), :] = piece
+    for load in loads:
+        load.wait()
     left_side = jnp.concatenate([windows[tap].astype(BF16) for tap in range(9)], axis=1)
     conv = jnp.dot(
         left_side, cw_ref[...].reshape(9 * 128, cw_ref.shape[2]), preferred_element_type=F32
     )
     conv = (conv + cb_ref[...]) * gg_ref[...] + gb_ref[...]
     out_ref[...] = (conv / (1.0 + jnp.exp(-conv))).astype(BF16)
-
-    for dy, dx in neighbours:
-
-        @pl.when(there(dy, dx))
-        def _(dy=dy, dx=dx):
-            halo_copy(dy, dx).wait_send()
 
 
 def on_device(
@@ -707,39 +730,21 @@
     dma = pltpu.SemaphoreType.DMA
     vae_width = conv_weight.shape[1]
     slots = 2 * HG * MOST_HOPS
-    features = pl.pallas_call(
-        whole_kernel,
-        out_shape=jax.ShapeDtypeStruct((4 * 4 * BR * BC, vae_width), BF16),
-        in_specs=[any_spec] * 13,
-        out_specs=pl.BlockSpec(memory_space=pltpu.VMEM),
+    vmem = pl.BlockSpec(memory_space=pltpu.VMEM)
+    limit = 30 * 1024 * 1024
+    q_items, own, beside, ring, cross = pl.pallas_call(
+        gather_kernel,
+        out_shape=[
+            jax.ShapeDtypeStruct((HG, NBLK, HD), BF16),
+            jax.ShapeDtypeStruct((HALVES, 2, HALF, GW), BF16),
+            jax.ShapeDtypeStruct((HALVES, 2, HALF, GW), BF16),
+            jax.ShapeDtypeStruct((slots, HALVES, 2, HALF, HD), BF16),
+            jax.ShapeDtypeStruct((slots, HALVES, 2, HALF, HD), BF16),
+        ],
+        in_specs=[any_spec] * 3,
+        out_specs=[vmem] * 5,
         scratch_shapes=[
             pltpu.VMEM((NBLK, GW), BF16),
-            pltpu.VMEM((HALVES, 2, HALF, GW), BF16),
-            pltpu.VMEM((HALVES, 2, HALF, GW), BF16),
-            pltpu.VMEM((slots, HALVES, 2, HALF, HD), BF16),
-            pltpu.VMEM((slots, HALVES, 2, HALF, HD), BF16),
-            pltpu.VMEM((HG, NBLK, HD), BF16),
-            pltpu.VMEM((HG, NBLK, HD), BF16),
-            pltpu.VMEM((TOK, H * HD), BF16),
-            pltpu.VMEM((HG, NBLK, HD), F32),
-            pltpu.VMEM((HG, NBLK, HD), F32),
-            pltpu.VMEM((HG, NBLK, HD), F32),
-            pltpu.VMEM((TOK, 4 * LATC), F32),
-            pltpu.VMEM((4, 8, 128), F32),
-            pltpu.VMEM((9, 4, 8, 128), F32),
-            pltpu.VMEM((9, 4 * 4 * BR * BC, 128), F32),
-            pltpu.VMEM((TOK, H * HD), BF16),
-            pltpu.VMEM((1, H * HD), F32),
-            pltpu.VMEM((1, H * HD), F32),
-            pltpu.VMEM((1, H * HD), F32),
-            pltpu.VMEM((4 * LATC, H * HD), BF16),
-            pltpu.VMEM((1, 4 * LATC), F32),
-            pltpu.VMEM((9, 128, vae_width), BF16),
-            pltpu.VMEM((1, vae_width), F32),
-            pltpu.VMEM((1, vae_width), F32),
-            pltpu.VMEM((1, vae_width), F32),
-            dma((9,)),
-            dma((9,)),
             dma((3, NZ)),
             dma((3, NZ)),
             dma((HG,)),
@@ -751,6 +756,36 @@
             dma((HALVES,)),
             dma((HALVES, slots)),
             dma((HALVES, slots)),
+        ],
+        compiler_params=pltpu.CompilerParams(
+            collective_id=0, has_side_effects=True, vmem_limit_bytes=limit
+        ),
+        name="gather",
+    )(queries[0], keys[0], values[0])
+    mixed = pl.pallas_call(
+        attention_kernel,
+        out_shape=jax.ShapeDtypeStruct((HG, NBLK, HD), BF16),
+        in_specs=[vmem] * 5,
+        out_specs=vmem,
+        scratch_shapes=[
+            pltpu.VMEM((HG, NBLK, HD), F32),
+            pltpu.VMEM((HG, NBLK, HD), F32),
+            pltpu.VMEM((HG, NBLK, HD), F32),
+        ],
+        compiler_params=pltpu.CompilerParams(vmem_limit_bytes=limit),
+        name="attention",
+    )(q_items, own, beside, ring, cross)
+    near_tiles = pl.pallas_call(
+        return_kernel,
+        out_shape=jax.ShapeDtypeStruct((9, 4, 8, 128), F32),
+        in_specs=[vmem, any_spec] + [vmem] * 5,
+        out_specs=vmem,
+        scratch_shapes=[
+            pltpu.VMEM((TOK, H * HD), BF16),
+            pltpu.VMEM((TOK, 4 * LATC), F32),
+            pltpu.VMEM((4, 8, 128), F32),
+            pltpu.VMEM((TOK, H * HD), BF16),
+            dma(()),
             dma((HG, NZ)),
             dma((HG, NZ)),
             dma((4,)),
@@ -759,24 +794,31 @@
             dma((9,)),
         ],
         compiler_params=pltpu.CompilerParams(
-            collective_id=0, has_side_effects=True, vmem_limit_bytes=60 * 1024 * 1024
+            collective_id=1, has_side_effects=True, vmem_limit_bytes=limit
         ),
-        name="whole",
+        name="return",
     )(
-        queries[0],
-        keys[0],
-        values[0],
+        mixed,
         residual[0],
         shift_mod,
         scale_mod,
         gate_mod,
         final_weight.T,
         final_bias[None],
-        conv_weight,
-        conv_bias[None],
-        group_gain[None],
-        group_bias[None],
     )
+    features = pl.pallas_call(
+        conv_kernel,
+        out_shape=jax.ShapeDtypeStruct((4 * 4 * BR * BC, vae_width), BF16),
+        in_specs=[vmem, any_spec, vmem, vmem, vmem],
+        out_specs=vmem,
+        scratch_shapes=[
+            pltpu.VMEM((9, 4 * 4 * BR * BC, 128), F32),
+            pltpu.VMEM((9, 128, vae_width), BF16),
+            dma((9,)),
+        ],
+        compiler_params=pltpu.CompilerParams(vmem_limit_bytes=limit),
+        name="convolution",
+    )(near_tiles, conv_weight, conv_bias[None], group_gain[None], group_bias[None])
     return features.reshape(4, 4, 1, BR * BC, vae_width)
 
 

time: 82.7 us -> 93.6 us (1.13)
  the two profiles are of different devices: /device:TPU:40 before, /device:TPU:1 now
where the time goes in v3:
time: 93.6 us; the launch traced here: 92.5 us
  Pallas kernels  89.4 us (96%)
  local copies, waits for them, and re-layouts  2.84 us (3%)
    pallas_call x1, Pallas kernels, on_device(): pl.pallas_call(gather_kernel, out_shape=[jax.ShapeDtypeStruct((HG, NBLK,...  51.4 us
    pallas_call x1, Pallas kernels, on_device(): pl.pallas_call(return_kernel, out_shape=jax.ShapeDtypeStruct((9, 4, 8, 12...  30.3 us
    pallas_call x1, Pallas kernels, on_device(): pl.pallas_call(attention_kernel, out_shape=jax.ShapeDtypeStruct((HG, NBLK...  5.73 us
    unnamed x26, local copies, waits for them, and re-layouts  2.84 us
    pallas_call x1, Pallas kernels, on_device(): pl.pallas_call(conv_kernel, out_shape=jax.ShapeDtypeStruct((4 * 4 * BR *...  2.02 us

profile of v3, /device:TPU:1, one launch (start us, length us, event | category | flops | bytes accessed | tf_op | source)
XLA Modules:
  0.0 92.5 jit_solution(8101961452825388671)
XLA Ops:
  0.0 0.0 copy-start.3
  0.0 0.9 %copy-done.3 = bf16[1,32,3072]{2,1,0:T(8,128)(2,1)S(1)} copy-done((bf16[1,32,3072]{2,1,0:T(8,128)(2,1)S(1)}, bf16[1,32,3072]{2,1,0:T(8,128)(2,1)}, u32[]{:S(2)}) %copy-start.3) | copy-done | bytes 196632
  0.9 0.0 copy-start.4
  0.9 0.9 %copy-done.4 = bf16[1,32,3072]{2,1,0:T(8,128)(2,1)S(1)} copy-done((bf16[1,32,3072]{2,1,0:T(8,128)(2,1)S(1)}, bf16[1,32,3072]{2,1,0:T(8,128)(2,1)}, u32[]{:S(2)}) %copy-start.4) | copy-done | bytes 196632
  1.9 0.0 copy-start.5
  1.9 0.9 %copy-done.5 = bf16[1,32,3072]{2,1,0:T(8,128)(2,1)S(1)} copy-done((bf16[1,32,3072]{2,1,0:T(8,128)(2,1)S(1)}, bf16[1,32,3072]{2,1,0:T(8,128)(2,1)}, u32[]{:S(2)}) %copy-start.5) | copy-done | bytes 196632
  2.8 51.4 %gather.1 = (bf16[3,256,128]{2,1,0:T(8,128)(2,1)S(1)}, bf16[2,2,128,384]{3,2,1,0:T(8,128)(2,1)S(1)}, bf16[2,2,128,384]{3,2,1,0:T(8,128)(2,1)S(1)}, bf16[30,2,2,1...) custom-call(bf16[32,3072]{1,0:T(8,128)(2,1)S(1)} %bitcast.14, bf16[32,3072]{1,0:T(8,128)(2,1)S(1)} %bitcast.15, ...), custom_call_target="tpu_custom_call" | custom-call | tf_op jit(solution)/shard_map/gather/pallas_call | solution.py:735
  54.2 0.0 copy-start.1
  54.2 0.0 copy-start.2
  54.2 0.0 copy-start.6
  54.2 0.0 copy-start.7
  54.2 0.0 copy-start.8
  54.2 0.0 copy-start.12
  54.2 0.0 copy-start
  54.3 0.0 copy-start.9
  54.3 0.0 copy-start.10
  54.3 0.0 copy-start.11
  54.3 5.7 %attention.1.ob = bf16[3,256,128]{2,1,0:T(8,128)(2,1)S(1)} custom-call(bf16[3,256,128]{2,1,0:T(8,128)(2,1)S(1)} %get-tuple-element.10.qb, bf16[2,2,128,384]{3,2,1,0:T(8,128)(2,1)S(1)} %get-tuple-element.11.own, bf16[2,2,128,384]{3,2,1,0:T(8,128)(2,1)S(1)} %get-tuple-element.12.beside, bf16[30,2,2,128,128]{4,3,2,1,0:T(8,128)(2,1)S(1)} %get-tuple-element.13.ring, ...), custom_call_target="tpu_custom_call" | custom-call | tf_op jit(solution)/shard_map/attention/pallas_call | solution.py:765
  60.0 0.0 copy-done.1
  60.0 0.0 copy-done.2
  60.0 0.0 copy-done.6
  60.1 0.0 copy-done.7
  60.1 0.0 copy-done.8
  60.1 0.0 copy-done.12
  60.1 30.3 %return.1.near_tiles = f32[9,4,8,128]{3,2,1,0:T(8,128)S(1)} custom-call(bf16[3,256,128]{2,1,0:T(8,128)(2,1)S(1)} %attention.1.ob, bf16[32,3072]{1,0:T(8,128)(2,1)S(1)} %bitcast.13, f32[1,3072]{1,0:T(1,128)S(1)} %copy-done.6, f32[1,3072]{1,0:T(1,128)S(1)} %copy-done.7, f32[1,3072]{1,0:T(1,128)S(1)} %copy-done.8, bf16[64,3072]{1,0:T(8,128)(2,1)S(1)} %bitcast.12, ...), custom_call_target="tpu_custom_call" | custom-call | tf_op jit(solution)/shard_map/return/pallas_call | solution.py:778
  90.4 0.0 copy-done
  90.4 0.0 copy-done.9
  90.4 0.0 copy-done.10
  90.4 0.0 copy-done.11
  90.4 2.0 %convolution.1 = bf16[128,512]{1,0:T(8,128)(2,1)} custom-call(f32[9,4,8,128]{3,2,1,0:T(8,128)S(1)} %return.1.near_tiles, bf16[432,512]{1,0:T(8,128)(2,1)S(1)} %copy-done, f32[1,512]{1,0:T(1,128)S(1)} %bitcast.17, f32[1,512]{1,0:T(1,128)S(1)} %bitcast.18, f32[1,512]{1,0:T(1,128)S(1)} %bitcast.19), custom_call_target="tpu_custom_call" | custom-call | tf_op jit(solution)/shard_map/convolution/pallas_call | solution.py:809
Async XLA Ops:
  0.0 0.9 %copy-start.3 = (bf16[1,32,3072]{2,1,0:T(8,128)(2,1)S(1)}, bf16[1,32,3072]{2,1,0:T(8,128)(2,1)}, u32[]{:S(2)}) copy-start(bf16[1,32,3072]{2,1,0:T(8,128)(2,1)} %param.13) | copy-start | bytes 589828
  0.9 0.9 %copy-start.4 = (bf16[1,32,3072]{2,1,0:T(8,128)(2,1)S(1)}, bf16[1,32,3072]{2,1,0:T(8,128)(2,1)}, u32[]{:S(2)}) copy-start(bf16[1,32,3072]{2,1,0:T(8,128)(2,1)} %param.14) | copy-start | bytes 589828
  1.9 0.9 %copy-start.5 = (bf16[1,32,3072]{2,1,0:T(8,128)(2,1)S(1)}, bf16[1,32,3072]{2,1,0:T(8,128)(2,1)}, u32[]{:S(2)}) copy-start(bf16[1,32,3072]{2,1,0:T(8,128)(2,1)} %param.15) | copy-start | bytes 589828
  54.2 5.9 %copy-start.1 = (bf16[3072,64]{0,1:T(8,128)(2,1)S(1)}, bf16[3072,64]{0,1:T(8,128)(2,1)}, u32[]{:S(2)}) copy-start(bf16[3072,64]{0,1:T(8,128)(2,1)} %param.20) | copy-start | bytes 1179652
  54.2 5.9 %copy-start.2 = (bf16[1,32,3072]{2,1,0:T(8,128)(2,1)S(1)}, bf16[1,32,3072]{2,1,0:T(8,128)(2,1)}, u32[]{:S(2)}) copy-start(bf16[1,32,3072]{2,1,0:T(8,128)(2,1)} %param.16) | copy-start | bytes 589828
  54.2 5.9 %copy-start.6 = (f32[1,3072]{1,0:T(1,128)S(1)}, f32[1,3072]{1,0:T(1,128)}, u32[]{:S(2)}) copy-start(f32[1,3072]{1,0:T(1,128)} %shift_ref.1) | copy-start | bytes 36868
  54.2 5.9 %copy-start.7 = (f32[1,3072]{1,0:T(1,128)S(1)}, f32[1,3072]{1,0:T(1,128)}, u32[]{:S(2)}) copy-start(f32[1,3072]{1,0:T(1,128)} %scale_ref.1) | copy-start | bytes 36868
  54.2 5.8 %copy-start.8 = (f32[1,3072]{1,0:T(1,128)S(1)}, f32[1,3072]{1,0:T(1,128)}, u32[]{:S(2)}) copy-start(f32[1,3072]{1,0:T(1,128)} %gate_ref.1) | copy-start | bytes 36868
  54.2 5.8 %copy-start.12 = (f32[64]{0:T(128)S(1)}, f32[64]{0:T(128)}, u32[]{:S(2)}) copy-start(f32[64]{0:T(128)} %param.21) | copy-start | bytes 772
  54.2 36.2 %copy-start = (bf16[432,512]{1,0:T(8,128)(2,1)S(1)}, bf16[432,512]{1,0:T(8,128)(2,1)}, u32[]{:S(2)}) copy-start(bf16[432,512]{1,0:T(8,128)(2,1)} %cw_hbm.1) | copy-start | bytes 1327108
  54.3 36.2 %copy-start.9 = (f32[512]{0:T(512)S(1)}, f32[512]{0:T(512)}, u32[]{:S(2)}) copy-start(f32[512]{0:T(512)} %param.23) | copy-start | bytes 6148
  54.3 36.2 %copy-start.10 = (f32[512]{0:T(512)S(1)}, f32[512]{0:T(512)}, u32[]{:S(2)}) copy-start(f32[512]{0:T(512)} %param.24) | copy-start | bytes 6148
  54.3 36.2 %copy-start.11 = (f32[512]{0:T(512)S(1)}, f32[512]{0:T(512)}, u32[]{:S(2)}) copy-start(f32[512]{0:T(512)} %param.25) | copy-start | bytes 6148

commit v4 on v1

v4 whole, which is shorter than its diff:
```python
import functools

import jax
import jax.numpy as jnp
from jax import lax
from jax.experimental import pallas as pl
from jax.experimental.pallas import tpu as pltpu
from jax.sharding import PartitionSpec as P

H = 24
HD = 128
LATC = 16
F = 16
BR = 2
BC = 4
NZ = 8
NY = 8
TOK = 32
HG = 3
GW = HG * HD
NBLK = NZ * TOK

scaling = 0.476986
norm_eps = 1e-06
EXP2_SCALE = HD ** (-0.5) * 1.4426950408889634
F32 = jnp.float32
BF16 = jnp.bfloat16


def remote(src, dst, send_sem, recv_sem, sec, seq):
    return pltpu.make_async_remote_copy(
        src_ref=src,
        dst_ref=dst,
        send_sem=send_sem,
        recv_sem=recv_sem,
        device_id={"sec": sec, "seq": seq},
        device_id_type=pl.DeviceIdType.MESH,
    )


def signal(sem, sec, seq):
    pl.semaphore_signal(
        sem, inc=1, device_id={"sec": sec, "seq": seq}, device_id_type=pl.DeviceIdType.MESH
    )


def position():
    s = lax.axis_index("sec")
    g = lax.axis_index("seq")
    return s, g, s % 2, s // 2, g // (2 * NY), (g // 2) % NY, g % 2

NEAREST = (0, 1, 7, 2, 6, 3, 5, 4)
AROUND = [(dy, dx) for dy in (-1, 0, 1) for dx in (-1, 0, 1)]

HALVES = 2
PER_HALF = NZ // HALVES
HALF = NBLK // HALVES


def whole_kernel(
    q_ref,
    k_ref,
    v_ref,
    res_hbm,
    shift_hbm,
    scale_hbm,
    gate_hbm,
    fw_hbm,
    fb_hbm,
    cw_hbm,
    cb_hbm,
    gg_hbm,
    gb_hbm,
    out_ref,
    qb,
    kb,
    vb,
    ob,
    att,
    peak,
    total,
    acc,
    pat,
    tiles,
    near_tiles,
    windows,
    res_ref,
    shift_ref,
    scale_ref,
    gate_ref,
    fw_ref,
    fb_ref,
    cw_ref,
    cb_ref,
    gg_ref,
    gb_ref,
    load_sem,
    cw_sem,
    s1_send,
    s1_recv,
    ring_send,
    ring_recv,
    last_recv,
    cross_send,
    cross_recv,
    o_send,
    o_recv,
    halo_send,
    halo_recv,
):
    s, g, core, xl, z, y, xh = position()
    stays = core == xh
    moves = jnp.logical_not(stays)
    swap_sec = xl * 2 + xh
    sibling = xl * 2 + 1 - core
    col = y * 2 + xh

    def swap_seq(zp, yp):
        return (zp * NY + yp) * 2 + core

    def ring_seq(yp):
        return (z * NY + yp) * 2 + xh

    right = ring_seq((y + 1) % NY)
    left = ring_seq((y + NY - 1) % NY)

    neighbours = [(dy, dx) for dy, dx in AROUND if (dy, dx) != (0, 0)]

    def tile_seq(dy, dx):
        return (z + NZ + dy) % NZ * (2 * NY) + (col + 2 * NY + dx) % (2 * NY)

    barrier = pltpu.get_barrier_semaphore()
    for e in NEAREST[1:]:
        signal(barrier, swap_sec, swap_seq((z + e) % NZ, y))

    @pl.when(moves)
    def _():
        signal(barrier, swap_sec, swap_seq(z, y))

    signal(barrier, s, right)
    signal(barrier, s, left)
    for ds in range(1, 4):
        signal(barrier, (s + ds) % 4, g)
    for dy, dx in neighbours:
        signal(barrier, s, tile_seq(dy, dx))

    def group_cols(zp):
        return pl.ds(pl.multiple_of(zp * GW, HD), GW)

    def head_cols(h):
        return pl.ds(pl.multiple_of(h * HD, HD), HD)

    def block_rows(place):
        return pl.ds(place * TOK, TOK)

    def await_bytes(ref, sem):
        pltpu.make_async_copy(ref, ref, sem).wait()

    stage_one = ((k_ref, kb.at[0]), (v_ref, vb.at[0]), (q_ref, qb))

    def stage_sem(t, place):
        return s1_recv.at[t, 0 if t == 2 else place // PER_HALF]

    def stage_copy(t, place):
        src, buf = stage_one[t]
        zp = (z + NZ - NEAREST[place]) % NZ
        return remote(
            src.at[:, group_cols(zp)],
            buf.at[block_rows(place), :],
            s1_send.at[t],
            stage_sem(t, place),
            swap_sec,
            swap_seq(zp, y),
        )

    def start_stage(t):
        src, buf = stage_one[t]

        @pl.when(stays)
        def _():
            pltpu.make_async_copy(
                src.at[:, group_cols(z)], buf.at[block_rows(0), :], stage_sem(t, 0)
            ).start()

        @pl.when(moves)
        def _():
            stage_copy(t, 0).start()

        for place in range(1, NZ):
            stage_copy(t, place).start()

    pl.semaphore_wait(barrier, 2 * NZ + 5 - jnp.where(stays, 1, 0))
    for t in range(3):
        start_stage(t)

    loads = [
        pltpu.make_async_copy(src, dst, load_sem.at[i])
        for i, (src, dst) in enumerate(
            (
                (res_hbm, res_ref),
                (shift_hbm, shift_ref),
                (scale_hbm, scale_ref),
                (gate_hbm, gate_ref),
                (fw_hbm, fw_ref),
                (fb_hbm, fb_ref),
                (cb_hbm, cb_ref),
                (gg_hbm, gg_ref),
                (gb_hbm, gb_ref),
            )
        )
    ]
    for load in loads:
        load.start()
    for tap in range(9):
        pltpu.make_async_copy(
            cw_hbm.at[pl.ds(tap * 48, 48), :], cw_ref.at[tap, pl.ds(0, 48), :], cw_sem
        ).start()

    bufs = (kb, vb)

    def slot_of(way, hops):
        if hops in (0, 4):
            return hops
        return hops if way == 0 else 4 + hops

    def half_of(t, slot, half):
        return bufs[t].at[slot, pl.ds(half * HALF, HALF), :]

    def head_of(t, slot, h):
        return bufs[t].at[slot, :, pl.ds(h * HD, HD)]

    def hop(way, t, half, hops):
        return remote(
            half_of(t, slot_of(way, hops - 1), half),
            half_of(t, slot_of(way, hops), half),
            ring_send.at[way],
            ring_recv.at[way, t, half, hops],
            s,
            (right, left)[way],
        )

    def last_hop(t, h):
        return remote(
            head_of(t, slot_of(t, 3), h),
            head_of(t, 4, h),
            ring_send.at[t],
            last_recv.at[t, h],
            s,
            (right, left)[t],
        )

    def across(piece, beside, step):
        remote(piece, beside, cross_send, cross_recv.at[step], sibling, g).start()

    def half_across(t, slot, half, step):
        across(half_of(t, slot, half), half_of(t, 8 + slot, half), step)

    def attend(h, slots, first):
        lanes = slice(h * HD, (h + 1) * HD)
        q = qb[:, lanes]
        scores = [
            lax.dot_general(
                q, kb[slot, :, lanes], (((1,), (1,)), ((), ())), preferred_element_type=F32
            )
            for slot in slots
        ]
        top = functools.reduce(jnp.maximum, scores)
        top = jnp.max(top, axis=1, keepdims=True)
        top = jnp.broadcast_to(top, (NBLK, HD))
        if not first:
            old = peak[h]
            top = jnp.maximum(old, top)
        peak[h] = top
        wide = jnp.concatenate([top, top], axis=1)
        part = None
        mixed = None
        for slot, score in zip(slots, scores):
            weights = jnp.exp2((score - wide) * EXP2_SCALE)
            halves = weights[:, :HD] + weights[:, HD:]
            part = halves if part is None else part + halves
            term = jnp.dot(weights.astype(BF16), vb[slot, :, lanes], preferred_element_type=F32)
            mixed = term if mixed is None else mixed + term
        if first:
            total[h] = part
            acc[h] = mixed
        else:
            fade = jnp.exp2((old - top) * EXP2_SCALE)
            total[h] = total[h] * fade + part
            acc[h] = acc[h] * fade + mixed

    pieces = [(t, half) for t in range(2) for half in range(HALVES)]
    for t, half in pieces:
        await_bytes(half_of(t, 0, half), s1_recv.at[t, half])
        hop(0, t, half, 1).start()
        hop(1, t, half, 1).start()
        half_across(t, 0, half, 0)
    cw_ref[:, 48:, :] = jnp.zeros((9, 80, cw_ref.shape[2]), BF16)
    for n in range(1, 4):
        for t, half in pieces:
            for way in range(2):
                hop(way, t, half, n).wait_recv()
                if n < 3:
                    hop(way, t, half, n + 1).start()
                elif way == t and half == HALVES - 1:
                    for h in range(HG):
                        last_hop(t, h).start()
                half_across(t, slot_of(way, n), half, n)
        if n == 1:
            await_bytes(qb, s1_recv.at[2, 0])
            await_bytes(kb.at[pl.ds(8, 2)], cross_recv.at[0])
            for h in range(HG):
                attend(h, (0, 8), True)
        await_bytes(kb.at[pl.ds(8, 4)], cross_recv.at[n])
        for h in range(HG):
            attend(h, (n, 4 + n, 8 + n, 12 + n), False)
    for h in range(HG):
        for t in range(2):
            last_hop(t, h).wait_recv()
            across(head_of(t, 4, h), head_of(t, 12, h), 4 + h)

    def back_copy(h, place):
        zp = (z + NEAREST[place]) % NZ
        return remote(
            ob.at[h, block_rows(place), :],
            att.at[:, head_cols(z * HG + h)],
            o_send.at[h],
            o_recv,
            swap_sec,
            swap_seq(zp, y),
        )

    for h in range(HG):
        await_bytes(kb.at[pl.ds(8, 2), :, pl.ds(0, HD)], cross_recv.at[4 + h])
        attend(h, (4, 12), False)
        ob[h] = (acc[h] / jnp.sum(total[h], axis=1, keepdims=True)).astype(BF16)
        for place in range(NZ - 1, 0, -1):
            back_copy(h, place).start()

        @pl.when(moves)
        def _(h=h):
            back_copy(h, 0).start()

        @pl.when(stays)
        def _(h=h):
            pltpu.make_async_copy(
                ob.at[h, block_rows(0), :], att.at[:, head_cols(z * HG + h)], o_recv
            ).start()

    def sent_blocks(ref, sem):
        @pl.when(moves)
        def _():
            await_bytes(ref, sem)

        @pl.when(stays)
        def _():
            await_bytes(ref.at[pl.ds(0, NBLK - TOK), :], sem)

    for t in range(3):
        sent_blocks(qb, s1_send.at[t])
    for way in range(2):
        await_bytes(kb.at[pl.ds(0, 7)], ring_send.at[way])
    await_bytes(kb, cross_send)
    for load in loads:
        load.wait()
    await_bytes(att, o_recv)

    hidden = res_ref[...].astype(F32) + gate_ref[...] * att[...].astype(F32)
    center = hidden - jnp.mean(hidden, axis=1, keepdims=True)
    normed = center * lax.rsqrt(jnp.mean(center * center, axis=1, keepdims=True) + norm_eps)
    modulated = (normed * (1.0 + scale_ref[...]) + shift_ref[...]).astype(BF16)
    patches = (
        lax.dot_general(
            modulated, fw_ref[...], (((1,), (1,)), ((), ())), preferred_element_type=F32
        )
        + fb_ref[...]
    ) / scaling
    pat[...] = patches.astype(BF16).astype(F32)
    even = pat[pl.ds(0, F, stride=2), :]
    odd = pat[pl.ds(1, F, stride=2), :]
    side = 2 * LATC
    tile = jnp.concatenate([even[:, :side], odd[:, :side], even[:, side:], odd[:, side:]], axis=1)
    tiles[0, 0:1, :] = tile[:1]
    tiles[0, 1:2, :] = tile[:1]
    tiles[0, 2:8, :] = tile[:6]
    for part in (1, 2):
        tiles[part] = tile[4 * part - 2 : 4 * part + 6]
    tiles[3, 0:6, :] = tile[10:16]
    tiles[3, 6:8, :] = tile[14:16]

    for ds in range(1, 4):
        sp = (s + ds) % 4
        remote(
            tiles.at[sp], near_tiles.at[4, s], halo_send.at[0], halo_recv.at[0], sp, g
        ).start()
    near_tiles[4, s] = tiles[s]
    for h in range(HG):
        sent_blocks(ob.at[h], o_send.at[h])
    await_bytes(tiles.at[pl.ds(0, 3)], halo_recv.at[0])
    for dy, dx in neighbours:
        remote(
            near_tiles.at[4],
            near_tiles.at[(1 - dy) * 3 + 1 - dx],
            halo_send.at[1],
            halo_recv.at[1],
            s,
            tile_seq(dy, dx),
        ).start()
    await_bytes(tiles.at[pl.ds(0, 3)], halo_send.at[0])
    await_bytes(near_tiles.at[pl.ds(0, 8)], halo_recv.at[1])

    def clear(at_edge, gone):
        @pl.when(at_edge)
        def _():
            for place in gone:
                near_tiles[place] = jnp.zeros((4, 8, 128), F32)

    clear(z == 0, (0, 1, 2))
    clear(z == NZ - 1, (6, 7, 8))
    clear(col == 0, (0, 3, 6))
    clear(col == 2 * NY - 1, (2, 5, 8))

    for yy in range(4):
        vert, dr = ((0, 1), (1, 0), (1, 1), (2, 0))[yy]
        lo = dr * BC * LATC
        hi = lo + BC * LATC
        sides = [near_tiles[vert * 3 + dx].reshape(32, 128) for dx in range(3)]
        strip = jnp.concatenate(
            [
                sides[0][:, hi - LATC : hi],
                sides[1][:, lo:hi],
                sides[2][:, lo : lo + LATC],
                jnp.zeros((32, 2 * LATC), F32),
            ],
            axis=1,
        )
        for x in range(BC):
            moved = strip if x == 0 else pltpu.roll(strip, 128 - x * LATC, axis=1)
            moved = moved.reshape(4, 8, 128)
            for dt in range(3):
                piece = moved[:, dt : dt + 4, :].reshape(16, 128)
                for dy in range(3):
                    row = yy - dy
                    if 0 <= row < BR:
                        windows[dt * 3 + dy, pl.ds(row * BC + x, 16, stride=8), :] = piece
    await_bytes(cw_ref.at[:, pl.ds(0, 48), :], cw_sem)
    left_side = jnp.concatenate([windows[tap].astype(BF16) for tap in range(9)], axis=1)
    conv = jnp.dot(
        left_side, cw_ref[...].reshape(9 * 128, cw_ref.shape[2]), preferred_element_type=F32
    )
    conv = (conv + cb_ref[...]) * gg_ref[...] + gb_ref[...]
    out_ref[...] = (conv / (1.0 + jnp.exp(-conv))).astype(BF16)

    await_bytes(near_tiles.at[pl.ds(0, 8)], halo_send.at[1])


def on_device(
    queries,
    keys,
    values,
    residual,
    shift_mod,
    scale_mod,
    gate_mod,
    final_weight,
    final_bias,
    conv_weight,
    conv_bias,
    group_gain,
    group_bias,
):
    any_spec = pl.BlockSpec(memory_space=pl.ANY)
    dma = pltpu.SemaphoreType.DMA
    vae_width = conv_weight.shape[1]
    features = pl.pallas_call(
        whole_kernel,
        out_shape=jax.ShapeDtypeStruct((4 * 4 * BR * BC, vae_width), BF16),
        in_specs=[any_spec] * 13,
        out_specs=pl.BlockSpec(memory_space=pltpu.VMEM),
        scratch_shapes=[
            pltpu.VMEM((NBLK, GW), BF16),
            pltpu.VMEM((16, NBLK, GW), BF16),
            pltpu.VMEM((16, NBLK, GW), BF16),
            pltpu.VMEM((HG, NBLK, HD), BF16),
            pltpu.VMEM((TOK, H * HD), BF16),
            pltpu.VMEM((HG, NBLK, HD), F32),
            pltpu.VMEM((HG, NBLK, HD), F32),
            pltpu.VMEM((HG, NBLK, HD), F32),
            pltpu.VMEM((TOK, 4 * LATC), F32),
            pltpu.VMEM((4, 8, 128), F32),
            pltpu.VMEM((9, 4, 8, 128), F32),
            pltpu.VMEM((9, 4 * 4 * BR * BC, 128), F32),
            pltpu.VMEM((TOK, H * HD), BF16),
            pltpu.VMEM((1, H * HD), F32),
            pltpu.VMEM((1, H * HD), F32),
            pltpu.VMEM((1, H * HD), F32),
            pltpu.VMEM((4 * LATC, H * HD), BF16),
            pltpu.VMEM((1, 4 * LATC), F32),
            pltpu.VMEM((9, 128, vae_width), BF16),
            pltpu.VMEM((1, vae_width), F32),
            pltpu.VMEM((1, vae_width), F32),
            pltpu.VMEM((1, vae_width), F32),
            dma((9,)),
            dma(()),
            dma((3,)),
            dma((3, HALVES)),
            dma((2,)),
            dma((2, 2, HALVES, 4)),
            dma((2, HG)),
            dma(()),
            dma((4 + HG,)),
            dma((HG,)),
            dma(()),
            dma((2,)),
            dma((2,)),
        ],
        compiler_params=pltpu.CompilerParams(
            collective_id=0, has_side_effects=True, vmem_limit_bytes=60 * 1024 * 1024
        ),
        name="whole",
    )(
        queries[0],
        keys[0],
        values[0],
        residual[0],
        shift_mod,
        scale_mod,
        gate_mod,
        final_weight.T,
        final_bias[None],
        conv_weight,
        conv_bias[None],
        group_gain[None],
        group_bias[None],
    )
    return features.reshape(4, 4, 1, BR * BC, vae_width)


def solution(mesh):
    return jax.shard_map(
        on_device,
        mesh=mesh,
        in_specs=(
            P("sec", "seq", None),
            P("sec", "seq", None),
            P("sec", "seq", None),
            P("sec", "seq", None),
            P("sec", None),
            P("sec", None),
            P("sec", None),
            P(),
            P(),
            P(),
            P(),
            P(),
            P(),
        ),
        out_specs=P(None, "sec", "seq", None, None),
        check_vma=False,
    )
```

time: 74.8 us -> 77.1 us (1.031)
  Pallas kernels: 73 us -> 75.4 us
    pallas_call x1, Pallas kernels: 73 us -> 75.4 us  [on_device(): pl.pallas_call(whole_kernel, out_shape=jax.ShapeDtypeStruct((4 * 4 * BR *...]
where the time goes in v4:
time: 77.1 us; the launch traced here: 77 us
  Pallas kernels  75.4 us (98%)
  local copies, waits for them, and re-layouts  1.57 us (2%)
    pallas_call x1, Pallas kernels, on_device(): pl.pallas_call(whole_kernel, out_shape=jax.ShapeDtypeStruct((4 * 4 * BR *...  75.4 us
    unnamed x1, local copies, waits for them, and re-layouts  1.57 us

profile of v4, /device:TPU:1, one launch (start us, length us, event | category | flops | bytes accessed | tf_op | source)
XLA Modules:
  0.0 77.0 jit_solution(7895544751599506731)
XLA Ops:
  0.0 75.4 %whole.1 = bf16[128,512]{1,0:T(8,128)(2,1)} custom-call(bf16[32,3072]{1,0:T(8,128)(2,1)} %bitcast.14, bf16[32,3072]{1,0:T(8,128)(2,1)} %bitcast.15, bf16[32,3072]{1,0:T(8,128)(2,1)} %bitcast.16, bf16[32,3072]{1,0:T(8,128)(2,1)} %bitcast.17, f32[1,3072]{1,0:T(1,128)} %shift_hbm.1, f32[1,3072]{1,0:T(1,128)} %scale_hbm.1, f32[1,3072]{1,0:T(1,128)} %gate_hbm.1, ...), custom_call_target="tpu_custom_call" | custom-call | tf_op jit(solution)/shard_map/whole/pallas_call | solution.py:474
  75.4 1.6 %copy.16 = bf16[4,4,1,8,512]{4,3,2,1,0:T(8,128)(2,1)} copy(bf16[4,4,1,8,512]{4,3,2,1,0:T(8,128)(2,1)} %bitcast.12) | data formatting | bytes 262144

commit v5 on v4

v5 whole, which is shorter than its diff:
```python
import functools

import jax
import jax.numpy as jnp
from jax import lax
from jax.experimental import pallas as pl
from jax.experimental.pallas import tpu as pltpu
from jax.sharding import PartitionSpec as P

H = 24
HD = 128
LATC = 16
F = 16
BR = 2
BC = 4
NZ = 8
NY = 8
TOK = 32
HG = 3
GW = HG * HD
NBLK = NZ * TOK

scaling = 0.476986
norm_eps = 1e-06
EXP2_SCALE = HD ** (-0.5) * 1.4426950408889634
F32 = jnp.float32
BF16 = jnp.bfloat16


def remote(src, dst, send_sem, recv_sem, sec, seq):
    return pltpu.make_async_remote_copy(
        src_ref=src,
        dst_ref=dst,
        send_sem=send_sem,
        recv_sem=recv_sem,
        device_id={"sec": sec, "seq": seq},
        device_id_type=pl.DeviceIdType.MESH,
    )


def signal(sem, sec, seq):
    pl.semaphore_signal(
        sem, inc=1, device_id={"sec": sec, "seq": seq}, device_id_type=pl.DeviceIdType.MESH
    )


def position():
    s = lax.axis_index("sec")
    g = lax.axis_index("seq")
    return s, g, s % 2, s // 2, g // (2 * NY), (g // 2) % NY, g % 2

NEAREST = (0, 1, 7, 2, 6, 3, 5, 4)
AROUND = [(dy, dx) for dy in (-1, 0, 1) for dx in (-1, 0, 1)]

ITEMS = (
    ((0, 0), (0, 7), (0, 6)),
    ((0, 1), (0, 2), (0, 5)),
    ((0, 3), (0, 4), (1, 1)),
    ((1, 2), (1, 3), (1, 0)),
    ((1, 4), (1, 5), (1, 7)),
    ((1, 6), (2, 3), (2, 4)),
    ((2, 5), (2, 6), (2, 2)),
    ((2, 7), (2, 0), (2, 1)),
)
STREAM_START = ((5, 0, 3), (4, 7, 2))
STREAM_HOPS = ((5, 5, 4), (4, 5, 5))
STREAM_ENTRY = ((3, 2, 2), (2, 2, 3))
MOST_HOPS = 5
MOST_STEPS = 4
HALVES = 2
PER_HALF = NZ // HALVES
HALF = NBLK // HALVES
STREAMS = [(way, h) for h in range(HG) for way in range(2)]


def stream_place(way, h, chip):
    first = STREAM_START[way][h]
    return (chip - first) % NY if way == 0 else (first - chip) % NY


def slot_of(way, h, n):
    return (h * 2 + way) * MOST_HOPS + n - 1


def chip_plan(chip):
    own_sends = []
    arrivals = [[] for _ in range(MOST_STEPS + 1)]
    for way, h in STREAMS:
        place = stream_place(way, h, chip)
        entry = STREAM_ENTRY[way][h]
        hops = STREAM_HOPS[way][h]
        if place < hops:
            target = max(entry, place + 1)
            ahead = target - place
            to = (chip + ahead) % NY if way == 0 else (chip - ahead) % NY
            own_sends.append((ahead, h, slot_of(way, h, ahead), to))
        if entry <= place <= hops:
            for n in range(1, place + 1):
                step = min(n, place - entry + 1)
                arrivals[step].append((n, slot_of(way, h, n), place < hops, way))
    own_sends = [item[1:] for item in sorted(own_sends, reverse=True)]
    return own_sends, [[item[1:] for item in sorted(step)] for step in arrivals]


PLANS = [chip_plan(chip) for chip in range(NY)]


def block_order(chip, h):
    slots = [item[0] for step in PLANS[chip][1] for item in step]
    return [slot for slot in slots if slot // (2 * MOST_HOPS) == h]


ORDER = [
    [[block_order(chip, ITEMS[chip][i][0])[k] for chip in range(NY)] for k in range(NY - 1)]
    for i in range(HG)
]


def pick(table, index):
    out = table[0]
    for k in range(1, len(table)):
        out = jnp.where(index == k, table[k], out)
    return out


def whole_kernel(
    q_ref,
    k_ref,
    v_ref,
    res_hbm,
    shift_hbm,
    scale_hbm,
    gate_hbm,
    fw_hbm,
    fb_hbm,
    cw_hbm,
    cb_hbm,
    gg_hbm,
    gb_hbm,
    out_ref,
    q_all,
    k_all,
    v_all,
    kv_pack,
    q_pack,
    kv_land,
    q_land,
    q_own,
    own,
    beside,
    ring,
    cross,
    qb,
    ob,
    att,
    peak,
    total,
    acc,
    pat,
    tiles,
    near_tiles,
    windows,
    res_ref,
    shift_ref,
    scale_ref,
    gate_ref,
    fw_ref,
    fb_ref,
    cw_ref,
    cb_ref,
    gg_ref,
    gb_ref,
    in_sem,
    load_sem,
    cw_sem,
    s1_send,
    s1_recv,
    q_send,
    q_recv,
    ring_send,
    ring_recv,
    beside_send,
    beside_recv,
    cross_send,
    cross_recv,
    o_send,
    o_recv,
    halo_send,
    halo_recv,
):
    s, g, core, xl, z, y, xh = position()
    stays = core == xh
    moves = jnp.logical_not(stays)
    swap_sec = xl * 2 + xh
    sibling = xl * 2 + 1 - core
    col = y * 2 + xh

    def swap_seq(zp, yp):
        return (zp * NY + yp) * 2 + core

    def ring_seq(yp):
        return (z * NY + yp) * 2 + xh

    neighbours = [(dy, dx) for dy, dx in AROUND if (dy, dx) != (0, 0)]

    def tile_seq(dy, dx):
        return (z + NZ + dy) % NZ * (2 * NY) + (col + 2 * NY + dx) % (2 * NY)

    fetches = [
        pltpu.make_async_copy(src, dst, in_sem.at[t])
        for t, (src, dst) in enumerate(((k_ref, k_all), (v_ref, v_all), (q_ref, q_all)))
    ]
    for fetch in fetches:
        fetch.start()

    barrier = pltpu.get_barrier_semaphore()
    for e in NEAREST[1:]:
        signal(barrier, swap_sec, swap_seq((z + e) % NZ, y))

    @pl.when(moves)
    def _():
        signal(barrier, swap_sec, swap_seq(z, y))

    for e in range(1, NY):
        signal(barrier, s, ring_seq((y + e) % NY))
    for ds in range(1, 4):
        signal(barrier, (s + ds) % 4, g)
    for dy, dx in neighbours:
        signal(barrier, s, tile_seq(dy, dx))

    item_head = [pick([ITEMS[k][i][0] for k in range(NY)], y) for i in range(HG)]
    item_y = [pick([ITEMS[k][i][1] for k in range(NY)], y) for i in range(HG)]

    def group_cols(zp):
        return pl.ds(pl.multiple_of(zp * GW, HD), GW)

    def block_rows(place):
        return pl.ds(place * TOK, TOK)

    def await_bytes(ref, sem):
        pltpu.make_async_copy(ref, ref, sem).wait()

    def group_at(place):
        return (z + NZ - NEAREST[place]) % NZ

    for fetch in fetches:
        fetch.wait()
    for place in range(NZ):
        cols = group_cols(group_at(place))
        kv_pack[place, 0] = k_all[:, cols]
        kv_pack[place, 1] = v_all[:, cols]
        q_pack[place] = q_all[:, cols]

    def start_stage(pack, land, send_sem, recv_sem, first, last):
        for place in range(first, last):

            def copy(place=place):
                return remote(
                    pack.at[place],
                    land.at[place],
                    send_sem,
                    recv_sem,
                    swap_sec,
                    swap_seq(group_at(place), y),
                )

            if place > 0:
                copy().start()
                continue

            @pl.when(stays)
            def _():
                pltpu.make_async_copy(pack.at[0], land.at[0], recv_sem).start()

            @pl.when(moves)
            def _():
                copy().start()

    pl.semaphore_wait(barrier, 3 * NZ + 2 - jnp.where(stays, 1, 0))
    for half in range(HALVES):
        start_stage(
            kv_pack,
            kv_land,
            s1_send.at[0],
            s1_recv.at[half],
            half * PER_HALF,
            (half + 1) * PER_HALF,
        )
    start_stage(q_pack, q_land, s1_send.at[1], s1_recv.at[HALVES], 0, NZ)

    loads = [
        pltpu.make_async_copy(src, dst, load_sem.at[i])
        for i, (src, dst) in enumerate(
            (
                (res_hbm, res_ref),
                (shift_hbm, shift_ref),
                (scale_hbm, scale_ref),
                (gate_hbm, gate_ref),
                (fw_hbm, fw_ref),
                (fb_hbm, fb_ref),
                (cb_hbm, cb_ref),
                (gg_hbm, gg_ref),
                (gb_hbm, gb_ref),
            )
        )
    ]
    for load in loads:
        load.start()
    for tap in range(9):
        pltpu.make_async_copy(
            cw_hbm.at[pl.ds(tap * 48, 48), :], cw_ref.at[tap, pl.ds(0, 48), :], cw_sem
        ).start()

    def own_hop(half, h, slot, to):
        return remote(
            own.at[half, h],
            ring.at[slot, half],
            ring_send.at[half],
            ring_recv.at[half, slot],
            s,
            ring_seq(to),
        )

    def hop(half, slot, to):
        return remote(
            ring.at[slot, half],
            ring.at[slot + 1, half],
            ring_send.at[half],
            ring_recv.at[half, slot + 1],
            s,
            ring_seq(to),
        )

    def across(src, dst, send_sem, recv_sem):
        remote(src, dst, send_sem, recv_sem, sibling, g).start()

    def by_chip(one):
        for chip in range(NY):

            @pl.when(y == chip)
            def _(chip=chip):
                one(chip)

    def start_streams(half):
        landed = range(half * PER_HALF, (half + 1) * PER_HALF)
        await_bytes(kv_land.at[pl.ds(half * PER_HALF, PER_HALF)], s1_recv.at[half])
        for place in landed:
            rows = block_rows(place % PER_HALF)
            for t in range(2):
                for h in range(HG):
                    own[half, h, t, rows, :] = kv_land[place, t, :, h * HD : (h + 1) * HD]

        def one(chip):
            for h, slot, to in PLANS[chip][0]:
                own_hop(half, h, slot, to).start()

        by_chip(one)
        across(own.at[half], beside.at[half], beside_send.at[half], beside_recv.at[half])

    def pass_on(half, *steps):
        def one(chip):
            for step in steps:
                for slot, passed, way in PLANS[chip][1][step]:
                    await_bytes(ring.at[slot, half], ring_recv.at[half, slot])
                    if passed:
                        hop(half, slot, (chip + (1, NY - 1)[way]) % NY).start()
                    across(
                        ring.at[slot, half],
                        cross.at[slot, half],
                        cross_send.at[half],
                        cross_recv.at[half],
                    )

        by_chip(one)

    def count_arrivals(chip):
        return sum(len(step) for step in PLANS[chip][1])

    def await_crossed(half, own_sem, sem):
        await_bytes(own.at[half], own_sem.at[half])
        by_chip(lambda chip: await_bytes(cross.at[pl.ds(0, count_arrivals(chip)), half], sem.at[half]))

    def attend(blocks_of, first):
        for i in range(HG):
            q = qb[i]
            blocks = blocks_of(i)
            scores = [
                lax.dot_general(
                    q, k_block(), (((1,), (1,)), ((), ())), preferred_element_type=F32
                )
                for k_block, _ in blocks
            ]
            top = functools.reduce(jnp.maximum, scores)
            top = jnp.max(top, axis=1, keepdims=True)
            top = jnp.broadcast_to(top, (NBLK, HD))
            if not first:
                old = peak[i]
                top = jnp.maximum(old, top)
            peak[i] = top
            wide = jnp.concatenate([top, top], axis=1)
            part = None
            mixed = None
            for (_, v_block), score in zip(blocks, scores):
                weights = jnp.exp2((score - wide) * EXP2_SCALE)
                halves = weights[:, :HD] + weights[:, HD:]
                part = halves if part is None else part + halves
                term = jnp.dot(weights.astype(BF16), v_block(), preferred_element_type=F32)
                mixed = term if mixed is None else mixed + term
            if first:
                total[i] = part
                acc[i] = mixed
            else:
                fade = jnp.exp2((old - top) * EXP2_SCALE)
                total[i] = total[i] * fade + part
                acc[i] = acc[i] * fade + mixed

    def joined(one, other):
        return lambda: jnp.concatenate([one(), other()], axis=0)

    def blocks_of(half, with_own, arrivals):
        def of(i):
            out = []
            if with_own:
                h = item_head[i]
                out.append(
                    tuple(
                        joined(
                            lambda t=t: own[half, h, t], lambda t=t: beside[half, h, t]
                        )
                        for t in range(2)
                    )
                )
            for k in arrivals:
                slot = pick(ORDER[i][k], y)
                out.append(
                    tuple(
                        joined(
                            lambda t=t, slot=slot: ring[slot, half, t],
                            lambda t=t, slot=slot: cross[slot, half, t],
                        )
                        for t in range(2)
                    )
                )
            return out

        return of

    start_streams(0)
    pass_on(0, 1)
    pass_on(0, 2)
    start_streams(1)
    pass_on(0, 3, 4)
    pass_on(1, 1)
    cw_ref[:, 48:, :] = jnp.zeros((9, 80, cw_ref.shape[2]), BF16)

    await_bytes(q_land, s1_recv.at[HALVES])
    for place in range(NZ):
        for h in range(HG):
            q_own[h, block_rows(place), :] = q_land[place, :, h * HD : (h + 1) * HD]
    homes = {item: (k, i) for k in range(NY) for i, item in enumerate(ITEMS[k])}

    def send_queries(chip):
        for j in range(HG):
            to, slot = homes[j, chip]
            src = q_own.at[j]
            if to == chip:
                pltpu.make_async_copy(src, qb.at[slot], q_recv).start()
            else:
                remote(src, qb.at[slot], q_send, q_recv, s, ring_seq(to)).start()

    by_chip(send_queries)
    pass_on(1, 2)
    await_bytes(qb, q_recv)
    await_crossed(0, beside_recv, cross_recv)
    attend(blocks_of(0, True, (0, 1, 2)), True)
    pass_on(1, 3)
    attend(blocks_of(0, False, (3, 4, 5, 6)), False)
    pass_on(1, 4)
    await_crossed(1, beside_recv, cross_recv)
    attend(blocks_of(1, True, (0, 1, 2)), False)
    attend(blocks_of(1, False, (3, 4, 5, 6)), False)

    def back_copy(i, place):
        zp = (z + NEAREST[place]) % NZ
        return remote(
            ob.at[i, block_rows(place), :],
            att.at[z * HG + item_head[i]],
            o_send.at[i],
            o_recv,
            swap_sec,
            swap_seq(zp, item_y[i]),
        )

    at_home = [jnp.logical_and(stays, item_y[i] == y) for i in range(HG)]
    for i in range(HG):
        ob[i] = (acc[i] / jnp.sum(total[i], axis=1, keepdims=True)).astype(BF16)
        for place in range(NZ - 1, 0, -1):
            back_copy(i, place).start()

        @pl.when(jnp.logical_not(at_home[i]))
        def _(i=i):
            back_copy(i, 0).start()

        @pl.when(at_home[i])
        def _(i=i):
            pltpu.make_async_copy(
                ob.at[i, block_rows(0), :], att.at[z * HG + item_head[i]], o_recv
            ).start()

    for pack, sem in ((kv_pack, s1_send.at[0]), (q_pack, s1_send.at[1])):

        @pl.when(moves)
        def _(pack=pack, sem=sem):
            await_bytes(pack, sem)

        @pl.when(stays)
        def _(pack=pack, sem=sem):
            await_bytes(pack.at[pl.ds(0, NZ - 1)], sem)

    def ring_sent(chip):
        count = len(PLANS[chip][0]) + sum(
            passed for step in PLANS[chip][1] for _, passed, _ in step
        )
        for half in range(HALVES):
            await_bytes(ring.at[pl.ds(0, count), half], ring_send.at[half])
        away = sum(homes[j, chip][0] != chip for j in range(HG))
        await_bytes(qb.at[pl.ds(0, away)], q_send)

    by_chip(ring_sent)
    for half in range(HALVES):
        await_crossed(half, beside_send, cross_send)
    for load in loads:
        load.wait()
    await_bytes(att, o_recv)

    attended = jnp.concatenate([att[h] for h in range(H)], axis=1)
    hidden = res_ref[...].astype(F32) + gate_ref[...] * attended.astype(F32)
    center = hidden - jnp.mean(hidden, axis=1, keepdims=True)
    normed = center * lax.rsqrt(jnp.mean(center * center, axis=1, keepdims=True) + norm_eps)
    modulated = (normed * (1.0 + scale_ref[...]) + shift_ref[...]).astype(BF16)
    patches = (
        lax.dot_general(
            modulated, fw_ref[...], (((1,), (1,)), ((), ())), preferred_element_type=F32
        )
        + fb_ref[...]
    ) / scaling
    pat[...] = patches.astype(BF16).astype(F32)
    even = pat[pl.ds(0, F, stride=2), :]
    odd = pat[pl.ds(1, F, stride=2), :]
    side = 2 * LATC
    tile = jnp.concatenate([even[:, :side], odd[:, :side], even[:, side:], odd[:, side:]], axis=1)
    tiles[0, 0:1, :] = tile[:1]
    tiles[0, 1:2, :] = tile[:1]
    tiles[0, 2:8, :] = tile[:6]
    for part in (1, 2):
        tiles[part] = tile[4 * part - 2 : 4 * part + 6]
    tiles[3, 0:6, :] = tile[10:16]
    tiles[3, 6:8, :] = tile[14:16]

    for ds in range(1, 4):
        sp = (s + ds) % 4
        remote(
            tiles.at[sp], near_tiles.at[4, s], halo_send.at[0], halo_recv.at[0], sp, g
        ).start()
    near_tiles[4, s] = tiles[s]
    for i in range(HG):

        @pl.when(at_home[i])
        def _(i=i):
            await_bytes(ob.at[i, pl.ds(0, NBLK - TOK), :], o_send.at[i])

        @pl.when(jnp.logical_not(at_home[i]))
        def _(i=i):
            await_bytes(ob.at[i], o_send.at[i])

    await_bytes(tiles.at[pl.ds(0, 3)], halo_recv.at[0])
    for dy, dx in neighbours:
        remote(
            near_tiles.at[4],
            near_tiles.at[(1 - dy) * 3 + 1 - dx],
            halo_send.at[1],
            halo_recv.at[1],
            s,
            tile_seq(dy, dx),
        ).start()
    await_bytes(tiles.at[pl.ds(0, 3)], halo_send.at[0])
    await_bytes(near_tiles.at[pl.ds(0, 8)], halo_recv.at[1])

    def clear(at_edge, gone):
        @pl.when(at_edge)
        def _():
            for place in gone:
                near_tiles[place] = jnp.zeros((4, 8, 128), F32)

    clear(z == 0, (0, 1, 2))
    clear(z == NZ - 1, (6, 7, 8))
    clear(col == 0, (0, 3, 6))
    clear(col == 2 * NY - 1, (2, 5, 8))

    for yy in range(4):
        vert, dr = ((0, 1), (1, 0), (1, 1), (2, 0))[yy]
        lo = dr * BC * LATC
        hi = lo + BC * LATC
        sides = [near_tiles[vert * 3 + dx].reshape(32, 128) for dx in range(3)]
        strip = jnp.concatenate(
            [
                sides[0][:, hi - LATC : hi],
                sides[1][:, lo:hi],
                sides[2][:, lo : lo + LATC],
                jnp.zeros((32, 2 * LATC), F32),
            ],
            axis=1,
        )
        for x in range(BC):
            moved = strip if x == 0 else pltpu.roll(strip, 128 - x * LATC, axis=1)
            moved = moved.reshape(4, 8, 128)
            for dt in range(3):
                piece = moved[:, dt : dt + 4, :].reshape(16, 128)
                for dy in range(3):
                    row = yy - dy
                    if 0 <= row < BR:
                        windows[dt * 3 + dy, pl.ds(row * BC + x, 16, stride=8), :] = piece
    await_bytes(cw_ref.at[:, pl.ds(0, 48), :], cw_sem)
    left_side = jnp.concatenate([windows[tap].astype(BF16) for tap in range(9)], axis=1)
    conv = jnp.dot(
        left_side, cw_ref[...].reshape(9 * 128, cw_ref.shape[2]), preferred_element_type=F32
    )
    conv = (conv + cb_ref[...]) * gg_ref[...] + gb_ref[...]
    out_ref[...] = (conv / (1.0 + jnp.exp(-conv))).astype(BF16)

    await_bytes(near_tiles.at[pl.ds(0, 8)], halo_send.at[1])


def on_device(
    queries,
    keys,
    values,
    residual,
    shift_mod,
    scale_mod,
    gate_mod,
    final_weight,
    final_bias,
    conv_weight,
    conv_bias,
    group_gain,
    group_bias,
):
    any_spec = pl.BlockSpec(memory_space=pl.ANY)
    dma = pltpu.SemaphoreType.DMA
    vae_width = conv_weight.shape[1]
    slots = 2 * HG * MOST_HOPS
    features = pl.pallas_call(
        whole_kernel,
        out_shape=jax.ShapeDtypeStruct((4 * 4 * BR * BC, vae_width), BF16),
        in_specs=[any_spec] * 13,
        out_specs=pl.BlockSpec(memory_space=pltpu.VMEM),
        scratch_shapes=[
            pltpu.VMEM((TOK, H * HD), BF16),
            pltpu.VMEM((TOK, H * HD), BF16),
            pltpu.VMEM((TOK, H * HD), BF16),
            pltpu.VMEM((NZ, 2, TOK, GW), BF16),
            pltpu.VMEM((NZ, TOK, GW), BF16),
            pltpu.VMEM((NZ, 2, TOK, GW), BF16),
            pltpu.VMEM((NZ, TOK, GW), BF16),
            pltpu.VMEM((HG, NBLK, HD), BF16),
            pltpu.VMEM((HALVES, HG, 2, HALF, HD), BF16),
            pltpu.VMEM((HALVES, HG, 2, HALF, HD), BF16),
            pltpu.VMEM((slots, HALVES, 2, HALF, HD), BF16),
            pltpu.VMEM((slots, HALVES, 2, HALF, HD), BF16),
            pltpu.VMEM((HG, NBLK, HD), BF16),
            pltpu.VMEM((HG, NBLK, HD), BF16),
            pltpu.VMEM((H, TOK, HD), BF16),
            pltpu.VMEM((HG, NBLK, HD), F32),
            pltpu.VMEM((HG, NBLK, HD), F32),
            pltpu.VMEM((HG, NBLK, HD), F32),
            pltpu.VMEM((TOK, 4 * LATC), F32),
            pltpu.VMEM((4, 8, 128), F32),
            pltpu.VMEM((9, 4, 8, 128), F32),
            pltpu.VMEM((9, 4 * 4 * BR * BC, 128), F32),
            pltpu.VMEM((TOK, H * HD), BF16),
            pltpu.VMEM((1, H * HD), F32),
            pltpu.VMEM((1, H * HD), F32),
            pltpu.VMEM((1, H * HD), F32),
            pltpu.VMEM((4 * LATC, H * HD), BF16),
            pltpu.VMEM((1, 4 * LATC), F32),
            pltpu.VMEM((9, 128, vae_width), BF16),
            pltpu.VMEM((1, vae_width), F32),
            pltpu.VMEM((1, vae_width), F32),
            pltpu.VMEM((1, vae_width), F32),
            dma((3,)),
            dma((9,)),
            dma(()),
            dma((2,)),
            dma((HALVES + 1,)),
            dma(()),
            dma(()),
            dma((HALVES,)),
            dma((HALVES, slots)),
            dma((HALVES,)),
            dma((HALVES,)),
            dma((HALVES,)),
            dma((HALVES,)),
            dma((HG,)),
            dma(()),
            dma((2,)),
            dma((2,)),
        ],
        compiler_params=pltpu.CompilerParams(
            collective_id=0, has_side_effects=True, vmem_limit_bytes=60 * 1024 * 1024
        ),
        name="whole",
    )(
        queries[0],
        keys[0],
        values[0],
        residual[0],
        shift_mod,
        scale_mod,
        gate_mod,
        final_weight.T,
        final_bias[None],
        conv_weight,
        conv_bias[None],
        group_gain[None],
        group_bias[None],
    )
    return features.reshape(4, 4, 1, BR * BC, vae_width)


def solution(mesh):
    return jax.shard_map(
        on_device,
        mesh=mesh,
        in_specs=(
            P("sec", "seq", None),
            P("sec", "seq", None),
            P("sec", "seq", None),
            P("sec", "seq", None),
            P("sec", None),
            P("sec", None),
            P("sec", None),
            P(),
            P(),
            P(),
            P(),
            P(),
            P(),
        ),
        out_specs=P(None, "sec", "seq", None, None),
        check_vma=False,
    )
```

time: 77.1 us -> 79.4 us (1.030)
  Pallas kernels: 75.4 us -> 76.9 us
    pallas_call x1, Pallas kernels: 75.4 us -> 76.9 us  [on_device(): pl.pallas_call(whole_kernel, out_shape=jax.ShapeDtypeStruct((4 * 4 * BR *...]
where the time goes in v5:
time: 79.4 us; the launch traced here: 78.5 us
  Pallas kernels  76.9 us (97%)
  local copies, waits for them, and re-layouts  1.57 us (2%)
    pallas_call x1, Pallas kernels, on_device(): pl.pallas_call(whole_kernel, out_shape=jax.ShapeDtypeStruct((4 * 4 * BR *...  76.9 us

profile of v5, /device:TPU:1, one launch (start us, length us, event | category | flops | bytes accessed | tf_op | source)
XLA Modules:
  0.0 78.5 jit_solution(12643261222381106622)
XLA Ops:
  0.0 76.9 %whole.1 = bf16[128,512]{1,0:T(8,128)(2,1)} custom-call(bf16[32,3072]{1,0:T(8,128)(2,1)} %bitcast.14, bf16[32,3072]{1,0:T(8,128)(2,1)} %bitcast.15, bf16[32,3072]{1,0:T(8,128)(2,1)} %bitcast.16, bf16[32,3072]{1,0:T(8,128)(2,1)} %bitcast.17, f32[1,3072]{1,0:T(1,128)} %shift_hbm.1, f32[1,3072]{1,0:T(1,128)} %scale_hbm.1, f32[1,3072]{1,0:T(1,128)} %gate_hbm.1, ...), custom_call_target="tpu_custom_call" | custom-call | tf_op jit(solution)/shard_map/whole/pallas_call | solution.py:653
  76.9 1.6 %copy.16 = bf16[4,4,1,8,512]{4,3,2,1,0:T(8,128)(2,1)} copy(bf16[4,4,1,8,512]{4,3,2,1,0:T(8,128)(2,1)} %bitcast.12) | data formatting | bytes 262144

commit v6 on v4

--- a/solution.py
+++ b/solution.py
@@ -73,6 +73,7 @@
     gb_hbm,
     out_ref,
     qb,
+    q_beside,
     kb,
     vb,
     ob,
@@ -80,6 +81,8 @@
     peak,
     total,
     acc,
+    give,
+    got,
     pat,
     tiles,
     near_tiles,
@@ -101,12 +104,15 @@
     ring_send,
     ring_recv,
     last_recv,
-    cross_send,
-    cross_recv,
+    q_send,
+    q_recv,
+    part_send,
+    part_recv,
     o_send,
     o_recv,
     halo_send,
     halo_recv,
+    ready,
 ):
     s, g, core, xl, z, y, xh = position()
     stays = core == xh
@@ -192,6 +198,8 @@
     pl.semaphore_wait(barrier, 2 * NZ + 5 - jnp.where(stays, 1, 0))
     for t in range(3):
         start_stage(t)
+    for ds in range(1, 4):
+        signal(ready, (s + ds) % 4, g)
 
     loads = [
         pltpu.make_async_copy(src, dst, load_sem.at[i])
@@ -249,15 +257,16 @@
             (right, left)[t],
         )
 
-    def across(piece, beside, step):
-        remote(piece, beside, cross_send, cross_recv.at[step], sibling, g).start()
-
-    def half_across(t, slot, half, step):
-        across(half_of(t, slot, half), half_of(t, 8 + slot, half), step)
-
-    def attend(h, slots, first):
+    both = slice(0, 2 * NBLK)
+    mine = slice(0, NBLK)
+    others = slice(NBLK, 2 * NBLK)
+
+    def attend(h, slots, rows, first):
         lanes = slice(h * HD, (h + 1) * HD)
-        q = qb[:, lanes]
+        if rows == both:
+            q = jnp.concatenate([qb[:, lanes], q_beside[:, lanes]], axis=0)
+        else:
+            q = (qb if rows == mine else q_beside)[:, lanes]
         scores = [
             lax.dot_general(
                 q, kb[slot, :, lanes], (((1,), (1,)), ((), ())), preferred_element_type=F32
@@ -266,11 +275,11 @@
         ]
         top = functools.reduce(jnp.maximum, scores)
         top = jnp.max(top, axis=1, keepdims=True)
-        top = jnp.broadcast_to(top, (NBLK, HD))
+        top = jnp.broadcast_to(top, (q.shape[0], HD))
         if not first:
-            old = peak[h]
+            old = peak[h, rows]
             top = jnp.maximum(old, top)
-        peak[h] = top
+        peak[h, rows] = top
         wide = jnp.concatenate([top, top], axis=1)
         part = None
         mixed = None
@@ -281,19 +290,18 @@
             term = jnp.dot(weights.astype(BF16), vb[slot, :, lanes], preferred_element_type=F32)
             mixed = term if mixed is None else mixed + term
         if first:
-            total[h] = part
-            acc[h] = mixed
+            total[h, rows] = part
+            acc[h, rows] = mixed
         else:
             fade = jnp.exp2((old - top) * EXP2_SCALE)
-            total[h] = total[h] * fade + part
-            acc[h] = acc[h] * fade + mixed
+            total[h, rows] = total[h, rows] * fade + part
+            acc[h, rows] = acc[h, rows] * fade + mixed
 
     pieces = [(t, half) for t in range(2) for half in range(HALVES)]
     for t, half in pieces:
         await_bytes(half_of(t, 0, half), s1_recv.at[t, half])
         hop(0, t, half, 1).start()
         hop(1, t, half, 1).start()
-        half_across(t, 0, half, 0)
     cw_ref[:, 48:, :] = jnp.zeros((9, 80, cw_ref.shape[2]), BF16)
     for n in range(1, 4):
         for t, half in pieces:
@@ -304,19 +312,31 @@
                 elif way == t and half == HALVES - 1:
                     for h in range(HG):
                         last_hop(t, h).start()
-                half_across(t, slot_of(way, n), half, n)
         if n == 1:
             await_bytes(qb, s1_recv.at[2, 0])
-            await_bytes(kb.at[pl.ds(8, 2)], cross_recv.at[0])
+            remote(qb, q_beside, q_send, q_recv, sibling, g).start()
+        if n == 2:
+            await_bytes(q_beside, q_recv)
             for h in range(HG):
-                attend(h, (0, 8), True)
-        await_bytes(kb.at[pl.ds(8, 4)], cross_recv.at[n])
-        for h in range(HG):
-            attend(h, (n, 4 + n, 8 + n, 12 + n), False)
+                attend(h, (0, 1, 5), both, True)
+        if n >= 2:
+            for h in range(HG):
+                attend(h, (n, 4 + n), both, False)
+
+    def part_copy(h):
+        return remote(give.at[h], got.at[h], part_send.at[h], part_recv.at[h], sibling, g)
+
+    first_lanes = lax.broadcasted_iota(jnp.int32, (NBLK, HD), 1) < HD // 2
     for h in range(HG):
         for t in range(2):
             last_hop(t, h).wait_recv()
-            across(head_of(t, 4, h), head_of(t, 12, h), 4 + h)
+        attend(h, (4,), others, False)
+        give[h, 0] = acc[h, others]
+        sums = jnp.sum(total[h, others], axis=1, keepdims=True)
+        give[h, 1] = jnp.where(first_lanes, peak[h, others], sums)
+        part_copy(h).start()
+    for h in range(HG):
+        attend(h, (4,), mine, False)
 
     def back_copy(h, place):
         zp = (z + NEAREST[place]) % NZ
@@ -330,9 +350,18 @@
         )
 
     for h in range(HG):
-        await_bytes(kb.at[pl.ds(8, 2), :, pl.ds(0, HD)], cross_recv.at[4 + h])
-        attend(h, (4, 12), False)
-        ob[h] = (acc[h] / jnp.sum(total[h], axis=1, keepdims=True)).astype(BF16)
+        part_copy(h).wait_recv()
+        packed = got[h, 1]
+        turned = pltpu.roll(packed, HD // 2, axis=1)
+        other_peak = jnp.where(first_lanes, packed, turned)
+        other_sums = jnp.where(first_lanes, turned, packed)
+        own_peak = peak[h, mine]
+        top = jnp.maximum(own_peak, other_peak)
+        own_fade = jnp.exp2((own_peak - top) * EXP2_SCALE)
+        other_fade = jnp.exp2((other_peak - top) * EXP2_SCALE)
+        sums = jnp.sum(total[h, mine], axis=1, keepdims=True)
+        mixed = acc[h, mine] * own_fade + got[h, 0] * other_fade
+        ob[h] = (mixed / (sums * own_fade + other_sums * other_fade)).astype(BF16)
         for place in range(NZ - 1, 0, -1):
             back_copy(h, place).start()
 
@@ -359,7 +388,9 @@
         sent_blocks(qb, s1_send.at[t])
     for way in range(2):
         await_bytes(kb.at[pl.ds(0, 7)], ring_send.at[way])
-    await_bytes(kb, cross_send)
+    await_bytes(qb, q_send)
+    for h in range(HG):
+        part_copy(h).wait_send()
     for load in loads:
         load.wait()
     await_bytes(att, o_recv)
@@ -387,32 +418,30 @@
     tiles[3, 0:6, :] = tile[10:16]
     tiles[3, 6:8, :] = tile[14:16]
 
-    for ds in range(1, 4):
-        sp = (s + ds) % 4
-        remote(
-            tiles.at[sp], near_tiles.at[4, s], halo_send.at[0], halo_recv.at[0], sp, g
-        ).start()
-    near_tiles[4, s] = tiles[s]
+    pl.semaphore_wait(ready, 3)
+    for dy, dx in AROUND:
+        place = (1 - dy) * 3 + 1 - dx
+        for ds in range(4):
+            if (dy, dx, ds) != (0, 0, 0):
+                sp = (s + ds) % 4
+                remote(
+                    tiles.at[sp],
+                    near_tiles.at[place * 4 + s],
+                    halo_send,
+                    halo_recv,
+                    sp,
+                    tile_seq(dy, dx),
+                ).start()
+    near_tiles[4 * 4 + s] = tiles[s]
     for h in range(HG):
         sent_blocks(ob.at[h], o_send.at[h])
-    await_bytes(tiles.at[pl.ds(0, 3)], halo_recv.at[0])
-    for dy, dx in neighbours:
-        remote(
-            near_tiles.at[4],
-            near_tiles.at[(1 - dy) * 3 + 1 - dx],
-            halo_send.at[1],
-            halo_recv.at[1],
-            s,
-            tile_seq(dy, dx),
-        ).start()
-    await_bytes(tiles.at[pl.ds(0, 3)], halo_send.at[0])
-    await_bytes(near_tiles.at[pl.ds(0, 8)], halo_recv.at[1])
+    await_bytes(near_tiles.at[pl.ds(0, 35)], halo_recv)
 
     def clear(at_edge, gone):
         @pl.when(at_edge)
         def _():
             for place in gone:
-                near_tiles[place] = jnp.zeros((4, 8, 128), F32)
+                near_tiles[place * 4 : place * 4 + 4] = jnp.zeros((4, 8, 128), F32)
 
     clear(z == 0, (0, 1, 2))
     clear(z == NZ - 1, (6, 7, 8))
@@ -423,7 +452,10 @@
         vert, dr = ((0, 1), (1, 0), (1, 1), (2, 0))[yy]
         lo = dr * BC * LATC
         hi = lo + BC * LATC
-        sides = [near_tiles[vert * 3 + dx].reshape(32, 128) for dx in range(3)]
+        sides = [
+            near_tiles[(vert * 3 + dx) * 4 : (vert * 3 + dx) * 4 + 4].reshape(32, 128)
+            for dx in range(3)
+        ]
         strip = jnp.concatenate(
             [
                 sides[0][:, hi - LATC : hi],
@@ -450,7 +482,7 @@
     conv = (conv + cb_ref[...]) * gg_ref[...] + gb_ref[...]
     out_ref[...] = (conv / (1.0 + jnp.exp(-conv))).astype(BF16)
 
-    await_bytes(near_tiles.at[pl.ds(0, 8)], halo_send.at[1])
+    await_bytes(near_tiles.at[pl.ds(0, 35)], halo_send)
 
 
 def on_device(
@@ -478,16 +510,19 @@
         out_specs=pl.BlockSpec(memory_space=pltpu.VMEM),
         scratch_shapes=[
             pltpu.VMEM((NBLK, GW), BF16),
-            pltpu.VMEM((16, NBLK, GW), BF16),
-            pltpu.VMEM((16, NBLK, GW), BF16),
+            pltpu.VMEM((NBLK, GW), BF16),
+            pltpu.VMEM((8, NBLK, GW), BF16),
+            pltpu.VMEM((8, NBLK, GW), BF16),
             pltpu.VMEM((HG, NBLK, HD), BF16),
             pltpu.VMEM((TOK, H * HD), BF16),
-            pltpu.VMEM((HG, NBLK, HD), F32),
-            pltpu.VMEM((HG, NBLK, HD), F32),
-            pltpu.VMEM((HG, NBLK, HD), F32),
+            pltpu.VMEM((HG, 2 * NBLK, HD), F32),
+            pltpu.VMEM((HG, 2 * NBLK, HD), F32),
+            pltpu.VMEM((HG, 2 * NBLK, HD), F32),
+            pltpu.VMEM((HG, 2, NBLK, HD), F32),
+            pltpu.VMEM((HG, 2, NBLK, HD), F32),
             pltpu.VMEM((TOK, 4 * LATC), F32),
             pltpu.VMEM((4, 8, 128), F32),
-            pltpu.VMEM((9, 4, 8, 128), F32),
+            pltpu.VMEM((36, 8, 128), F32),
             pltpu.VMEM((9, 4 * 4 * BR * BC, 128), F32),
             pltpu.VMEM((TOK, H * HD), BF16),
             pltpu.VMEM((1, H * HD), F32),
@@ -507,11 +542,14 @@
             dma((2, 2, HALVES, 4)),
             dma((2, HG)),
             dma(()),
-            dma((4 + HG,)),
+            dma(()),
+            dma((HG,)),
+            dma((HG,)),
             dma((HG,)),
             dma(()),
-            dma((2,)),
-            dma((2,)),
+            dma(()),
+            dma(()),
+            pltpu.SemaphoreType.REGULAR,
         ],
         compiler_params=pltpu.CompilerParams(
             collective_id=0, has_side_effects=True, vmem_limit_bytes=60 * 1024 * 1024

time: 77.1 us -> 75.3 us (0.977)
  Pallas kernels: 75.4 us -> 73.6 us
    pallas_call x1, Pallas kernels: 75.4 us -> 73.6 us  [on_device(): pl.pallas_call(whole_kernel, out_shape=jax.ShapeDtypeStruct((4 * 4 * BR *...]
where the time goes in v6:
time: 75.3 us; the launch traced here: 75.2 us
  Pallas kernels  73.6 us (98%)
  local copies, waits for them, and re-layouts  1.57 us (2%)
    pallas_call x1, Pallas kernels, on_device(): pl.pallas_call(whole_kernel, out_shape=jax.ShapeDtypeStruct((4 * 4 * BR *...  73.6 us
    unnamed x1, local copies, waits for them, and re-layouts  1.57 us

profile of v6, /device:TPU:1, one launch (start us, length us, event | category | flops | bytes accessed | tf_op | source)
XLA Modules:
  0.0 75.2 jit_solution(17363076641503937797)
XLA Ops:
  0.0 73.6 %whole.1 = bf16[128,512]{1,0:T(8,128)(2,1)} custom-call(bf16[32,3072]{1,0:T(8,128)(2,1)} %bitcast.14, bf16[32,3072]{1,0:T(8,128)(2,1)} %bitcast.15, bf16[32,3072]{1,0:T(8,128)(2,1)} %bitcast.16, bf16[32,3072]{1,0:T(8,128)(2,1)} %bitcast.17, f32[1,3072]{1,0:T(1,128)} %shift_hbm.1, f32[1,3072]{1,0:T(1,128)} %scale_hbm.1, f32[1,3072]{1,0:T(1,128)} %gate_hbm.1, ...), custom_call_target="tpu_custom_call" | custom-call | tf_op jit(solution)/shard_map/whole/pallas_call | solution.py:506
  73.6 1.6 %copy.16 = bf16[4,4,1,8,512]{4,3,2,1,0:T(8,128)(2,1)} copy(bf16[4,4,1,8,512]{4,3,2,1,0:T(8,128)(2,1)} %bitcast.12) | data formatting | bytes 262144

commit v7 on v6

--- a/solution.py
+++ b/solution.py
@@ -17,7 +17,6 @@
 NY = 8
 TOK = 32
 HG = 3
-GW = HG * HD
 NBLK = NZ * TOK
 
 scaling = 0.476986
@@ -52,9 +51,10 @@
 NEAREST = (0, 1, 7, 2, 6, 3, 5, 4)
 AROUND = [(dy, dx) for dy in (-1, 0, 1) for dx in (-1, 0, 1)]
 
-HALVES = 2
-PER_HALF = NZ // HALVES
-HALF = NBLK // HALVES
+RING_HEADS = ((0, 1), (2,))
+FIRST_HEAD = (0, 2 * NZ)
+PARTS = (2, 1)
+WIDTH = (2 * HD, HD)
 
 
 def whole_kernel(
@@ -72,10 +72,14 @@
     gg_hbm,
     gb_hbm,
     out_ref,
-    qb,
-    q_beside,
-    kb,
-    vb,
+    q_rows,
+    q_rows_beside,
+    k_rows,
+    v_rows,
+    q_cols,
+    q_cols_beside,
+    k_cols,
+    v_cols,
     ob,
     att,
     peak,
@@ -127,8 +131,14 @@
     def ring_seq(yp):
         return (z * NY + yp) * 2 + xh
 
-    right = ring_seq((y + 1) % NY)
-    left = ring_seq((y + NY - 1) % NY)
+    ways = (
+        (ring_seq((y + 1) % NY), ring_seq((y + NY - 1) % NY)),
+        (
+            ((z + 1) % NZ * NY + y) * 2 + xh,
+            ((z + NZ - 1) % NZ * NY + y) * 2 + xh,
+        ),
+    )
+    along = (z, y)
 
     neighbours = [(dy, dx) for dy, dx in AROUND if (dy, dx) != (0, 0)]
 
@@ -143,61 +153,74 @@
     def _():
         signal(barrier, swap_sec, swap_seq(z, y))
 
-    signal(barrier, s, right)
-    signal(barrier, s, left)
+    for e in NEAREST[1:]:
+        signal(barrier, swap_sec, swap_seq(z, (y + e) % NY))
+    for r in range(2):
+        for way in range(2):
+            signal(barrier, s, ways[r][way])
     for ds in range(1, 4):
         signal(barrier, (s + ds) % 4, g)
     for dy, dx in neighbours:
         signal(barrier, s, tile_seq(dy, dx))
 
-    def group_cols(zp):
-        return pl.ds(pl.multiple_of(zp * GW, HD), GW)
+    def group_cols(r, group):
+        first = FIRST_HEAD[r] * HD + group * WIDTH[r]
+        return pl.ds(pl.multiple_of(first, HD), WIDTH[r])
 
     def head_cols(h):
         return pl.ds(pl.multiple_of(h * HD, HD), HD)
 
+    def swap_along(r, group):
+        return swap_seq(group, y) if r == 0 else swap_seq(z, group)
+
     def block_rows(place):
         return pl.ds(place * TOK, TOK)
 
     def await_bytes(ref, sem):
         pltpu.make_async_copy(ref, ref, sem).wait()
 
-    stage_one = ((k_ref, kb.at[0]), (v_ref, vb.at[0]), (q_ref, qb))
-
-    def stage_sem(t, place):
-        return s1_recv.at[t, 0 if t == 2 else place // PER_HALF]
-
-    def stage_copy(t, place):
-        src, buf = stage_one[t]
-        zp = (z + NZ - NEAREST[place]) % NZ
+    sources = (k_ref, v_ref, q_ref)
+    queries = (q_rows, q_cols)
+    beside = (q_rows_beside, q_cols_beside)
+    bufs = ((k_rows, v_rows), (k_cols, v_cols))
+
+    def landing(r, t):
+        return queries[r] if t == 2 else bufs[r][t].at[0]
+
+    def stage_sem(r, t, place):
+        return s1_recv.at[r, t, 0 if t == 2 else place * PARTS[r] // NZ]
+
+    def stage_copy(r, t, place):
+        group = (along[r] + NZ - NEAREST[place]) % NZ
         return remote(
-            src.at[:, group_cols(zp)],
-            buf.at[block_rows(place), :],
-            s1_send.at[t],
-            stage_sem(t, place),
+            sources[t].at[:, group_cols(r, group)],
+            landing(r, t).at[block_rows(place), :],
+            s1_send.at[r, t],
+            stage_sem(r, t, place),
             swap_sec,
-            swap_seq(zp, y),
+            swap_along(r, group),
         )
 
-    def start_stage(t):
-        src, buf = stage_one[t]
-
+    def start_stage(r, t):
         @pl.when(stays)
         def _():
             pltpu.make_async_copy(
-                src.at[:, group_cols(z)], buf.at[block_rows(0), :], stage_sem(t, 0)
+                sources[t].at[:, group_cols(r, along[r])],
+                landing(r, t).at[block_rows(0), :],
+                stage_sem(r, t, 0),
             ).start()
 
         @pl.when(moves)
         def _():
-            stage_copy(t, 0).start()
+            stage_copy(r, t, 0).start()
 
         for place in range(1, NZ):
-            stage_copy(t, place).start()
-
-    pl.semaphore_wait(barrier, 2 * NZ + 5 - jnp.where(stays, 1, 0))
+            stage_copy(r, t, place).start()
+
+    pl.semaphore_wait(barrier, 3 * NZ + 6 - jnp.where(stays, 1, 0))
     for t in range(3):
-        start_stage(t)
+        for r in range(2):
+            start_stage(r, t)
     for ds in range(1, 4):
         signal(ready, (s + ds) % 4, g)
 
@@ -224,37 +247,39 @@
             cw_hbm.at[pl.ds(tap * 48, 48), :], cw_ref.at[tap, pl.ds(0, 48), :], cw_sem
         ).start()
 
-    bufs = (kb, vb)
-
     def slot_of(way, hops):
         if hops in (0, 4):
             return hops
         return hops if way == 0 else 4 + hops
 
-    def half_of(t, slot, half):
-        return bufs[t].at[slot, pl.ds(half * HALF, HALF), :]
-
-    def head_of(t, slot, h):
-        return bufs[t].at[slot, :, pl.ds(h * HD, HD)]
-
-    def hop(way, t, half, hops):
+    def part_of(r, t, slot, part):
+        rows = NBLK // PARTS[r]
+        return bufs[r][t].at[slot, pl.ds(part * rows, rows), :]
+
+    def head_of(h, t, slot):
+        if h == 2:
+            return k_cols.at[slot] if t == 0 else v_cols.at[slot]
+        return bufs[0][t].at[slot, :, pl.ds(h * HD, HD)]
+
+    def hop(r, way, t, part, hops):
         return remote(
-            half_of(t, slot_of(way, hops - 1), half),
-            half_of(t, slot_of(way, hops), half),
-            ring_send.at[way],
-            ring_recv.at[way, t, half, hops],
+            part_of(r, t, slot_of(way, hops - 1), part),
+            part_of(r, t, slot_of(way, hops), part),
+            ring_send.at[r, way],
+            ring_recv.at[r, way, t, part, hops],
             s,
-            (right, left)[way],
+            ways[r][way],
         )
 
     def last_hop(t, h):
+        r = 0 if h < 2 else 1
         return remote(
-            head_of(t, slot_of(t, 3), h),
-            head_of(t, 4, h),
-            ring_send.at[t],
+            head_of(h, t, slot_of(t, 3)),
+            head_of(h, t, 4),
+            ring_send.at[r, t],
             last_recv.at[t, h],
             s,
-            (right, left)[t],
+            ways[r][t],
         )
 
     both = slice(0, 2 * NBLK)
@@ -262,14 +287,14 @@
     others = slice(NBLK, 2 * NBLK)
 
     def attend(h, slots, rows, first):
-        lanes = slice(h * HD, (h + 1) * HD)
+        r, lanes = (1, slice(0, HD)) if h == 2 else (0, slice(h * HD, (h + 1) * HD))
         if rows == both:
-            q = jnp.concatenate([qb[:, lanes], q_beside[:, lanes]], axis=0)
+            q = jnp.concatenate([queries[r][:, lanes], beside[r][:, lanes]], axis=0)
         else:
-            q = (qb if rows == mine else q_beside)[:, lanes]
+            q = (queries if rows == mine else beside)[r][:, lanes]
         scores = [
             lax.dot_general(
-                q, kb[slot, :, lanes], (((1,), (1,)), ((), ())), preferred_element_type=F32
+                q, head_of(h, 0, slot)[...], (((1,), (1,)), ((), ())), preferred_element_type=F32
             )
             for slot in slots
         ]
@@ -287,7 +312,9 @@
             weights = jnp.exp2((score - wide) * EXP2_SCALE)
             halves = weights[:, :HD] + weights[:, HD:]
             part = halves if part is None else part + halves
-            term = jnp.dot(weights.astype(BF16), vb[slot, :, lanes], preferred_element_type=F32)
+            term = jnp.dot(
+                weights.astype(BF16), head_of(h, 1, slot)[...], preferred_element_type=F32
+            )
             mixed = term if mixed is None else mixed + term
         if first:
             total[h, rows] = part
@@ -297,26 +324,28 @@
             total[h, rows] = total[h, rows] * fade + part
             acc[h, rows] = acc[h, rows] * fade + mixed
 
-    pieces = [(t, half) for t in range(2) for half in range(HALVES)]
-    for t, half in pieces:
-        await_bytes(half_of(t, 0, half), s1_recv.at[t, half])
-        hop(0, t, half, 1).start()
-        hop(1, t, half, 1).start()
+    pieces = [(0, 0, 0), (1, 0, 0), (0, 0, 1), (0, 1, 0), (1, 1, 0), (0, 1, 1)]
+    for r, t, part in pieces:
+        await_bytes(part_of(r, t, 0, part), s1_recv.at[r, t, part])
+        for way in range(2):
+            hop(r, way, t, part, 1).start()
     cw_ref[:, 48:, :] = jnp.zeros((9, 80, cw_ref.shape[2]), BF16)
     for n in range(1, 4):
-        for t, half in pieces:
+        for r, t, part in pieces:
             for way in range(2):
-                hop(way, t, half, n).wait_recv()
+                hop(r, way, t, part, n).wait_recv()
                 if n < 3:
-                    hop(way, t, half, n + 1).start()
-                elif way == t and half == HALVES - 1:
-                    for h in range(HG):
+                    hop(r, way, t, part, n + 1).start()
+                elif way == t and part == PARTS[r] - 1:
+                    for h in RING_HEADS[r]:
                         last_hop(t, h).start()
         if n == 1:
-            await_bytes(qb, s1_recv.at[2, 0])
-            remote(qb, q_beside, q_send, q_recv, sibling, g).start()
+            for r in range(2):
+                await_bytes(queries[r], s1_recv.at[r, 2, 0])
+                remote(queries[r], beside[r], q_send.at[r], q_recv.at[r], sibling, g).start()
         if n == 2:
-            await_bytes(q_beside, q_recv)
+            for r in range(2):
+                await_bytes(beside[r], q_recv.at[r])
             for h in range(HG):
                 attend(h, (0, 1, 5), both, True)
         if n >= 2:
@@ -338,15 +367,18 @@
     for h in range(HG):
         attend(h, (4,), mine, False)
 
+    def home_cols(h):
+        return head_cols(z * 2 + h if h < 2 else FIRST_HEAD[1] + y)
+
     def back_copy(h, place):
-        zp = (z + NEAREST[place]) % NZ
+        r = 0 if h < 2 else 1
         return remote(
             ob.at[h, block_rows(place), :],
-            att.at[:, head_cols(z * HG + h)],
+            att.at[:, home_cols(h)],
             o_send.at[h],
             o_recv,
             swap_sec,
-            swap_seq(zp, y),
+            swap_along(r, (along[r] + NEAREST[place]) % NZ),
         )
 
     for h in range(HG):
@@ -372,7 +404,7 @@
         @pl.when(stays)
         def _(h=h):
             pltpu.make_async_copy(
-                ob.at[h, block_rows(0), :], att.at[:, head_cols(z * HG + h)], o_recv
+                ob.at[h, block_rows(0), :], att.at[:, home_cols(h)], o_recv
             ).start()
 
     def sent_blocks(ref, sem):
@@ -384,11 +416,12 @@
         def _():
             await_bytes(ref.at[pl.ds(0, NBLK - TOK), :], sem)
 
-    for t in range(3):
-        sent_blocks(qb, s1_send.at[t])
-    for way in range(2):
-        await_bytes(kb.at[pl.ds(0, 7)], ring_send.at[way])
-    await_bytes(qb, q_send)
+    for r in range(2):
+        for t in range(3):
+            sent_blocks(queries[r], s1_send.at[r, t])
+        for way in range(2):
+            await_bytes(bufs[r][0].at[pl.ds(0, 7)], ring_send.at[r, way])
+        await_bytes(queries[r], q_send.at[r])
     for h in range(HG):
         part_copy(h).wait_send()
     for load in loads:
@@ -509,10 +542,14 @@
         in_specs=[any_spec] * 13,
         out_specs=pl.BlockSpec(memory_space=pltpu.VMEM),
         scratch_shapes=[
-            pltpu.VMEM((NBLK, GW), BF16),
-            pltpu.VMEM((NBLK, GW), BF16),
-            pltpu.VMEM((8, NBLK, GW), BF16),
-            pltpu.VMEM((8, NBLK, GW), BF16),
+            pltpu.VMEM((NBLK, 2 * HD), BF16),
+            pltpu.VMEM((NBLK, 2 * HD), BF16),
+            pltpu.VMEM((8, NBLK, 2 * HD), BF16),
+            pltpu.VMEM((8, NBLK, 2 * HD), BF16),
+            pltpu.VMEM((NBLK, HD), BF16),
+            pltpu.VMEM((NBLK, HD), BF16),
+            pltpu.VMEM((8, NBLK, HD), BF16),
+            pltpu.VMEM((8, NBLK, HD), BF16),
             pltpu.VMEM((HG, NBLK, HD), BF16),
             pltpu.VMEM((TOK, H * HD), BF16),
             pltpu.VMEM((HG, 2 * NBLK, HD), F32),
@@ -536,13 +573,13 @@
             pltpu.VMEM((1, vae_width), F32),
             dma((9,)),
             dma(()),
-            dma((3,)),
-            dma((3, HALVES)),
+            dma((2, 3)),
+            dma((2, 3, 2)),
+            dma((2, 2)),
+            dma((2, 2, 2, 2, 4)),
+            dma((2, HG)),
             dma((2,)),
-            dma((2, 2, HALVES, 4)),
-            dma((2, HG)),
-            dma(()),
-            dma(()),
+            dma((2,)),
             dma((HG,)),
             dma((HG,)),
             dma((HG,)),

time: 75.3 us -> 65.2 us (0.87)
  Pallas kernels: 73.6 us -> 63.5 us
    pallas_call x1, Pallas kernels: 73.6 us -> 63.5 us  [on_device(): pl.pallas_call(whole_kernel, out_shape=jax.ShapeDtypeStruct((4 * 4 * BR *...]
where the time goes in v7:
time: 65.2 us; the launch traced here: 65.1 us
  Pallas kernels  63.5 us (97%)
  local copies, waits for them, and re-layouts  1.57 us (2%)
    pallas_call x1, Pallas kernels, on_device(): pl.pallas_call(whole_kernel, out_shape=jax.ShapeDtypeStruct((4 * 4 * BR *...  63.5 us
    unnamed x1, local copies, waits for them, and re-layouts  1.57 us

profile of v7, /device:TPU:1, one launch (start us, length us, event | category | flops | bytes accessed | tf_op | source)
XLA Modules:
  0.0 65.1 jit_solution(13872629023854997247)
XLA Ops:
  0.0 63.5 %whole.1 = bf16[128,512]{1,0:T(8,128)(2,1)} custom-call(bf16[32,3072]{1,0:T(8,128)(2,1)} %bitcast.14, bf16[32,3072]{1,0:T(8,128)(2,1)} %bitcast.15, bf16[32,3072]{1,0:T(8,128)(2,1)} %bitcast.16, bf16[32,3072]{1,0:T(8,128)(2,1)} %bitcast.17, f32[1,3072]{1,0:T(1,128)} %shift_hbm.1, f32[1,3072]{1,0:T(1,128)} %scale_hbm.1, f32[1,3072]{1,0:T(1,128)} %gate_hbm.1, ...), custom_call_target="tpu_custom_call" | custom-call | tf_op jit(solution)/shard_map/whole/pallas_call | solution.py:539
  63.5 1.6 %copy.16 = bf16[4,4,1,8,512]{4,3,2,1,0:T(8,128)(2,1)} copy(bf16[4,4,1,8,512]{4,3,2,1,0:T(8,128)(2,1)} %bitcast.12) | data formatting | bytes 262144

commit v8 on v7

--- a/solution.py
+++ b/solution.py
@@ -67,10 +67,6 @@
     gate_hbm,
     fw_hbm,
     fb_hbm,
-    cw_hbm,
-    cb_hbm,
-    gg_hbm,
-    gb_hbm,
     out_ref,
     q_rows,
     q_rows_beside,
@@ -97,12 +93,7 @@
     gate_ref,
     fw_ref,
     fb_ref,
-    cw_ref,
-    cb_ref,
-    gg_ref,
-    gb_ref,
     load_sem,
-    cw_sem,
     s1_send,
     s1_recv,
     ring_send,
@@ -234,19 +225,11 @@
                 (gate_hbm, gate_ref),
                 (fw_hbm, fw_ref),
                 (fb_hbm, fb_ref),
-                (cb_hbm, cb_ref),
-                (gg_hbm, gg_ref),
-                (gb_hbm, gb_ref),
             )
         )
     ]
     for load in loads:
         load.start()
-    for tap in range(9):
-        pltpu.make_async_copy(
-            cw_hbm.at[pl.ds(tap * 48, 48), :], cw_ref.at[tap, pl.ds(0, 48), :], cw_sem
-        ).start()
-
     def slot_of(way, hops):
         if hops in (0, 4):
             return hops
@@ -329,7 +312,6 @@
         await_bytes(part_of(r, t, 0, part), s1_recv.at[r, t, part])
         for way in range(2):
             hop(r, way, t, part, 1).start()
-    cw_ref[:, 48:, :] = jnp.zeros((9, 80, cw_ref.shape[2]), BF16)
     for n in range(1, 4):
         for r, t, part in pieces:
             for way in range(2):
@@ -507,13 +489,8 @@
                     row = yy - dy
                     if 0 <= row < BR:
                         windows[dt * 3 + dy, pl.ds(row * BC + x, 16, stride=8), :] = piece
-    await_bytes(cw_ref.at[:, pl.ds(0, 48), :], cw_sem)
-    left_side = jnp.concatenate([windows[tap].astype(BF16) for tap in range(9)], axis=1)
-    conv = jnp.dot(
-        left_side, cw_ref[...].reshape(9 * 128, cw_ref.shape[2]), preferred_element_type=F32
-    )
-    conv = (conv + cb_ref[...]) * gg_ref[...] + gb_ref[...]
-    out_ref[...] = (conv / (1.0 + jnp.exp(-conv))).astype(BF16)
+    taps = [windows[tap][:, : 3 * LATC] for tap in range(9)]
+    out_ref[...] = jnp.concatenate(taps, axis=1).astype(BF16)
 
     await_bytes(near_tiles.at[pl.ds(0, 35)], halo_send)
 
@@ -536,10 +513,11 @@
     any_spec = pl.BlockSpec(memory_space=pl.ANY)
     dma = pltpu.SemaphoreType.DMA
     vae_width = conv_weight.shape[1]
-    features = pl.pallas_call(
+    kin = conv_weight.shape[0]
+    columns = pl.pallas_call(
         whole_kernel,
-        out_shape=jax.ShapeDtypeStruct((4 * 4 * BR * BC, vae_width), BF16),
-        in_specs=[any_spec] * 13,
+        out_shape=jax.ShapeDtypeStruct((4 * 4 * BR * BC, kin), BF16),
+        in_specs=[any_spec] * 9,
         out_specs=pl.BlockSpec(memory_space=pltpu.VMEM),
         scratch_shapes=[
             pltpu.VMEM((NBLK, 2 * HD), BF16),
@@ -567,12 +545,7 @@
             pltpu.VMEM((1, H * HD), F32),
             pltpu.VMEM((4 * LATC, H * HD), BF16),
             pltpu.VMEM((1, 4 * LATC), F32),
-            pltpu.VMEM((9, 128, vae_width), BF16),
-            pltpu.VMEM((1, vae_width), F32),
-            pltpu.VMEM((1, vae_width), F32),
-            pltpu.VMEM((1, vae_width), F32),
-            dma((9,)),
-            dma(()),
+            dma((6,)),
             dma((2, 3)),
             dma((2, 3, 2)),
             dma((2, 2)),
@@ -602,11 +575,9 @@
         gate_mod,
         final_weight.T,
         final_bias[None],
-        conv_weight,
-        conv_bias[None],
-        group_gain[None],
-        group_bias[None],
     )
+    conv_out = jnp.dot(columns, conv_weight, preferred_element_type=F32) + conv_bias
+    features = jax.nn.silu(conv_out * group_gain + group_bias).astype(BF16)
     return features.reshape(4, 4, 1, BR * BC, vae_width)
 
 

time: 65.2 us -> 65.3 us (level)
  matrix products: 0 us -> 1.85 us
  local copies, waits for them, and re-layouts: 1.57 us -> 0.02 us
    dot_general x0 -> x1, matrix products: none -> 1.85 us  [on_device(): jnp.dot(columns, conv_weight, preferred_element_type=F32) + conv_bias]
    unnamed x1 -> x8, local copies, waits for them, and re-layouts: 1.57 us -> 0.02 us
where the time goes in v8:
time: 65.3 us; the launch traced here: 65.2 us
  Pallas kernels  63.3 us (97%)
  matrix products  1.85 us (3%)
    pallas_call x1, Pallas kernels, on_device(): pl.pallas_call(whole_kernel, out_shape=jax.ShapeDtypeStruct((4 * 4 * BR *...  63.3 us
    dot_general x1, matrix products, on_device(): jnp.dot(columns, conv_weight, preferred_element_type=F32) + conv_bias  1.85 us

profile of v8, /device:TPU:1, one launch (start us, length us, event | category | flops | bytes accessed | tf_op | source)
XLA Modules:
  0.0 65.2 jit_solution(12756976328847318270)
XLA Ops:
  0.0 0.0 copy-start
  0.0 0.0 copy-start.1
  0.0 0.0 copy-start.2
  0.0 0.0 copy-start.3
  0.0 63.3 %whole.1 = bf16[128,432]{1,0:T(8,128)(2,1)} custom-call(bf16[32,3072]{1,0:T(8,128)(2,1)} %bitcast.12, bf16[32,3072]{1,0:T(8,128)(2,1)} %bitcast.13, bf16[32,3072]{1,0:T(8,128)(2,1)} %bitcast.14, bf16[32,3072]{1,0:T(8,128)(2,1)} %bitcast.15, f32[1,3072]{1,0:T(1,128)} %shift_hbm.1, f32[1,3072]{1,0:T(1,128)} %scale_hbm.1, f32[1,3072]{1,0:T(1,128)} %gate_hbm.1, ...), custom_call_target="tpu_custom_call" | custom-call | tf_op jit(solution)/shard_map/whole/pallas_call | solution.py:517
  63.3 0.0 copy-done
  63.3 0.0 copy-done.1
  63.3 0.0 copy-done.2
  63.3 0.0 copy-done.3
  63.3 1.8 %multiply_convert_fusion = bf16[128,512]{1,0:T(8,128)(2,1)} fusion(bf16[128,432]{1,0:T(8,128)(2,1)} %whole.1, bf16[432,512]{1,0:T(8,128)(2,1)S(1)} %copy-done, f32[512]{0:T(512)S(1)} %copy-done.1, f32[512]{0:T(512)S(1)} %copy-done.2, f32[512]{0:T(512)S(1)} %copy-done.3), kind=kOutput, calls=%fused_computation.3 | convolution fusion | flops 57147392 | bytes 690176 | tf_op jit(solution)/shard_map/dot_general | solution.py:579
Async XLA Ops:
  0.0 63.3 %copy-start = (bf16[432,512]{1,0:T(8,128)(2,1)S(1)}, bf16[432,512]{1,0:T(8,128)(2,1)}, u32[]{:S(2)}) copy-start(bf16[432,512]{1,0:T(8,128)(2,1)} %param.22) | copy-start | bytes 1327108
  0.0 63.3 %copy-start.1 = (f32[512]{0:T(512)S(1)}, f32[512]{0:T(512)}, u32[]{:S(2)}) copy-start(f32[512]{0:T(512)} %param.25) | copy-start | bytes 6148
  0.0 63.3 %copy-start.2 = (f32[512]{0:T(512)S(1)}, f32[512]{0:T(512)}, u32[]{:S(2)}) copy-start(f32[512]{0:T(512)} %param.24) | copy-start | bytes 6148
  0.0 63.3 %copy-start.3 = (f32[512]{0:T(512)S(1)}, f32[512]{0:T(512)}, u32[]{:S(2)}) copy-start(f32[512]{0:T(512)} %param.23) | copy-start | bytes 6148

commit v9 on v7

--- a/solution.py
+++ b/solution.py
@@ -218,7 +218,7 @@
             stage_copy(r, t, place).start()
 
     pl.semaphore_wait(barrier, 3 * NZ + 6 - jnp.where(stays, 1, 0))
-    for t in range(3):
+    for t in range(2):
         for r in range(2):
             start_stage(r, t)
     for ds in range(1, 4):
@@ -324,11 +324,14 @@
             total[h, rows] = total[h, rows] * fade + part
             acc[h, rows] = acc[h, rows] * fade + mixed
 
-    pieces = [(0, 0, 0), (1, 0, 0), (0, 0, 1), (0, 1, 0), (1, 1, 0), (0, 1, 1)]
-    for r, t, part in pieces:
+    for r, t, part in [(0, 0, 0), (1, 0, 0), (0, 0, 1), (1, 1, 0), (0, 1, 0), (0, 1, 1)]:
         await_bytes(part_of(r, t, 0, part), s1_recv.at[r, t, part])
         for way in range(2):
             hop(r, way, t, part, 1).start()
+        if (r, t) == (1, 1):
+            for q_ring in range(2):
+                start_stage(q_ring, 2)
+    pieces = [(0, 0, 0), (0, 0, 1), (0, 1, 0), (0, 1, 1), (1, 0, 0), (1, 1, 0)]
     cw_ref[:, 48:, :] = jnp.zeros((9, 80, cw_ref.shape[2]), BF16)
     for n in range(1, 4):
         for r, t, part in pieces:

time: 65.2 us -> 66.4 us (1.018)
  Pallas kernels: 63.5 us -> 64.7 us
    pallas_call x1, Pallas kernels: 63.5 us -> 64.7 us  [on_device(): pl.pallas_call(whole_kernel, out_shape=jax.ShapeDtypeStruct((4 * 4 * BR *...]
where the time goes in v9:
time: 66.4 us; the launch traced here: 66.3 us
  Pallas kernels  64.7 us (97%)
  local copies, waits for them, and re-layouts  1.57 us (2%)
    pallas_call x1, Pallas kernels, on_device(): pl.pallas_call(whole_kernel, out_shape=jax.ShapeDtypeStruct((4 * 4 * BR *...  64.7 us
    unnamed x1, local copies, waits for them, and re-layouts  1.57 us

profile of v9, /device:TPU:1, one launch (start us, length us, event | category | flops | bytes accessed | tf_op | source)
XLA Modules:
  0.0 66.3 jit_solution(7890832994051511290)
XLA Ops:
  0.0 64.7 %whole.1 = bf16[128,512]{1,0:T(8,128)(2,1)} custom-call(bf16[32,3072]{1,0:T(8,128)(2,1)} %bitcast.14, bf16[32,3072]{1,0:T(8,128)(2,1)} %bitcast.15, bf16[32,3072]{1,0:T(8,128)(2,1)} %bitcast.16, bf16[32,3072]{1,0:T(8,128)(2,1)} %bitcast.17, f32[1,3072]{1,0:T(1,128)} %shift_hbm.1, f32[1,3072]{1,0:T(1,128)} %scale_hbm.1, f32[1,3072]{1,0:T(1,128)} %gate_hbm.1, ...), custom_call_target="tpu_custom_call" | custom-call | tf_op jit(solution)/shard_map/whole/pallas_call | solution.py:542
  64.7 1.6 %copy.16 = bf16[4,4,1,8,512]{4,3,2,1,0:T(8,128)(2,1)} copy(bf16[4,4,1,8,512]{4,3,2,1,0:T(8,128)(2,1)} %bitcast.12) | data formatting | bytes 262144

commit v10 on v7

--- a/solution.py
+++ b/solution.py
@@ -87,6 +87,8 @@
     acc,
     give,
     got,
+    give_stats,
+    got_stats,
     pat,
     tiles,
     near_tiles,
@@ -339,33 +341,39 @@
                 elif way == t and part == PARTS[r] - 1:
                     for h in RING_HEADS[r]:
                         last_hop(t, h).start()
-        if n == 1:
+        if n == 2:
             for r in range(2):
                 await_bytes(queries[r], s1_recv.at[r, 2, 0])
                 remote(queries[r], beside[r], q_send.at[r], q_recv.at[r], sibling, g).start()
-        if n == 2:
-            for r in range(2):
-                await_bytes(beside[r], q_recv.at[r])
-            for h in range(HG):
-                attend(h, (0, 1, 5), both, True)
-        if n >= 2:
-            for h in range(HG):
-                attend(h, (n, 4 + n), both, False)
-
-    def part_copy(h):
-        return remote(give.at[h], got.at[h], part_send.at[h], part_recv.at[h], sibling, g)
-
-    first_lanes = lax.broadcasted_iota(jnp.int32, (NBLK, HD), 1) < HD // 2
+    for r in range(2):
+        await_bytes(beside[r], q_recv.at[r])
+    for h in range(HG):
+        attend(h, (0, 1, 5), both, True)
+    for n in (2, 3):
+        for h in range(HG):
+            attend(h, (n, 4 + n), both, False)
+
+    lane = lax.broadcasted_iota(jnp.int32, (NBLK, HD), 1)
+    stats = jnp.zeros((NBLK, HD), F32)
     for h in range(HG):
         for t in range(2):
             last_hop(t, h).wait_recv()
         attend(h, (4,), others, False)
-        give[h, 0] = acc[h, others]
+        give[h] = acc[h, others].astype(BF16)
         sums = jnp.sum(total[h, others], axis=1, keepdims=True)
-        give[h, 1] = jnp.where(first_lanes, peak[h, others], sums)
-        part_copy(h).start()
+        stats = jnp.where(lane == 2 * h, peak[h, others], stats)
+        stats = jnp.where(lane == 2 * h + 1, sums, stats)
+    give_stats[...] = stats
+    hand_over = (
+        remote(give_stats, got_stats, part_send.at[0], part_recv.at[0], sibling, g),
+        remote(give, got, part_send.at[1], part_recv.at[1], sibling, g),
+    )
+    for copy in hand_over:
+        copy.start()
     for h in range(HG):
         attend(h, (4,), mine, False)
+    for copy in hand_over:
+        copy.wait_recv()
 
     def home_cols(h):
         return head_cols(z * 2 + h if h < 2 else FIRST_HEAD[1] + y)
@@ -382,17 +390,14 @@
         )
 
     for h in range(HG):
-        part_copy(h).wait_recv()
-        packed = got[h, 1]
-        turned = pltpu.roll(packed, HD // 2, axis=1)
-        other_peak = jnp.where(first_lanes, packed, turned)
-        other_sums = jnp.where(first_lanes, turned, packed)
+        other_peak = jnp.broadcast_to(got_stats[:, 2 * h : 2 * h + 1], (NBLK, HD))
+        other_sums = jnp.broadcast_to(got_stats[:, 2 * h + 1 : 2 * h + 2], (NBLK, HD))
         own_peak = peak[h, mine]
         top = jnp.maximum(own_peak, other_peak)
         own_fade = jnp.exp2((own_peak - top) * EXP2_SCALE)
         other_fade = jnp.exp2((other_peak - top) * EXP2_SCALE)
         sums = jnp.sum(total[h, mine], axis=1, keepdims=True)
-        mixed = acc[h, mine] * own_fade + got[h, 0] * other_fade
+        mixed = acc[h, mine] * own_fade + got[h].astype(F32) * other_fade
         ob[h] = (mixed / (sums * own_fade + other_sums * other_fade)).astype(BF16)
         for place in range(NZ - 1, 0, -1):
             back_copy(h, place).start()
@@ -422,8 +427,8 @@
         for way in range(2):
             await_bytes(bufs[r][0].at[pl.ds(0, 7)], ring_send.at[r, way])
         await_bytes(queries[r], q_send.at[r])
-    for h in range(HG):
-        part_copy(h).wait_send()
+    for copy in hand_over:
+        copy.wait_send()
     for load in loads:
         load.wait()
     await_bytes(att, o_recv)
@@ -555,8 +560,10 @@
             pltpu.VMEM((HG, 2 * NBLK, HD), F32),
             pltpu.VMEM((HG, 2 * NBLK, HD), F32),
             pltpu.VMEM((HG, 2 * NBLK, HD), F32),
-            pltpu.VMEM((HG, 2, NBLK, HD), F32),
-            pltpu.VMEM((HG, 2, NBLK, HD), F32),
+            pltpu.VMEM((HG, NBLK, HD), BF16),
+            pltpu.VMEM((HG, NBLK, HD), BF16),
+            pltpu.VMEM((NBLK, HD), F32),
+            pltpu.VMEM((NBLK, HD), F32),
             pltpu.VMEM((TOK, 4 * LATC), F32),
             pltpu.VMEM((4, 8, 128), F32),
             pltpu.VMEM((36, 8, 128), F32),

time: 65.2 us -> 67.2 us (1.031)
  Pallas kernels: 63.5 us -> 65.5 us
    pallas_call x1, Pallas kernels: 63.5 us -> 65.5 us  [on_device(): pl.pallas_call(whole_kernel, out_shape=jax.ShapeDtypeStruct((4 * 4 * BR *...]
where the time goes in v10:
time: 67.2 us; the launch traced here: 67.1 us
  Pallas kernels  65.5 us (97%)
  local copies, waits for them, and re-layouts  1.57 us (2%)
    pallas_call x1, Pallas kernels, on_device(): pl.pallas_call(whole_kernel, out_shape=jax.ShapeDtypeStruct((4 * 4 * BR *...  65.5 us
    unnamed x1, local copies, waits for them, and re-layouts  1.57 us

profile of v10, /device:TPU:1, one launch (start us, length us, event | category | flops | bytes accessed | tf_op | source)
XLA Modules:
  0.0 67.1 jit_solution(11454107641253906335)
XLA Ops:
  0.0 65.5 %whole.1 = bf16[128,512]{1,0:T(8,128)(2,1)} custom-call(bf16[32,3072]{1,0:T(8,128)(2,1)} %bitcast.14, bf16[32,3072]{1,0:T(8,128)(2,1)} %bitcast.15, bf16[32,3072]{1,0:T(8,128)(2,1)} %bitcast.16, bf16[32,3072]{1,0:T(8,128)(2,1)} %bitcast.17, f32[1,3072]{1,0:T(1,128)} %shift_hbm.1, f32[1,3072]{1,0:T(1,128)} %scale_hbm.1, f32[1,3072]{1,0:T(1,128)} %gate_hbm.1, ...), custom_call_target="tpu_custom_call" | custom-call | tf_op jit(solution)/shard_map/whole/pallas_call | solution.py:544
  65.5 1.6 %copy.16 = bf16[4,4,1,8,512]{4,3,2,1,0:T(8,128)(2,1)} copy(bf16[4,4,1,8,512]{4,3,2,1,0:T(8,128)(2,1)} %bitcast.12) | data formatting | bytes 262144

commit v11 on v7

--- a/solution.py
+++ b/solution.py
@@ -589,7 +589,7 @@
             pltpu.SemaphoreType.REGULAR,
         ],
         compiler_params=pltpu.CompilerParams(
-            collective_id=0, has_side_effects=True, vmem_limit_bytes=60 * 1024 * 1024
+            collective_id=0, has_side_effects=True, vmem_limit_bytes=54976 * 1024
         ),
         name="whole",
     )(

time: 65.2 us -> 66.7 us (1.023)
  local copies, waits for them, and re-layouts: 1.57 us -> 3.46 us
    unnamed x1 -> x15, local copies, waits for them, and re-layouts: 1.57 us -> 3.46 us
where the time goes in v11:
time: 66.7 us; the launch traced here: 66.3 us
  Pallas kernels  62.9 us (94%)
  local copies, waits for them, and re-layouts  3.46 us (5%)
    pallas_call x1, Pallas kernels, on_device(): pl.pallas_call(whole_kernel, out_shape=jax.ShapeDtypeStruct((4 * 4 * BR *...  62.9 us
    unnamed x15, local copies, waits for them, and re-layouts  3.46 us

profile of v11, /device:TPU:1, one launch (start us, length us, event | category | flops | bytes accessed | tf_op | source)
XLA Modules:
  0.0 66.3 jit_solution(1274986652480940674)
XLA Ops:
  0.0 0.0 copy-start
  0.0 0.0 copy-start.4
  0.0 0.0 copy-start.3
  0.0 0.0 copy-start.6
  0.0 0.7 %copy-done = f32[1,3072]{1,0:T(1,128)S(1)} copy-done((f32[1,3072]{1,0:T(1,128)S(1)}, f32[1,3072]{1,0:T(1,128)}, u32[]{:S(2)}) %copy-start) | copy-done | bytes 12312
  0.7 0.0 copy-done.4
  0.7 0.0 copy-done.3
  0.7 0.0 copy-done.6
  0.7 0.0 copy-start.1
  0.7 0.7 %copy-done.1 = f32[1,3072]{1,0:T(1,128)S(1)} copy-done((f32[1,3072]{1,0:T(1,128)S(1)}, f32[1,3072]{1,0:T(1,128)}, u32[]{:S(2)}) %copy-start.1) | copy-done | bytes 12312
  1.4 0.0 copy-start.2
  1.4 0.7 %copy-done.2 = f32[1,3072]{1,0:T(1,128)S(1)} copy-done((f32[1,3072]{1,0:T(1,128)S(1)}, f32[1,3072]{1,0:T(1,128)}, u32[]{:S(2)}) %copy-start.2) | copy-done | bytes 12312
  2.1 0.0 copy-start.5
  2.1 0.7 %copy-done.5 = f32[512]{0:T(512)S(1)} copy-done((f32[512]{0:T(512)S(1)}, f32[512]{0:T(512)}, u32[]{:S(2)}) %copy-start.5) | copy-done | bytes 2072
  2.8 62.9 %whole.1 = bf16[128,512]{1,0:T(8,128)(2,1)S(1)} custom-call(bf16[32,3072]{1,0:T(8,128)(2,1)} %bitcast.18, bf16[32,3072]{1,0:T(8,128)(2,1)} %bitcast.19, bf16[32,3072]{1,0:T(8,128)(2,1)} %bitcast.20, bf16[32,3072]{1,0:T(8,128)(2,1)} %bitcast.21, f32[1,3072]{1,0:T(1,128)S(1)} %copy-done, f32[1,3072]{1,0:T(1,128)S(1)} %copy-done.1, f32[1,3072]{1,0:T(1,128)S(1)} %copy-done.2, ...), custom_call_target="tpu_custom_call" | custom-call | tf_op jit(solution)/shard_map/whole/pallas_call | solution.py:539
  65.7 0.7 copy.16
Async XLA Ops:
  0.0 0.7 %copy-start = (f32[1,3072]{1,0:T(1,128)S(1)}, f32[1,3072]{1,0:T(1,128)}, u32[]{:S(2)}) copy-start(f32[1,3072]{1,0:T(1,128)} %shift_hbm.1) | copy-start | bytes 36868
  0.0 0.7 %copy-start.4 = (f32[512]{0:T(512)S(1)}, f32[512]{0:T(512)}, u32[]{:S(2)}) copy-start(f32[512]{0:T(512)} %param.24) | copy-start | bytes 6148
  0.0 0.7 %copy-start.3 = (f32[512]{0:T(512)S(1)}, f32[512]{0:T(512)}, u32[]{:S(2)}) copy-start(f32[512]{0:T(512)} %param.23) | copy-start | bytes 6148
  0.0 0.7 %copy-start.6 = (f32[64]{0:T(128)S(1)}, f32[64]{0:T(128)}, u32[]{:S(2)}) copy-start(f32[64]{0:T(128)} %param.21) | copy-start | bytes 772
  0.7 0.7 %copy-start.1 = (f32[1,3072]{1,0:T(1,128)S(1)}, f32[1,3072]{1,0:T(1,128)}, u32[]{:S(2)}) copy-start(f32[1,3072]{1,0:T(1,128)} %scale_hbm.1) | copy-start | bytes 36868
  1.4 0.7 %copy-start.2 = (f32[1,3072]{1,0:T(1,128)S(1)}, f32[1,3072]{1,0:T(1,128)}, u32[]{:S(2)}) copy-start(f32[1,3072]{1,0:T(1,128)} %gate_hbm.1) | copy-start | bytes 36868
  2.1 0.7 %copy-start.5 = (f32[512]{0:T(512)S(1)}, f32[512]{0:T(512)}, u32[]{:S(2)}) copy-start(f32[512]{0:T(512)} %param.25) | copy-start | bytes 6148
